TPU v7x, 128 devices: a whole 4x4x4 slice. The times are simulated.
128 devices in a mesh: em: 8 (over z, core), th: 16 (over y, x).
Axes of the slice: x: 4, y: 4, z: 4, core: 2. Of those that a mesh axis runs over, the one named last changes fastest.
Arguments:
- e_real: float32 [131072, 128], P(('em', 'th')), may hold values from -6 to 6
- e_imag: float32 [131072, 128], P(('em', 'th')), may hold values from -6 to 6
- sigma_em: float32 [131072, 128], P(('em', 'th')), may hold values from 0.5 to 2
- temp_coef: float32 [131072, 128], P(('em', 'th')), may hold values from 0.05 to 0.5
- dest_dev: int32 [131072, 1], P(('em', 'th')), may hold values from 0 to 127; in each aligned block of 1024 rows (0 to 1023, 1024 to 2047, ...) at most 16 rows name the same one
- dest_tile: int32 [131072, 1], P(('em', 'th')), may hold values from 0 to 1023
- t_old: float32 [4096, 4096], P('th', 'em'), may hold values from 0.5 to 2
- heat_cap: float32 [4096, 4096], P('th', 'em'), may hold values from 0.05 to 0.5
- conduct: float32 [4096, 4096], P('th', 'em'), may hold values from 0.5 to 2
Outputs:
- temperature: float32 [4096, 4096], P('th', 'em')
- sigma_new: float32 [131072, 128], P(('em', 'th'))
Inputs may be any that keep to these rules, and one draw needn't show every extreme that they name: `dest_dev`: in the rows of one device (aligned blocks of 1024 rows), no owner is named by more than 16 rows, a bound that some block reaches.
All inputs are finite; a program needn't handle non-finite values.
Results may differ from a plain program's by a relative error of at most 0.00002.
Values sent between devices are 32-bit elements; how exact they have to be, the bound alone decides.
No kernel may reach another device: no remote copies, remote signals or barrier semaphores. Data moves between devices by JAX's collectives and lax.ppermute only.
A program may use at most 64 MiB of HBM per device.

v0:
```python
import jax
import jax.numpy as jnp
from jax import lax
from jax.sharding import PartitionSpec as P

SWEEPS = 3


def extended(block, sides, width):
    for axis, dim in sides:
        count = lax.axis_size(axis)
        forward = [(i, i + 1) for i in range(count - 1)]
        backward = [(target, source) for source, target in forward]
        low = lax.ppermute(
            lax.slice_in_dim(block, block.shape[dim] - width, None, axis=dim), axis, forward
        )
        high = lax.ppermute(lax.slice_in_dim(block, 0, width, axis=dim), axis, backward)
        block = jnp.concatenate([low, block, high], axis=dim)
    return block


def local(e_real, e_imag, sigma_em, temp_coef, dest_dev, dest_tile, t_old, heat_cap, conduct):
    n_em = lax.axis_size("em")
    n_th = lax.axis_size("th")
    devices = n_em * n_th
    count = e_real.shape[0]
    capacity = 2 * count // devices
    loss = sigma_em * (e_real * e_real + e_imag * e_imag)
    target = dest_dev[:, 0]
    tile_ids = dest_tile[:, 0]
    owners = jnp.arange(devices, dtype=jnp.int32)
    onehot = (target[:, None] == owners[None, :]).astype(jnp.int32)
    ranking = jnp.sum(jnp.cumsum(onehot, axis=0) * onehot, axis=1) - 1
    slots = target * capacity + ranking
    send = jnp.zeros((devices * capacity, 128), jnp.float32).at[slots].set(loss)
    send_ids = jnp.zeros((devices * capacity,), jnp.int32).at[slots].set(tile_ids)
    got, got_ids = (
        lax.all_to_all(
            send.reshape(devices, capacity, 128),
            ("em", "th"),
            split_axis=0,
            concat_axis=0,
            tiled=True,
        ),
        lax.all_to_all(
            send_ids.reshape(devices, capacity),
            ("em", "th"),
            split_axis=0,
            concat_axis=0,
            tiled=True,
        ),
    )
    got = got.reshape(devices * capacity, 128)
    got_ids = got_ids.reshape(devices * capacity)
    rows, cols = t_old.shape
    tiles = rows * cols // 128
    heat = jnp.zeros((tiles, 128), jnp.float32).at[got_ids].add(got).reshape(rows, cols)
    rhs = heat_cap * t_old + heat
    diag = heat_cap + 4.0 * conduct
    temp = t_old
    for sweep in range(SWEEPS):
        padded = extended(temp, (("th", 0), ("em", 1)), 1)
        beside_all = padded[2:, 1:-1] + padded[:-2, 1:-1] + padded[1:-1, 2:] + padded[1:-1, :-2]
        temp = (rhs + conduct * beside_all) / diag
    reply = temp.reshape(tiles, 128)[got_ids]
    returned = lax.all_to_all(
        reply.reshape(devices, capacity, 128), ("em", "th"), split_axis=0, concat_axis=0, tiled=True
    )
    hot = returned.reshape(devices * capacity, 128)[slots]
    return (temp, sigma_em / (1.0 + temp_coef * hot))


def solution(mesh):
    in_specs = (
        P(("em", "th"), None),
        P(("em", "th"), None),
        P(("em", "th"), None),
        P(("em", "th"), None),
        P(("em", "th"), None),
        P(("em", "th"), None),
        P("th", "em"),
        P("th", "em"),
        P("th", "em"),
    )
    out_specs = (P("th", "em"), P(("em", "th"), None))
    return jax.shard_map(local, mesh=mesh, in_specs=in_specs, out_specs=out_specs, check_vma=False)
```

profile of v0, /device:TPU:1, one launch (start us, length us, event | category | flops | bytes accessed | tf_op | source)
XLA Modules:
  0.0 147.8 jit_solution(8894840214029101330)
XLA Ops:
  2.8 4.5 %scatter_custom_fusion = s32[2048]{0:T(1024)S(1)} fusion(s32[1024]{0:T(1024)S(1)} %bitcast.27, s32[1024]{0:T(1024)} %bitcast.31, s32[]{:T(128)} %constant.9.clone.1), kind=kCustom, calls=%fused_computation.79 | custom fusion | bytes 8704 | tf_op jit(solution)/shard_map/scatter | solution.py:36
  8.0 11.5 %all-to-all-start = ((s32[128,1,16]{2,1,0:T(1,128)}), s32[128,1,16]{2,1,0:T(1,128)S(1)}, u32[]{:S(2)}, u32[]{:S(2)}) async-start(s32[128,1,16]{2,1,0:T(1,128)} %bitcast.8), calls=%async_computation | async-start | bytes 131072 | tf_op jit(solution)/shard_map/all_to_all | solution.py:45
  19.5 4.2 %scatter_custom_fusion.1 = f32[2048,128]{1,0:T(8,128)} fusion(s32[1024]{0:T(1024)S(1)} %bitcast.28, f32[1024,128]{1,0:T(8,128)S(1)} %copy-done.4, f32[1024,128]{1,0:T(8,128)S(1)} %copy-done.5, f32[1024,128]{1,0:T(8,128)S(1)} %copy-done.6, f32[]{:T(128)} %constant.8.clone.1), kind=kCustom, calls=%fused_computation.51 | custom fusion | flops 524288 | bytes 2621444 | tf_op jit(solution)/shard_map/scatter | solution.py:35
  23.6 5.3 %all-to-all-done = s32[128,1,16]{2,1,0:T(1,128)S(1)} async-done(((s32[128,1,16]{2,1,0:T(1,128)}), s32[128,1,16]{2,1,0:T(1,128)S(1)}, u32[]{:S(2)}, u32[]{:S(2)}) %all-to-all-start) | async-done | bytes 8224 | tf_op jit(solution)/shard_map/all_to_all | solution.py:45
  29.0 4.5 %all-to-all-start.1 = ((f32[128,16,128]{2,1,0:T(8,128)}), f32[128,16,128]{2,1,0:T(8,128)S(1)}, u32[]{:S(2)}, u32[]{:S(2)}) async-start(f32[128,16,128]{2,1,0:T(8,128)} %bitcast.10), calls=%async_computation.1 | async-start | bytes 2097152 | tf_op jit(solution)/shard_map/all_to_all | solution.py:38
  33.5 3.3 %collective-permute-start.1 = (f32[1,512]{1,0:T(1,128)S(1)}, f32[1,512]{1,0:T(1,128)S(1)}, u32[]{:S(2)}, u32[]{:S(2)}) collective-permute-start(f32[1,512]{1,0:T(1,128)S(1)} %get-tuple-element.12), channel_id=1, source_target_pairs={{0,1},{1,2},{2,3},{3,4},{4,5},{5,6},{6,7},{7,8},{8,9},{9,10},{10,1... | collective-permute-start | bytes 6152 | tf_op jit(solution)/shard_map/ppermute | solution.py:14
  36.8 1.3 collective-permute-start
  38.1 5.2 %collective-permute-done.1 = f32[1,512]{1,0:T(1,128)S(1)} collective-permute-done((f32[1,512]{1,0:T(1,128)S(1)}, f32[1,512]{1,0:T(1,128)S(1)}, u32[]{:S(2)}, u32[]{:S(2)}) %collective-permute-start.1) | collective-permute-done | bytes 2080 | tf_op jit(solution)/shard_map/ppermute | solution.py:14
  43.3 2.9 %collective-permute-done = f32[1,512]{1,0:T(1,128)S(1)} collective-permute-done((f32[1,512]{1,0:T(1,128)S(1)}, f32[1,512]{1,0:T(1,128)S(1)}, u32[]{:S(2)}, u32[]{:S(2)}) %collective-permute-start) | collective-permute-done | bytes 2080 | tf_op jit(solution)/shard_map/ppermute | solution.py:17
  47.0 2.8 %collective-permute-start.2 = (f32[258,1]{1,0:T(8,128)}, f32[258,1]{1,0:T(8,128)S(1)}, u32[]{:S(2)}, u32[]{:S(2)}) collective-permute-start(f32[258,1]{1,0:T(8,128)} %get-tuple-element.6), channel_id=1, source_target_pairs={{16,0},{32,16},{48,32},{64,48},{80,64},{96,80},{112,96},{17,1},{33... | collective-permute-start | bytes 3104 | tf_op jit(solution)/shard_map/ppermute | solution.py:17
  49.8 3.3 %collective-permute-start.3 = (f32[258,1]{1,0:T(8,128)S(1)}, f32[258,1]{1,0:T(8,128)S(1)}, u32[]{:S(2)}, u32[]{:S(2)}) collective-permute-start(f32[258,1]{1,0:T(8,128)S(1)} %get-tuple-element.7), channel_id=1, source_target_pairs={{0,16},{16,32},{32,48},{48,64},{64,80},{80,96},{96,112},{1,17},{17... | collective-permute-start | bytes 3104 | tf_op jit(solution)/shard_map/ppermute | solution.py:14
  53.5 0.8 reduce.3
  55.1 11.6 %scatter_custom_fusion.2 = f32[1024,128]{1,0:T(8,128)S(1)} fusion(s32[2048]{0:T(1024)S(1)} %bitcast.25, f32[2048,128]{1,0:T(8,128)S(1)} %bitcast.22, f32[]{:T(128)} %constant.8.clone.1), kind=kCustom, calls=%fused_computation.64 | custom fusion | flops 262144 | bytes 524292 | tf_op jit(solution)/shard_map/scatter-add | solution.py:57
  66.8 0.9 copy-done.1
  67.9 1.3 fusion.15
  69.2 2.4 %collective-permute-start.5 = (f32[1,512]{1,0:T(1,128)S(1)}, f32[1,512]{1,0:T(1,128)S(1)}, u32[]{:S(2)}, u32[]{:S(2)}) collective-permute-start(f32[1,512]{1,0:T(1,128)S(1)} %get-tuple-element.10), channel_id=1, source_target_pairs={{0,1},{1,2},{2,3},{3,4},{4,5},{5,6},{6,7},{7,8},{8,9},{9,10},{10,1... | collective-permute-start | bytes 6152 | tf_op jit(solution)/shard_map/ppermute | solution.py:14
  71.6 1.3 collective-permute-start.4
  72.9 3.3 %collective-permute-done.4 = f32[1,512]{1,0:T(1,128)S(1)} collective-permute-done((f32[1,512]{1,0:T(1,128)S(1)}, f32[1,512]{1,0:T(1,128)S(1)}, u32[]{:S(2)}, u32[]{:S(2)}) %collective-permute-start.4) | collective-permute-done | bytes 2080 | tf_op jit(solution)/shard_map/ppermute | solution.py:17
  76.3 2.3 %collective-permute-start.6 = (f32[258,1]{1,0:T(8,128)S(1)}, f32[258,1]{1,0:T(8,128)S(1)}, u32[]{:S(2)}, u32[]{:S(2)}) collective-permute-start(f32[258,1]{1,0:T(8,128)S(1)} %get-tuple-element.4), channel_id=1, source_target_pairs={{16,0},{32,16},{48,32},{64,48},{80,64},{96,80},{112,96},{17,1},{33... | collective-permute-start | bytes 3104 | tf_op jit(solution)/shard_map/ppermute | solution.py:17
  78.6 3.3 %collective-permute-start.7 = (f32[258,1]{1,0:T(8,128)S(1)}, f32[258,1]{1,0:T(8,128)S(1)}, u32[]{:S(2)}, u32[]{:S(2)}) collective-permute-start(f32[258,1]{1,0:T(8,128)S(1)} %get-tuple-element.5), channel_id=1, source_target_pairs={{0,16},{16,32},{32,48},{48,64},{64,80},{80,96},{96,112},{1,17},{17... | collective-permute-start | bytes 3104 | tf_op jit(solution)/shard_map/ppermute | solution.py:14
  82.6 1.2 collective-permute-done.7
  84.5 3.4 %collective-permute-start.9 = (f32[1,512]{1,0:T(1,128)S(1)}, f32[1,512]{1,0:T(1,128)S(1)}, u32[]{:S(2)}, u32[]{:S(2)}) collective-permute-start(f32[1,512]{1,0:T(1,128)S(1)} %get-tuple-element.8), channel_id=1, source_target_pairs={{0,1},{1,2},{2,3},{3,4},{4,5},{5,6},{6,7},{7,8},{8,9},{9,10},{10,1... | collective-permute-start | bytes 6152 | tf_op jit(solution)/shard_map/ppermute | solution.py:14
  87.9 1.3 collective-permute-start.8
  89.2 3.2 %collective-permute-done.8 = f32[1,512]{1,0:T(1,128)S(1)} collective-permute-done((f32[1,512]{1,0:T(1,128)S(1)}, f32[1,512]{1,0:T(1,128)S(1)}, u32[]{:S(2)}, u32[]{:S(2)}) %collective-permute-start.8) | collective-permute-done | bytes 2080 | tf_op jit(solution)/shard_map/ppermute | solution.py:17
  92.6 1.9 %collective-permute-start.10 = (f32[258,1]{1,0:T(8,128)S(1)}, f32[258,1]{1,0:T(8,128)S(1)}, u32[]{:S(2)}, u32[]{:S(2)}) collective-permute-start(f32[258,1]{1,0:T(8,128)S(1)} %get-tuple-element.2), channel_id=1, source_target_pairs={{16,0},{32,16},{48,32},{64,48},{80,64},{96,80},{112,96},{17,1},{33... | collective-permute-start | bytes 3104 | tf_op jit(solution)/shard_map/ppermute | solution.py:17
  94.5 5.6 %collective-permute-start.11 = (f32[258,1]{1,0:T(8,128)S(1)}, f32[258,1]{1,0:T(8,128)S(1)}, u32[]{:S(2)}, u32[]{:S(2)}) collective-permute-start(f32[258,1]{1,0:T(8,128)S(1)} %get-tuple-element.3), channel_id=1, source_target_pairs={{0,16},{16,32},{32,48},{48,64},{64,80},{80,96},{96,112},{1,17},{17... | collective-permute-start | bytes 3104 | tf_op jit(solution)/shard_map/ppermute | solution.py:14
  100.9 1.2 collective-permute-done.11
  103.5 7.6 %gather_fusion = f32[2048,128]{1,0:T(8,128)} fusion(f32[1024,128]{1,0:T(8,128)S(1)} %reshape.88, s32[2048]{0:T(1024)S(1)} %broadcast_clamp_fusion), kind=kCustom, calls=%fused_computation | custom fusion | bytes 2105344 | tf_op jit(solution)/shard_map/gather | solution.py:65
  111.1 14.2 %all-to-all-start.2 = ((f32[128,16,128]{2,1,0:T(8,128)}), f32[128,16,128]{2,1,0:T(8,128)S(1)}, u32[]{:S(2)}, u32[]{:S(2)}) async-start(f32[128,16,128]{2,1,0:T(8,128)} %bitcast.12), calls=%async_computation.2 | async-start | bytes 2097152 | tf_op jit(solution)/shard_map/all_to_all | solution.py:66
  125.3 18.8 %all-to-all-done.2 = f32[128,16,128]{2,1,0:T(8,128)S(1)} async-done(((f32[128,16,128]{2,1,0:T(8,128)}), f32[128,16,128]{2,1,0:T(8,128)S(1)}, u32[]{:S(2)}, u32[]{:S(2)}) %all-to-all-start.2) | async-done | bytes 1048608 | tf_op jit(solution)/shard_map/all_to_all | solution.py:66
  144.1 2.8 %gather_fusion.1 = f32[1024,128]{1,0:T(8,128)S(1)} fusion(f32[2048,128]{1,0:T(8,128)S(1)} %bitcast.21, s32[1024]{0:T(1024)S(1)} %broadcast_clamp_fusion.1), kind=kCustom, calls=%fused_computation.1 | custom fusion | bytes 1052672 | tf_op jit(solution)/shard_map/gather | solution.py:69
  146.9 0.9 add_divide_fusion
  (58 shorter events, 8.7 us)
Async XLA Ops:
  1.7 0.7 copy-start.8
  1.7 17.7 %copy-start.5 = (f32[1024,128]{1,0:T(8,128)S(1)}, f32[1024,128]{1,0:T(8,128)}, u32[]{:S(2)}) copy-start(f32[1024,128]{1,0:T(8,128)} %param.10) | copy-start | bytes 1572868
  1.7 17.7 %copy-start.6 = (f32[1024,128]{1,0:T(8,128)S(1)}, f32[1024,128]{1,0:T(8,128)}, u32[]{:S(2)}) copy-start(f32[1024,128]{1,0:T(8,128)} %param.9) | copy-start | bytes 1572868
  1.9 17.6 %copy-start.4 = (f32[1024,128]{1,0:T(8,128)S(1)}, f32[1024,128]{1,0:T(8,128)}, u32[]{:S(2)}) copy-start(f32[1024,128]{1,0:T(8,128)} %param.11) | copy-start | bytes 1572868
  8.0 21.0 %all-to-all-start = ((s32[128,1,16]{2,1,0:T(1,128)}), s32[128,1,16]{2,1,0:T(1,128)S(1)}, u32[]{:S(2)}, u32[]{:S(2)}) async-start(s32[128,1,16]{2,1,0:T(1,128)} %bitcast.8), calls=%async_computation | async-start | bytes 131072 | tf_op jit(solution)/shard_map/all_to_all | solution.py:45
  29.0 4.5 %copy-start = (f32[256,512]{1,0:T(8,128)S(1)}, f32[256,512]{1,0:T(8,128)}, u32[]{:S(2)}) copy-start(f32[256,512]{1,0:T(8,128)} %param.15) | copy-start | bytes 1572868
  29.0 25.5 %all-to-all-start.1 = ((f32[128,16,128]{2,1,0:T(8,128)}), f32[128,16,128]{2,1,0:T(8,128)S(1)}, u32[]{:S(2)}, u32[]{:S(2)}) async-start(f32[128,16,128]{2,1,0:T(8,128)} %bitcast.10), calls=%async_computation.1 | async-start | bytes 2097152 | tf_op jit(solution)/shard_map/all_to_all | solution.py:38
  33.5 9.8 %collective-permute-start.1 = (f32[1,512]{1,0:T(1,128)S(1)}, f32[1,512]{1,0:T(1,128)S(1)}, u32[]{:S(2)}, u32[]{:S(2)}) collective-permute-start(f32[1,512]{1,0:T(1,128)S(1)} %get-tuple-element.12), channel_id=1, source_target_pairs={{0,1},{1,2},{2,3},{3,4},{4,5},{5,6},{6,7},{7,8},{8,9},{9,10},{10,1... | collective-permute-start | bytes 6152 | tf_op jit(solution)/shard_map/ppermute | solution.py:14
  36.8 9.4 %collective-permute-start = (f32[1,512]{1,0:T(1,128)S(1)}, f32[1,512]{1,0:T(1,128)S(1)}, u32[]{:S(2)}, u32[]{:S(2)}) collective-permute-start(f32[1,512]{1,0:T(1,128)S(1)} %get-tuple-element.13), channel_id=1, source_target_pairs={{1,0},{2,1},{3,2},{4,3},{5,4},{6,5},{7,6},{8,7},{9,8},{10,9},{11,1... | collective-permute-start | bytes 6152 | tf_op jit(solution)/shard_map/ppermute | solution.py:17
  43.3 3.7 %copy-start.11 = (f32[1,512]{1,0:T(1,128)}, f32[1,512]{1,0:T(1,128)S(1)}, u32[]{:S(2)}) copy-start(f32[1,512]{1,0:T(1,128)S(1)} %collective-permute-done.1) | copy-start | bytes 6148
  46.3 0.7 copy-start.12
  47.0 19.8 %collective-permute-start.2 = (f32[258,1]{1,0:T(8,128)}, f32[258,1]{1,0:T(8,128)S(1)}, u32[]{:S(2)}, u32[]{:S(2)}) collective-permute-start(f32[258,1]{1,0:T(8,128)} %get-tuple-element.6), channel_id=1, source_target_pairs={{16,0},{32,16},{48,32},{64,48},{80,64},{96,80},{112,96},{17,1},{33... | collective-permute-start | bytes 3104 | tf_op jit(solution)/shard_map/ppermute | solution.py:17
  49.8 17.0 %collective-permute-start.3 = (f32[258,1]{1,0:T(8,128)S(1)}, f32[258,1]{1,0:T(8,128)S(1)}, u32[]{:S(2)}, u32[]{:S(2)}) collective-permute-start(f32[258,1]{1,0:T(8,128)S(1)} %get-tuple-element.7), channel_id=1, source_target_pairs={{0,16},{16,32},{32,48},{48,64},{64,80},{80,96},{96,112},{1,17},{17... | collective-permute-start | bytes 3104 | tf_op jit(solution)/shard_map/ppermute | solution.py:14
  54.5 0.6 copy-start.9
  66.7 1.0 copy-start.1
  66.7 1.2 copy-start.2
  69.2 3.7 %collective-permute-start.5 = (f32[1,512]{1,0:T(1,128)S(1)}, f32[1,512]{1,0:T(1,128)S(1)}, u32[]{:S(2)}, u32[]{:S(2)}) collective-permute-start(f32[1,512]{1,0:T(1,128)S(1)} %get-tuple-element.10), channel_id=1, source_target_pairs={{0,1},{1,2},{2,3},{3,4},{4,5},{5,6},{6,7},{7,8},{8,9},{9,10},{10,1... | collective-permute-start | bytes 6152 | tf_op jit(solution)/shard_map/ppermute | solution.py:14
  71.6 4.6 %collective-permute-start.4 = (f32[1,512]{1,0:T(1,128)S(1)}, f32[1,512]{1,0:T(1,128)S(1)}, u32[]{:S(2)}, u32[]{:S(2)}) collective-permute-start(f32[1,512]{1,0:T(1,128)S(1)} %get-tuple-element.11), channel_id=1, source_target_pairs={{1,0},{2,1},{3,2},{4,3},{5,4},{6,5},{7,6},{8,7},{9,8},{10,9},{11,1... | collective-permute-start | bytes 6152 | tf_op jit(solution)/shard_map/ppermute | solution.py:17
  76.3 6.4 %collective-permute-start.6 = (f32[258,1]{1,0:T(8,128)S(1)}, f32[258,1]{1,0:T(8,128)S(1)}, u32[]{:S(2)}, u32[]{:S(2)}) collective-permute-start(f32[258,1]{1,0:T(8,128)S(1)} %get-tuple-element.4), channel_id=1, source_target_pairs={{16,0},{32,16},{48,32},{64,48},{80,64},{96,80},{112,96},{17,1},{33... | collective-permute-start | bytes 3104 | tf_op jit(solution)/shard_map/ppermute | solution.py:17
  78.6 5.3 %collective-permute-start.7 = (f32[258,1]{1,0:T(8,128)S(1)}, f32[258,1]{1,0:T(8,128)S(1)}, u32[]{:S(2)}, u32[]{:S(2)}) collective-permute-start(f32[258,1]{1,0:T(8,128)S(1)} %get-tuple-element.5), channel_id=1, source_target_pairs={{0,16},{16,32},{32,48},{48,64},{64,80},{80,96},{96,112},{1,17},{17... | collective-permute-start | bytes 3104 | tf_op jit(solution)/shard_map/ppermute | solution.py:14
  84.5 4.8 %collective-permute-start.9 = (f32[1,512]{1,0:T(1,128)S(1)}, f32[1,512]{1,0:T(1,128)S(1)}, u32[]{:S(2)}, u32[]{:S(2)}) collective-permute-start(f32[1,512]{1,0:T(1,128)S(1)} %get-tuple-element.8), channel_id=1, source_target_pairs={{0,1},{1,2},{2,3},{3,4},{4,5},{5,6},{6,7},{7,8},{8,9},{9,10},{10,1... | collective-permute-start | bytes 6152 | tf_op jit(solution)/shard_map/ppermute | solution.py:14
  87.9 4.5 %collective-permute-start.8 = (f32[1,512]{1,0:T(1,128)S(1)}, f32[1,512]{1,0:T(1,128)S(1)}, u32[]{:S(2)}, u32[]{:S(2)}) collective-permute-start(f32[1,512]{1,0:T(1,128)S(1)} %get-tuple-element.9), channel_id=1, source_target_pairs={{1,0},{2,1},{3,2},{4,3},{5,4},{6,5},{7,6},{8,7},{9,8},{10,9},{11,1... | collective-permute-start | bytes 6152 | tf_op jit(solution)/shard_map/ppermute | solution.py:17
  92.4 7.7 %copy-start.10 = (s32[2048,1]{0,1:T(1,128)S(1)}, s32[2048,1]{0,1:T(1,128)}, u32[]{:S(2)}) copy-start(s32[2048,1]{0,1:T(1,128)} %copy-done.9) | copy-start | bytes 24580
  92.6 8.3 %collective-permute-start.10 = (f32[258,1]{1,0:T(8,128)S(1)}, f32[258,1]{1,0:T(8,128)S(1)}, u32[]{:S(2)}, u32[]{:S(2)}) collective-permute-start(f32[258,1]{1,0:T(8,128)S(1)} %get-tuple-element.2), channel_id=1, source_target_pairs={{16,0},{32,16},{48,32},{64,48},{80,64},{96,80},{112,96},{17,1},{33... | collective-permute-start | bytes 3104 | tf_op jit(solution)/shard_map/ppermute | solution.py:17
  94.5 7.6 %collective-permute-start.11 = (f32[258,1]{1,0:T(8,128)S(1)}, f32[258,1]{1,0:T(8,128)S(1)}, u32[]{:S(2)}, u32[]{:S(2)}) collective-permute-start(f32[258,1]{1,0:T(8,128)S(1)} %get-tuple-element.3), channel_id=1, source_target_pairs={{0,16},{16,32},{32,48},{48,64},{64,80},{80,96},{96,112},{1,17},{17... | collective-permute-start | bytes 3104 | tf_op jit(solution)/shard_map/ppermute | solution.py:14
  102.7 0.8 copy-start.3
  111.1 33.0 %all-to-all-start.2 = ((f32[128,16,128]{2,1,0:T(8,128)}), f32[128,16,128]{2,1,0:T(8,128)S(1)}, u32[]{:S(2)}, u32[]{:S(2)}) async-start(f32[128,16,128]{2,1,0:T(8,128)} %bitcast.12), calls=%async_computation.2 | async-start | bytes 2097152 | tf_op jit(solution)/shard_map/all_to_all | solution.py:66
  144.1 2.8 %copy-start.7 = (f32[1024,128]{1,0:T(8,128)S(1)}, f32[1024,128]{1,0:T(8,128)}, u32[]{:S(2)}) copy-start(f32[1024,128]{1,0:T(8,128)} %param.12) | copy-start | bytes 1572868
where the time goes:
time: 148 us
  starting transfers between devices  62.4 us (42%)
  waiting for transfers between devices  42.6 us (29%)
  other arithmetic  21.5 us (15%)
  local copies, waits for them, and re-layouts  20.1 us (14%)
    ppermute x6, starting transfers between devices, extended(): lax.ppermute(lax.slice_in_dim(block, block.shape[dim] - width, None, axis...  21.3 us
    all_to_all x1, waiting for transfers between devices, local(): lax.all_to_all(reply.reshape(devices, capacity, 128), ('em', 'th'), split...  18.8 us
    all_to_all x1, starting transfers between devices, local(): lax.all_to_all(reply.reshape(devices, capacity, 128), ('em', 'th'), split...  14.2 us
    scatter-add x1, other arithmetic, local(): jnp.zeros((tiles, 128), jnp.float32).at[got_ids].add(got)  11.6 us
    all_to_all x1, starting transfers between devices, local(): lax.all_to_all(send_ids.reshape(devices, capacity), ('em', 'th'), split_a...  11.5 us
    ppermute x6, waiting for transfers between devices, extended(): lax.ppermute(lax.slice_in_dim(block, 0, width, axis=dim), axis, backward)  10.9 us
    ppermute x6, starting transfers between devices, extended(): lax.ppermute(lax.slice_in_dim(block, 0, width, axis=dim), axis, backward)  10.9 us
    ppermute x6, waiting for transfers between devices, extended(): lax.ppermute(lax.slice_in_dim(block, block.shape[dim] - width, None, axis...  7.63 us
  transfers between devices with their start and end apart: 15, of which 10 were waited for; matrix products, arithmetic and copies ran while one was open for 12% of the time, Pallas kernels for 0%

commit v1 on v0

v1 whole, which is shorter than its diff:
```python
import functools
import jax
import jax.numpy as jnp
from jax import lax
from jax.experimental import pallas as pl
from jax.experimental.pallas import tpu as pltpu
from jax.sharding import PartitionSpec as P

F32 = jnp.float32
BF16 = jnp.bfloat16
I32 = jnp.int32
RIM = 8
SIDE = 128


def iota(shape, dim):
    return lax.broadcasted_iota(I32, shape, dim)


def halves(x):
    high = x.astype(BF16)
    low = (x - high.astype(F32)).astype(BF16)
    return high, low


def select(mask):
    return jnp.where(mask, 1.0, 0.0).astype(BF16)


def joined(y):
    return y[:, :128] + y[:, 128:]


def route_kernel(owners, slots, rows, dev_ref, tile_ref, er_ref, ei_ref, sg_ref, send_ref, slot_ref, pair_ref):
    count = er_ref.shape[0]
    blocks = count // 128
    er = er_ref[...]
    ei = ei_ref[...]
    high, low = halves(sg_ref[...] * (er * er + ei * ei))
    pair_ref[:, :128] = high
    pair_ref[:, 128:] = low
    dev = dev_ref[...]
    tile = tile_ref[...]
    tile = (tile & 3) * rows + (tile >> 2)
    hits = [jnp.broadcast_to(dev[b : b + 1], (owners, 128)) == iota((owners, 128), 0) for b in range(blocks)]
    ahead = select(iota((128, 256), 0) < iota((128, 256), 1))
    sums = jnp.dot(
        jnp.concatenate([select(h) for h in hits], axis=0), ahead, preferred_element_type=F32
    )
    carry = jnp.zeros((owners, 128), F32)
    ranks = []
    for b in range(blocks):
        part = sums[b * owners : (b + 1) * owners]
        ranks.append(
            jnp.sum(jnp.where(hits[b], part[:, :128] + carry, 0.0), axis=0, keepdims=True)
        )
        carry = carry + part[:, 128:]
    rank = jnp.concatenate(ranks, axis=0).astype(I32)
    slot_ref[...] = dev * slots + rank
    line = lambda x: jnp.concatenate([x[b : b + 1] for b in range(blocks)], axis=1)
    place = line(dev * (slots + 1) + rank)
    step = 4 * 136
    for start in range(0, owners * (slots + 1), step):
        mask = jnp.broadcast_to(place, (step, count)) == iota((step, count), 0) + start
        send_ref[start : start + step, :] = joined(
            jnp.dot(select(mask), pair_ref[...], preferred_element_type=F32)
        )
    hit = jnp.concatenate(hits, axis=1)
    tiles = line(tile)
    upper = jnp.where(hit, jnp.broadcast_to(tiles >> 5, (owners, count)), 0)
    lower = jnp.where(hit, jnp.broadcast_to(tiles & 31, (owners, count)), 0)
    numbers = jnp.concatenate([upper, lower], axis=0).astype(F32).astype(BF16)
    which = select(jnp.broadcast_to(line(rank), (128, count)) == iota((128, count), 0))
    ids = lax.dot_general(
        numbers, which, (((1,), (1,)), ((), ())), preferred_element_type=F32
    )
    send_ref[pl.ds(slots, owners, stride=slots + 1), :] = ids[:owners] * 32.0 + ids[owners:]


def route(dev, tile, er, ei, sg, owners, slots, rows):
    count = er.shape[0]
    return pl.pallas_call(
        functools.partial(route_kernel, owners, slots, rows),
        out_shape=(
            jax.ShapeDtypeStruct((owners * (slots + 1), 128), F32),
            jax.ShapeDtypeStruct((count // 128, 128), I32),
        ),
        scratch_shapes=[pltpu.VMEM((count, 256), BF16)],
        compiler_params=pltpu.CompilerParams(vmem_limit_bytes=32 << 20),
        name="route",
    )(dev.reshape(count // 128, 128), tile.reshape(count // 128, 128), er, ei, sg)


def heat_kernel(owners, slots, got_ref, heat_ref, ids_ref, pair_ref):
    rows = heat_ref.shape[0]
    groups = heat_ref.shape[1] // 128
    ids = got_ref[pl.ds(slots, owners, stride=slots + 1), :].astype(I32)
    ids_ref[...] = ids
    flat = ids.T
    for r in range(slots):
        high, low = halves(got_ref[pl.ds(r, owners, stride=slots + 1), :])
        pair_ref[r * owners : (r + 1) * owners, :128] = high
        pair_ref[r * owners : (r + 1) * owners, 128:] = low
    line = jnp.concatenate([flat[r : r + 1] for r in range(slots)], axis=1)
    for q in range(groups):
        shape = (rows, owners * slots)
        mask = jnp.broadcast_to(line, shape) == iota(shape, 0) + q * rows
        heat_ref[:, q * 128 : (q + 1) * 128] = joined(
            jnp.dot(select(mask), pair_ref[...], preferred_element_type=F32)
        )


def gather_heat(got, owners, slots, rows, cols):
    return pl.pallas_call(
        functools.partial(heat_kernel, owners, slots),
        out_shape=(
            jax.ShapeDtypeStruct((rows, cols), F32),
            jax.ShapeDtypeStruct((owners, 128), I32),
        ),
        scratch_shapes=[pltpu.VMEM((owners * slots, 256), BF16)],
        compiler_params=pltpu.CompilerParams(vmem_limit_bytes=32 << 20),
        name="heat",
    )(got)


def around(x):
    rows, cols = x.shape
    return (
        pltpu.roll(x, 1, 0) + pltpu.roll(x, rows - 1, 0)
    ) + (pltpu.roll(x, 1, 1) + pltpu.roll(x, cols - 1, 1))


def base_kernel(sweeps, t_ref, hc_ref, c_ref, base_ref, a_ref, g_ref):
    hc = hc_ref[...]
    c = c_ref[...]
    diag = hc + 4.0 * c
    g = jnp.where(diag > 0.0, 1.0 / jnp.where(diag > 0.0, diag, 1.0), 0.0)
    g_ref[...] = g
    a_ref[...] = c * g
    r0 = hc * t_ref[...] * g
    temp = t_ref[...]
    for _ in range(sweeps):
        temp = r0 + a_ref[...] * around(temp)
    base_ref[...] = temp


def base(t, hc, c, sweeps):
    shape = jax.ShapeDtypeStruct(t.shape, F32)
    return pl.pallas_call(
        functools.partial(base_kernel, sweeps),
        out_shape=(shape, shape, shape),
        compiler_params=pltpu.CompilerParams(vmem_limit_bytes=32 << 20),
        name="base",
    )(t, hc, c)


def solve_kernel(sweeps, owners, slots, heat_ref, base_ref, a_ref, g_ref, ids_ref, temp_ref, reply_ref, pair_ref):
    rows, cols = temp_ref.shape
    h = heat_ref[...] * g_ref[...]
    u = h
    for _ in range(sweeps - 1):
        u = h + a_ref[...] * around(u)
    temp = (base_ref[...] + u)[RIM : RIM + rows, SIDE : SIDE + cols]
    temp_ref[...] = temp
    groups = cols // 128
    for q in range(groups):
        high, low = halves(temp[:, q * 128 : (q + 1) * 128])
        pair_ref[q * rows : (q + 1) * rows, :128] = high
        pair_ref[q * rows : (q + 1) * rows, 128:] = low
    tiles = groups * rows
    ids = ids_ref[...]
    for r in range(0, slots, 4):
        column = jnp.concatenate(
            [jnp.broadcast_to(ids[:, k : k + 1], (owners, 128)) for k in range(r, r + 4)], axis=0
        )
        mask = jnp.concatenate(
            [column == iota((4 * owners, 128), 1) + 128 * k for k in range(tiles // 128)], axis=1
        )
        got = joined(jnp.dot(select(mask), pair_ref[...], preferred_element_type=F32))
        for k in range(4):
            reply_ref[pl.ds(r + k, owners, stride=slots), :] = got[k * owners : (k + 1) * owners]


def solve(heat, base_t, a, g, ids, sweeps, owners, slots, rows, cols):
    return pl.pallas_call(
        functools.partial(solve_kernel, sweeps, owners, slots),
        out_shape=(
            jax.ShapeDtypeStruct((rows, cols), F32),
            jax.ShapeDtypeStruct((owners * slots, 128), F32),
        ),
        scratch_shapes=[pltpu.VMEM((rows * cols // 128, 256), BF16)],
        compiler_params=pltpu.CompilerParams(vmem_limit_bytes=32 << 20),
        name="solve",
    )(heat, base_t, a, g, ids)


def final_kernel(slot_ref, back_ref, sg_ref, tc_ref, out_ref, pair_ref):
    total = back_ref.shape[0]
    blocks = slot_ref.shape[0]
    high, low = halves(back_ref[...])
    pair_ref[:, :128] = high
    pair_ref[:, 128:] = low
    slot = slot_ref[...].T
    for b in range(0, blocks, 4):
        column = jnp.concatenate(
            [jnp.broadcast_to(slot[:, k : k + 1], (128, 128)) for k in range(b, b + 4)], axis=0
        )
        mask = jnp.concatenate(
            [column == iota((512, 128), 1) + 128 * k for k in range(total // 128)], axis=1
        )
        hot = joined(jnp.dot(select(mask), pair_ref[...], preferred_element_type=F32))
        span = slice(b * 128, b * 128 + 512)
        out_ref[span, :] = sg_ref[span, :] / (1.0 + tc_ref[span, :] * hot)


def final(slot, back, sg, tc):
    return pl.pallas_call(
        final_kernel,
        out_shape=jax.ShapeDtypeStruct(sg.shape, F32),
        scratch_shapes=[pltpu.VMEM((back.shape[0], 256), BF16)],
        compiler_params=pltpu.CompilerParams(vmem_limit_bytes=32 << 20),
        name="final",
    )(slot, back, sg, tc)


def swap(low_part, high_part, axis):
    count = lax.axis_size(axis)
    up = [(i, i + 1) for i in range(count - 1)]
    down = [(i + 1, i) for i in range(count - 1)]
    return lax.ppermute(high_part, axis, up), lax.ppermute(low_part, axis, down)


def widened(blocks, width):
    n = len(blocks)
    rows, cols = blocks[0].shape
    pack = lambda f: jnp.concatenate([f(x).T for x in blocks], axis=0)
    left, right = swap(pack(lambda x: x[:, :width]), pack(lambda x: x[:, cols - width :]), "em")
    wide = []
    for k, x in enumerate(blocks):
        lo = jnp.pad(left[k * width : (k + 1) * width].T, ((0, 0), (SIDE - width, 0)))
        hi = jnp.pad(right[k * width : (k + 1) * width].T, ((0, 0), (0, SIDE - width)))
        wide.append(jnp.concatenate([lo, x, hi], axis=1))
    pack = lambda f: jnp.concatenate([f(x) for x in wide], axis=0)
    above, below = swap(pack(lambda x: x[:width]), pack(lambda x: x[rows - width :]), "th")
    out = []
    for k, x in enumerate(wide):
        lo = jnp.pad(above[k * width : (k + 1) * width], ((RIM - width, 0), (0, 0)))
        hi = jnp.pad(below[k * width : (k + 1) * width], ((0, RIM - width), (0, 0)))
        out.append(jnp.concatenate([lo, x, hi], axis=0))
    return out


def exchanged(x, owners):
    rows = x.shape[0]
    x = x.reshape(owners, 1, rows // owners * 128)
    x = lax.all_to_all(x, ("em", "th"), split_axis=0, concat_axis=0, tiled=True)
    return x.reshape(rows, 128)


SWEEPS = 3


def local(e_real, e_imag, sigma_em, temp_coef, dest_dev, dest_tile, t_old, heat_cap, conduct):
    owners = lax.axis_size("em") * lax.axis_size("th")
    slots = 2 * e_real.shape[0] // owners
    rows, cols = t_old.shape
    send, slot = route(dest_dev, dest_tile, e_real, e_imag, sigma_em, owners, slots, rows)
    got = exchanged(send, owners)
    base_t, a, g = base(*widened([t_old, heat_cap, conduct], SWEEPS), SWEEPS)
    heat, ids = gather_heat(got, owners, slots, rows, cols)
    (heat,) = widened([heat], SWEEPS - 1)
    temp, reply = solve(heat, base_t, a, g, ids, SWEEPS, owners, slots, rows, cols)
    back = exchanged(reply, owners)
    return temp, final(slot, back, sigma_em, temp_coef)


def solution(mesh):
    tiles = P(("em", "th"), None)
    grid = P("th", "em")
    return jax.shard_map(
        local,
        mesh=mesh,
        in_specs=(tiles,) * 6 + (grid,) * 3,
        out_specs=(grid, tiles),
        check_vma=False,
    )
```

time: 148 us -> 94.1 us (0.64)
  starting transfers between devices: 62.4 us -> 31 us
  blocking collectives: 0 us -> 26.9 us
  waiting for transfers between devices: 42.6 us -> 16.9 us
  other arithmetic: 21.5 us -> 0.38 us
  local copies, waits for them, and re-layouts: 20.1 us -> 6.57 us
  Pallas kernels: 0 us -> 10.8 us
    all_to_all x0 -> x1, blocking collectives: none -> 26.9 us  [exchanged(): x = lax.all_to_all(x, ('em', 'th'), split_axis=0, concat_axis=0, tiled=True)]
    all_to_all x3 -> x1, starting transfers between devices: 30.2 us -> 9.65 us  [exchanged(): x = lax.all_to_all(x, ('em', 'th'), split_axis=0, concat_axis=0, tiled=True)]
    all_to_all x3 -> x1, waiting for transfers between devices: 24.1 us -> 4.48 us  [exchanged(): x = lax.all_to_all(x, ('em', 'th'), split_axis=0, concat_axis=0, tiled=True)]
    scatter-add x1 -> x0, other arithmetic: 11.6 us -> none  [local(): jnp.zeros((tiles, 128), jnp.float32).at[got_ids].add(got)]
    ppermute x12 -> x8, starting transfers between devices: 32.2 us -> 21.3 us  [the longest x4 13.5 us: swap(): lax.ppermute(high_part, axis, up)]
    pallas_call x0 -> x5, Pallas kernels: none -> 10.8 us  [the longest x1 3.06 us: route(): pl.pallas_call(functools.partial(route_kernel, owners, slots, rows), out_...]
    gather x2 -> x0, local copies, waits for them, and re-layouts: 10.4 us -> none  [the longest x1 7.59 us: local(): reply = temp.reshape(tiles, 128)[got_ids]]
    ppermute x12 -> x8, waiting for transfers between devices: 18.5 us -> 12.5 us  [the longest x4 12.4 us: swap(): lax.ppermute(low_part, axis, down)]
  transfers between devices with their start and end apart: 15 -> 9, of which waited for: 10 -> 4; matrix products, arithmetic and copies ran while one was open for 12% -> 3% of each run, Pallas kernels for 0% -> 5%
where the time goes in v1:
time: 94.1 us; the launch traced here: 93.7 us
  starting transfers between devices  31 us (33%)
  blocking collectives  26.9 us (29%)
  waiting for transfers between devices  16.9 us (18%)
  Pallas kernels  10.8 us (11%)
  local copies, waits for them, and re-layouts  6.57 us (7%)
  between operations  1.12 us (1%)
    all_to_all x1, blocking collectives, exchanged(): x = lax.all_to_all(x, ('em', 'th'), split_axis=0, concat_axis=0, tiled=True)  26.9 us
    ppermute x4, starting transfers between devices, swap(): lax.ppermute(high_part, axis, up)  13.5 us
    ppermute x4, waiting for transfers between devices, swap(): lax.ppermute(low_part, axis, down)  12.4 us
    all_to_all x1, starting transfers between devices, exchanged(): x = lax.all_to_all(x, ('em', 'th'), split_axis=0, concat_axis=0, tiled=True)  9.65 us
    ppermute x4, starting transfers between devices, swap(): lax.ppermute(low_part, axis, down)  7.82 us
    all_to_all x1, waiting for transfers between devices, exchanged(): x = lax.all_to_all(x, ('em', 'th'), split_axis=0, concat_axis=0, tiled=True)  4.48 us
    pallas_call x1, Pallas kernels, route(): pl.pallas_call(functools.partial(route_kernel, owners, slots, rows), out_...  3.06 us
    slice x3, local copies, waits for them, and re-layouts, widened(): x[:, cols - width:]  2.39 us
  transfers between devices with their start and end apart: 9, of which 4 were waited for; matrix products, arithmetic and copies ran while one was open for 3% of the time, Pallas kernels for 5%

profile of v1, /device:TPU:1, one launch (start us, length us, event | category | flops | bytes accessed | tf_op | source)
XLA Modules:
  0.0 93.7 jit_solution(12221817627120915990)
XLA Ops:
  0.6 1.1 %fusion.6 = (f32[256,3]{1,0:T(8,128)S(1)}, f32[256,3]{1,0:T(8,128)S(1)}) fusion(f32[256,512]{1,0:T(8,128)} %param.15), kind=kLoop, calls=%fused_computation.45 | loop fusion | bytes 12288 | tf_op jit(solution)/shard_map/slice | solution.py:237
  1.9 1.2 %fusion.7 = (f32[256,3]{1,0:T(8,128)S(1)}, f32[256,3]{1,0:T(8,128)S(1)}) fusion(f32[256,512]{1,0:T(8,128)} %param.16), kind=kLoop, calls=%fused_computation.46 | loop fusion | bytes 12288 | tf_op jit(solution)/shard_map/slice | solution.py:237
  3.2 0.1 fusion.8
  3.4 0.1 copy.19
  3.5 3.3 %collective-permute-start.5 = (f32[9,256]{0,1:T(8,128)S(1)}, f32[9,256]{0,1:T(8,128)S(1)}, u32[]{:S(2)}, u32[]{:S(2)}) collective-permute-start(f32[9,256]{0,1:T(8,128)S(1)} %copy.19), channel_id=1, source_target_pairs={{16,0},{32,16},{48,32},{64,48},{80,64},{96,80},{112,96},{17,1},{33... | collective-permute-start | bytes 27656 | tf_op jit(solution)/shard_map/ppermute | solution.py:230
  7.1 0.8 copy.15
  7.9 3.5 %collective-permute-start.4 = (f32[9,256]{0,1:T(8,128)}, f32[9,256]{0,1:T(8,128)S(1)}, u32[]{:S(2)}, u32[]{:S(2)}) collective-permute-start(f32[9,256]{0,1:T(8,128)} %copy.15), channel_id=1, source_target_pairs={{0,16},{16,32},{32,48},{48,64},{64,80},{80,96},{96,112},{1,17},{17... | collective-permute-start | bytes 27656 | tf_op jit(solution)/shard_map/ppermute | solution.py:230
  11.4 3.1 %route.1 = (f32[2176,128]{1,0:T(8,128)}, s32[8,128]{1,0:T(8,128)S(1)}) custom-call(s32[8,128]{1,0:T(8,128)S(1)} %bitcast.33, s32[8,128]{1,0:T(8,128)S(1)} %bitcast.34, f32[1024,128]{1,0:T(8,128)S(1)} %copy-done.1, f32[1024,128]{1,0:T(8,128)S(1)} %copy-done.2, f32[1024,128]{1,0:T(8,128)S(1)} %copy-done), custom_call_target="tpu_custom_call" | custom-call | tf_op jit(solution)/shard_map/route/pallas_call | solution.py:82
  14.5 9.7 %all-to-all-start = ((f32[128,1,2176]{2,1,0:T(1,128)}), f32[128,1,2176]{2,1,0:T(1,128)S(1)}, u32[]{:S(2)}, u32[]{:S(2)}) async-start(f32[128,1,2176]{2,1,0:T(1,128)} %bitcast.2), calls=%async_computation | async-start | bytes 2228224 | tf_op jit(solution)/shard_map/all_to_all | solution.py:256
  24.2 0.1 slice_bitcast_fusion.4
  24.4 0.1 slice_bitcast_fusion.5
  24.7 0.1 pad.64
  24.9 0.6 copy-done.7
  25.5 0.2 copy-done.8
  25.7 0.6 copy-done.15
  26.3 1.3 %collective-permute-start.7 = (f32[9,768]{1,0:T(8,128)S(1)}, f32[9,768]{1,0:T(8,128)S(1)}, u32[]{:S(2)}, u32[]{:S(2)}) collective-permute-start(f32[9,768]{1,0:T(8,128)S(1)} %get-tuple-element.20), channel_id=1, source_target_pairs={{1,0},{2,1},{3,2},{4,3},{5,4},{6,5},{7,6},{8,7},{9,8},{10,9},{11,1... | collective-permute-start | bytes 82952 | tf_op jit(solution)/shard_map/ppermute | solution.py:230
  27.6 4.0 %collective-permute-start.6 = (f32[9,768]{1,0:T(8,128)S(1)}, f32[9,768]{1,0:T(8,128)S(1)}, u32[]{:S(2)}, u32[]{:S(2)}) collective-permute-start(f32[9,768]{1,0:T(8,128)S(1)} %get-tuple-element.21), channel_id=1, source_target_pairs={{0,1},{1,2},{2,3},{3,4},{4,5},{5,6},{6,7},{7,8},{8,9},{9,10},{10,1... | collective-permute-start | bytes 82952 | tf_op jit(solution)/shard_map/ppermute | solution.py:230
  31.6 7.1 %collective-permute-done.7 = f32[9,768]{1,0:T(8,128)S(1)} collective-permute-done((f32[9,768]{1,0:T(8,128)S(1)}, f32[9,768]{1,0:T(8,128)S(1)}, u32[]{:S(2)}, u32[]{:S(2)}) %collective-permute-start.7) | collective-permute-done | bytes 27680 | tf_op jit(solution)/shard_map/ppermute | solution.py:230
  38.7 0.6 fusion.10
  39.3 4.5 %all-to-all-done = f32[128,1,2176]{2,1,0:T(1,128)S(1)} async-done(((f32[128,1,2176]{2,1,0:T(1,128)}), f32[128,1,2176]{2,1,0:T(1,128)S(1)}, u32[]{:S(2)}, u32[]{:S(2)}) %all-to-all-start) | async-done | bytes 1114144 | tf_op jit(solution)/shard_map/all_to_all | solution.py:256
  43.8 1.3 %heat.1 = (f32[256,512]{1,0:T(8,128)S(1)}, s32[128,128]{1,0:T(8,128)S(1)}) custom-call(f32[2176,128]{1,0:T(8,128)S(1)} %bitcast.30), custom_call_target="tpu_custom_call" | custom-call | tf_op jit(solution)/shard_map/heat/pallas_call | solution.py:114
  45.2 3.6 %collective-permute-start = (f32[2,256]{0,1:T(8,128)S(1)}, f32[2,256]{0,1:T(8,128)S(1)}, u32[]{:S(2)}, u32[]{:S(2)}) collective-permute-start(f32[2,256]{0,1:T(8,128)S(1)} %get-tuple-element.30), channel_id=1, source_target_pairs={{0,16},{16,32},{32,48},{48,64},{64,80},{80,96},{96,112},{1,17},{17... | collective-permute-start | bytes 6152 | tf_op jit(solution)/shard_map/ppermute | solution.py:230
  48.8 1.9 %collective-permute-start.1 = (f32[2,256]{0,1:T(8,128)S(1)}, f32[2,256]{0,1:T(8,128)S(1)}, u32[]{:S(2)}, u32[]{:S(2)}) collective-permute-start(f32[2,256]{0,1:T(8,128)S(1)} %get-tuple-element.31), channel_id=1, source_target_pairs={{16,0},{32,16},{48,32},{64,48},{80,64},{96,80},{112,96},{17,1},{33... | collective-permute-start | bytes 6152 | tf_op jit(solution)/shard_map/ppermute | solution.py:230
  50.8 0.1 select_maximum_fusion
  51.1 4.1 %collective-permute-done.1 = f32[2,256]{0,1:T(8,128)S(1)} collective-permute-done((f32[2,256]{0,1:T(8,128)S(1)}, f32[2,256]{0,1:T(8,128)S(1)}, u32[]{:S(2)}, u32[]{:S(2)}) %collective-permute-start.1) | collective-permute-done | bytes 2080 | tf_op jit(solution)/shard_map/ppermute | solution.py:230
  55.2 2.4 %collective-permute-start.2 = (f32[2,768]{1,0:T(2,128)S(1)}, f32[2,768]{1,0:T(2,128)S(1)}, u32[]{:S(2)}, u32[]{:S(2)}) collective-permute-start(f32[2,768]{1,0:T(2,128)S(1)} %get-tuple-element.22), channel_id=1, source_target_pairs={{0,1},{1,2},{2,3},{3,4},{4,5},{5,6},{6,7},{7,8},{8,9},{9,10},{10,1... | collective-permute-start | bytes 18440 | tf_op jit(solution)/shard_map/ppermute | solution.py:230
  57.6 1.3 %collective-permute-start.3 = (f32[2,768]{1,0:T(2,128)S(1)}, f32[2,768]{1,0:T(2,128)S(1)}, u32[]{:S(2)}, u32[]{:S(2)}) collective-permute-start(f32[2,768]{1,0:T(2,128)S(1)} %get-tuple-element.23), channel_id=1, source_target_pairs={{1,0},{2,1},{3,2},{4,3},{5,4},{6,5},{7,6},{8,7},{9,8},{10,9},{11,1... | collective-permute-start | bytes 18440 | tf_op jit(solution)/shard_map/ppermute | solution.py:230
  58.9 1.7 %base.1 = (f32[272,768]{1,0:T(8,128)S(1)}, f32[272,768]{1,0:T(8,128)S(1)}, f32[272,768]{1,0:T(8,128)S(1)}) custom-call(f32[272,768]{1,0:T(8,128)S(1)} %fusion.t_ref, f32[272,768]{1,0:T(8,128)S(1)} %get-tuple-element.44.hc_ref, f32[272,768]{1,0:T(8,128)S(1)} %get-tuple-element.43.c_ref), custom_call_target="tpu_custom_call" | custom-call | tf_op jit(solution)/shard_map/base/pallas_call | solution.py:149
  60.6 1.3 %collective-permute-done.3 = f32[2,768]{1,0:T(2,128)S(1)} collective-permute-done((f32[2,768]{1,0:T(2,128)S(1)}, f32[2,768]{1,0:T(2,128)S(1)}, u32[]{:S(2)}, u32[]{:S(2)}) %collective-permute-start.3) | collective-permute-done | bytes 6176 | tf_op jit(solution)/shard_map/ppermute | solution.py:230
  62.0 2.4 %solve.1 = (f32[256,512]{1,0:T(8,128)}, f32[2048,128]{1,0:T(8,128)S(1)}) custom-call(f32[272,768]{1,0:T(8,128)S(1)} %select_maximum_fusion.5.heat_ref, f32[272,768]{1,0:T(8,128)S(1)} %get-tuple-element.13.base_ref, f32[272,768]{1,0:T(8,128)S(1)} %get-tuple-element.14.a_ref, f32[272,768]{1,0:T(8,128)S(1)} %get-tuple-element.15.g_ref, ...), custom_call_target="tpu_custom_call" | custom-call | tf_op jit(solution)/shard_map/solve/pallas_call | solution.py:185
  64.4 26.9 %all_to_all.10 = f32[128,1,2048]{2,1,0:T(1,128)S(1)} all-to-all(f32[128,1,2048]{2,1,0:T(1,128)S(1)} %bitcast.32), channel_id=1, replica_groups=mesh['em'=8,'th'=16] {'em','th'}, dimensions={0} | all-to-all | bytes 2097152 | tf_op jit(solution)/shard_map/all_to_all | solution.py:256
  91.3 2.4 %final.1 = f32[1024,128]{1,0:T(8,128)} custom-call(s32[8,128]{1,0:T(8,128)S(1)} %get-tuple-element.18.slot_ref, f32[2048,128]{1,0:T(8,128)S(1)} %bitcast.31, f32[1024,128]{1,0:T(8,128)S(1)} %copy-done, f32[1024,128]{1,0:T(8,128)S(1)} %copy-done.3), custom_call_target="tpu_custom_call" | custom-call | tf_op jit(solution)/shard_map/final/pallas_call | solution.py:217
  (62 shorter events, 1.3 us)
Async XLA Ops:
  0.6 2.5 %copy-start.6 = (f32[256,512]{1,0:T(8,128)S(1)}, f32[256,512]{1,0:T(8,128)}, u32[]{:S(2)}) copy-start(f32[256,512]{1,0:T(8,128)} %param.17) | copy-start | bytes 1572868
  1.8 9.6 %copy-start = (f32[1024,128]{1,0:T(8,128)S(1)}, f32[1024,128]{1,0:T(8,128)}, u32[]{:S(2)}) copy-start(f32[1024,128]{1,0:T(8,128)} %sg_ref.3) | copy-start | bytes 1572868
  1.8 9.6 %copy-start.1 = (f32[1024,128]{1,0:T(8,128)S(1)}, f32[1024,128]{1,0:T(8,128)}, u32[]{:S(2)}) copy-start(f32[1024,128]{1,0:T(8,128)} %er_ref.1) | copy-start | bytes 1572868
  1.8 9.6 %copy-start.2 = (f32[1024,128]{1,0:T(8,128)S(1)}, f32[1024,128]{1,0:T(8,128)}, u32[]{:S(2)}) copy-start(f32[1024,128]{1,0:T(8,128)} %ei_ref.1) | copy-start | bytes 1572868
  1.8 9.6 %copy-start.4 = (s32[1024,1]{0,1:T(1,128)S(1)}, s32[1024,1]{0,1:T(1,128)}, u32[]{:S(2)}) copy-start(s32[1024,1]{0,1:T(1,128)} %param.13) | copy-start | bytes 12292
  1.8 9.6 %copy-start.5 = (s32[1024,1]{0,1:T(1,128)S(1)}, s32[1024,1]{0,1:T(1,128)}, u32[]{:S(2)}) copy-start(s32[1024,1]{0,1:T(1,128)} %param.14) | copy-start | bytes 12292
  3.5 20.7 %collective-permute-start.5 = (f32[9,256]{0,1:T(8,128)S(1)}, f32[9,256]{0,1:T(8,128)S(1)}, u32[]{:S(2)}, u32[]{:S(2)}) collective-permute-start(f32[9,256]{0,1:T(8,128)S(1)} %copy.19), channel_id=1, source_target_pairs={{16,0},{32,16},{48,32},{64,48},{80,64},{96,80},{112,96},{17,1},{33... | collective-permute-start | bytes 27656 | tf_op jit(solution)/shard_map/ppermute | solution.py:230
  7.9 16.6 %collective-permute-start.4 = (f32[9,256]{0,1:T(8,128)}, f32[9,256]{0,1:T(8,128)S(1)}, u32[]{:S(2)}, u32[]{:S(2)}) collective-permute-start(f32[9,256]{0,1:T(8,128)} %copy.15), channel_id=1, source_target_pairs={{0,16},{16,32},{32,48},{48,64},{64,80},{80,96},{96,112},{1,17},{17... | collective-permute-start | bytes 27656 | tf_op jit(solution)/shard_map/ppermute | solution.py:230
  14.5 29.3 %all-to-all-start = ((f32[128,1,2176]{2,1,0:T(1,128)}), f32[128,1,2176]{2,1,0:T(1,128)S(1)}, u32[]{:S(2)}, u32[]{:S(2)}) async-start(f32[128,1,2176]{2,1,0:T(1,128)} %bitcast.2), calls=%async_computation | async-start | bytes 2228224 | tf_op jit(solution)/shard_map/all_to_all | solution.py:256
  24.3 1.1 %copy-start.7 = (f32[256,512]{1,0:T(8,128)S(1)}, f32[256,512]{1,0:T(8,128)}, u32[]{:S(2)}) copy-start(f32[256,512]{1,0:T(8,128)} %param.16) | copy-start | bytes 1572868
  24.3 1.3 %copy-start.8 = (f32[256,512]{1,0:T(8,128)S(1)}, f32[256,512]{1,0:T(8,128)}, u32[]{:S(2)}) copy-start(f32[256,512]{1,0:T(8,128)} %param.15) | copy-start | bytes 1572868
  24.4 1.3 %copy-start.9 = (f32[256,128]{1,0:T(8,128)}, f32[256,128]{1,0:T(8,128)S(1)}, u32[]{:S(2)}) copy-start(f32[256,128]{1,0:T(8,128)S(1)} %pad.65) | copy-start | bytes 393220
  24.4 1.3 %copy-start.11 = (f32[256,128]{1,0:T(8,128)}, f32[256,128]{1,0:T(8,128)S(1)}, u32[]{:S(2)}) copy-start(f32[256,128]{1,0:T(8,128)S(1)} %pad.63) | copy-start | bytes 393220
  24.8 0.9 copy-start.13
  25.6 0.7 copy-start.15
  25.6 13.0 %copy-start.18 = (pred[8]{0:T(512)(128)(4,1)S(1)}, pred[8]{0:T(512)(128)(4,1)}, u32[]{:S(2)}) copy-start(pred[8]{0:T(512)(128)(4,1)} %constant.4.clone.1) | copy-start | bytes 28
  26.3 12.4 %collective-permute-start.7 = (f32[9,768]{1,0:T(8,128)S(1)}, f32[9,768]{1,0:T(8,128)S(1)}, u32[]{:S(2)}, u32[]{:S(2)}) collective-permute-start(f32[9,768]{1,0:T(8,128)S(1)} %get-tuple-element.20), channel_id=1, source_target_pairs={{1,0},{2,1},{3,2},{4,3},{5,4},{6,5},{7,6},{8,7},{9,8},{10,9},{11,1... | collective-permute-start | bytes 82952 | tf_op jit(solution)/shard_map/ppermute | solution.py:230
  27.6 11.8 %collective-permute-start.6 = (f32[9,768]{1,0:T(8,128)S(1)}, f32[9,768]{1,0:T(8,128)S(1)}, u32[]{:S(2)}, u32[]{:S(2)}) collective-permute-start(f32[9,768]{1,0:T(8,128)S(1)} %get-tuple-element.21), channel_id=1, source_target_pairs={{0,1},{1,2},{2,3},{3,4},{4,5},{5,6},{6,7},{7,8},{8,9},{9,10},{10,1... | collective-permute-start | bytes 82952 | tf_op jit(solution)/shard_map/ppermute | solution.py:230
  43.8 7.0 %copy-start.10 = (f32[256,128]{1,0:T(8,128)S(1)}, f32[256,128]{1,0:T(8,128)}, u32[]{:S(2)}) copy-start(f32[256,128]{1,0:T(8,128)} %copy-done.9) | copy-start | bytes 393220
  43.8 7.0 %copy-start.12 = (f32[256,128]{1,0:T(8,128)S(1)}, f32[256,128]{1,0:T(8,128)}, u32[]{:S(2)}) copy-start(f32[256,128]{1,0:T(8,128)} %copy-done.11) | copy-start | bytes 393220
  43.8 7.0 %copy-start.14 = (f32[256,128]{1,0:T(8,128)S(1)}, f32[256,128]{1,0:T(8,128)}, u32[]{:S(2)}) copy-start(f32[256,128]{1,0:T(8,128)} %copy-done.13) | copy-start | bytes 393220
  43.8 7.0 %copy-start.16 = (f32[256,128]{1,0:T(8,128)S(1)}, f32[256,128]{1,0:T(8,128)}, u32[]{:S(2)}) copy-start(f32[256,128]{1,0:T(8,128)} %copy-done.15) | copy-start | bytes 393220
  43.8 7.0 %copy-start.17 = (f32[3,768]{1,0:T(4,128)S(1)}, f32[3,768]{1,0:T(4,128)}, u32[]{:S(2)}) copy-start(f32[3,768]{1,0:T(4,128)} %get-tuple-element.42) | copy-start | bytes 27652
  45.2 5.7 %collective-permute-start = (f32[2,256]{0,1:T(8,128)S(1)}, f32[2,256]{0,1:T(8,128)S(1)}, u32[]{:S(2)}, u32[]{:S(2)}) collective-permute-start(f32[2,256]{0,1:T(8,128)S(1)} %get-tuple-element.30), channel_id=1, source_target_pairs={{0,16},{16,32},{32,48},{48,64},{64,80},{80,96},{96,112},{1,17},{17... | collective-permute-start | bytes 6152 | tf_op jit(solution)/shard_map/ppermute | solution.py:230
  48.8 6.3 %collective-permute-start.1 = (f32[2,256]{0,1:T(8,128)S(1)}, f32[2,256]{0,1:T(8,128)S(1)}, u32[]{:S(2)}, u32[]{:S(2)}) collective-permute-start(f32[2,256]{0,1:T(8,128)S(1)} %get-tuple-element.31), channel_id=1, source_target_pairs={{16,0},{32,16},{48,32},{64,48},{80,64},{96,80},{112,96},{17,1},{33... | collective-permute-start | bytes 6152 | tf_op jit(solution)/shard_map/ppermute | solution.py:230
  55.2 5.5 %collective-permute-start.2 = (f32[2,768]{1,0:T(2,128)S(1)}, f32[2,768]{1,0:T(2,128)S(1)}, u32[]{:S(2)}, u32[]{:S(2)}) collective-permute-start(f32[2,768]{1,0:T(2,128)S(1)} %get-tuple-element.22), channel_id=1, source_target_pairs={{0,1},{1,2},{2,3},{3,4},{4,5},{5,6},{6,7},{7,8},{8,9},{9,10},{10,1... | collective-permute-start | bytes 18440 | tf_op jit(solution)/shard_map/ppermute | solution.py:230
  57.6 4.4 %collective-permute-start.3 = (f32[2,768]{1,0:T(2,128)S(1)}, f32[2,768]{1,0:T(2,128)S(1)}, u32[]{:S(2)}, u32[]{:S(2)}) collective-permute-start(f32[2,768]{1,0:T(2,128)S(1)} %get-tuple-element.23), channel_id=1, source_target_pairs={{1,0},{2,1},{3,2},{4,3},{5,4},{6,5},{7,6},{8,7},{9,8},{10,9},{11,1... | collective-permute-start | bytes 18440 | tf_op jit(solution)/shard_map/ppermute | solution.py:230
  64.4 26.9 %copy-start.3 = (f32[1024,128]{1,0:T(8,128)S(1)}, f32[1024,128]{1,0:T(8,128)}, u32[]{:S(2)}) copy-start(f32[1024,128]{1,0:T(8,128)} %tc_ref.1) | copy-start | bytes 1572868

commit v2 on v1

v2 whole, which is shorter than its diff:
```python
import functools
import jax
import jax.numpy as jnp
from jax import lax
from jax.experimental import pallas as pl
from jax.experimental.pallas import tpu as pltpu
from jax.sharding import PartitionSpec as P

F32 = jnp.float32
BF16 = jnp.bfloat16
I32 = jnp.int32
RIM = 8
SIDE = 128


def iota(shape, dim):
    return lax.broadcasted_iota(I32, shape, dim)


def halves(x):
    high = x.astype(BF16)
    low = (x - high.astype(F32)).astype(BF16)
    return high, low


def select(mask):
    return jnp.where(mask, 1.0, 0.0).astype(BF16)


def joined(y):
    return y[:, :128] + y[:, 128:]


def route_kernel(owners, slots, rows, near, dev_hbm, tile_hbm, er_hbm, ei_hbm, sg_hbm, out_ref, slot_ref, dev_ref, tile_ref, er_ref, ei_ref, sg_ref, pair_ref, send_ref, ids_ref, rims_ref, sems, out_sems):
    count = er_ref.shape[0]
    blocks = count // 128
    copies = [
        pltpu.make_async_copy(source, target, sems.at[k])
        for k, (source, target) in enumerate(
            (
                (dev_hbm, dev_ref),
                (tile_hbm, tile_ref),
                (er_hbm, er_ref),
                (ei_hbm, ei_ref),
                (sg_hbm, sg_ref),
            )
        )
    ]
    for copy in copies:
        copy.start()
    copies[0].wait()
    copies[1].wait()
    dev = dev_ref[...]
    tile = tile_ref[...]
    tile = (tile & 3) * rows + (tile >> 2)
    hits = [jnp.broadcast_to(dev[b : b + 1], (owners, 128)) == iota((owners, 128), 0) for b in range(blocks)]
    ahead = select(iota((128, 256), 0) < iota((128, 256), 1))
    sums = jnp.dot(
        jnp.concatenate([select(h) for h in hits], axis=0), ahead, preferred_element_type=F32
    )
    carry = jnp.zeros((owners, 128), F32)
    ranks = []
    for b in range(blocks):
        part = sums[b * owners : (b + 1) * owners]
        ranks.append(
            jnp.sum(jnp.where(hits[b], part[:, :128] + carry, 0.0), axis=0, keepdims=True)
        )
        carry = carry + part[:, 128:]
    rank = jnp.concatenate(ranks, axis=0).astype(I32)
    slot_ref[...] = dev * slots + rank
    line = lambda x: jnp.concatenate([x[b : b + 1] for b in range(blocks)], axis=1)
    place = line(dev * (slots + 1) + rank)
    hit = jnp.concatenate(hits, axis=1)
    tiles = line(tile)
    upper = jnp.where(hit, jnp.broadcast_to(tiles >> 5, (owners, count)), 0)
    lower = jnp.where(hit, jnp.broadcast_to(tiles & 31, (owners, count)), 0)
    numbers = jnp.concatenate([upper, lower], axis=0).astype(F32).astype(BF16)
    which = select(jnp.broadcast_to(line(rank), (128, count)) == iota((128, count), 0))
    ids = lax.dot_general(
        numbers, which, (((1,), (1,)), ((), ())), preferred_element_type=F32
    )
    none = jnp.zeros((near, 128), F32)
    for ref in (ids_ref, rims_ref):
        ref[:near] = none
        ref[near + owners :] = none
    ids_ref[near : near + owners] = ids[:owners] * 32.0 + ids[owners:]
    for copy in copies[2:]:
        copy.wait()
    er = er_ref[...]
    ei = ei_ref[...]
    high, low = halves(sg_ref[...] * (er * er + ei * ei))
    pair_ref[:, :128] = high
    pair_ref[:, 128:] = low
    part = 2 * near
    step = part * (slots + 1)
    lane = iota((part, 128), 1)
    own_at, left_at, right_at = (4 * slots + k * slots for k in range(3))
    writes = []
    for c in range(owners // part + 1):
        if c < owners // part:
            mask = jnp.broadcast_to(place, (step, count)) == iota((step, count), 0) + c * step
            send_ref[c * step : (c + 1) * step, :] = joined(
                jnp.dot(select(mask), pair_ref[...], preferred_element_type=F32)
            )
            rims = jnp.zeros((part, 128), F32)
            for r in range(slots):
                values = send_ref[pl.ds(c * step + r, part, stride=slots + 1), :]
                rims = jnp.where(lane >> 2 == r, pltpu.roll(values, 2 + 4 * r, 1), rims)
            rims_ref[near + c * part : near + (c + 1) * part] = rims
        if c > 0:
            at = (c - 1) * part
            left, own, right = (slice(at + k * near, at + k * near + part) for k in range(3))
            info = jnp.where(lane & 3 < 2, rims_ref[left], rims_ref[right])
            info = jnp.where(lane >= own_at, pltpu.roll(ids_ref[own], own_at, 1), info)
            info = jnp.where(lane >= left_at, pltpu.roll(ids_ref[left], left_at, 1), info)
            info = jnp.where(lane >= right_at, pltpu.roll(ids_ref[right], right_at, 1), info)
            send_ref[pl.ds((c - 1) * step + slots, part, stride=slots + 1), :] = info
            span = pl.ds((c - 1) * step, step)
            write = pltpu.make_async_copy(send_ref.at[span], out_ref.at[span], out_sems.at[c - 1])
            write.start()
            writes.append(write)
    for write in writes:
        write.wait()


def route(dev, tile, er, ei, sg, owners, slots, rows, near):
    count = er.shape[0]
    return pl.pallas_call(
        functools.partial(route_kernel, owners, slots, rows, near),
        out_shape=(
            jax.ShapeDtypeStruct((owners * (slots + 1), 128), F32),
            jax.ShapeDtypeStruct((count // 128, 128), I32),
        ),
        in_specs=[pl.BlockSpec(memory_space=pltpu.HBM)] * 5,
        out_specs=(pl.BlockSpec(memory_space=pltpu.HBM), pl.BlockSpec(memory_space=pltpu.VMEM)),
        scratch_shapes=[
            pltpu.VMEM((count // 128, 128), I32),
            pltpu.VMEM((count // 128, 128), I32),
            pltpu.VMEM((count, 128), F32),
            pltpu.VMEM((count, 128), F32),
            pltpu.VMEM((count, 128), F32),
            pltpu.VMEM((count, 256), BF16),
            pltpu.VMEM((owners * (slots + 1), 128), F32),
            pltpu.VMEM((owners + 2 * near, 128), F32),
            pltpu.VMEM((owners + 2 * near, 128), F32),
            pltpu.SemaphoreType.DMA((5,)),
            pltpu.SemaphoreType.DMA((owners // (2 * near),)),
        ],
        compiler_params=pltpu.CompilerParams(vmem_limit_bytes=16 << 20),
        name="route",
    )(*pinned(dev.reshape(count // 128, 128), tile.reshape(count // 128, 128), er, ei, sg))


def places(flat, first, slots):
    return jnp.concatenate([flat[first + r : first + r + 1] for r in range(slots)], axis=1)


def side_columns(x):
    lane = iota(x.shape, 1)
    x = pltpu.roll(x + pltpu.roll(x, 124, 1), 126, 1)
    return jnp.where(lane >= 126, x, 0.0), jnp.where(lane < 2, x, 0.0)


def rims_kernel(owners, slots, rows, got_ref, low_ref, high_ref, pair_ref, rims_ref, flat_ref, ids_ref, top_ref, bottom_ref):
    groups = top_ref.shape[1] // 128 - 2
    info = got_ref[pl.ds(slots, owners, stride=slots + 1), :]
    ids_ref[...] = info.astype(I32)
    flat = info.T.astype(I32)
    flat_ref[...] = flat
    lane = iota((owners, 128), 1)
    for r in range(slots):
        span = slice(r * owners, (r + 1) * owners)
        high, low = halves(got_ref[pl.ds(r, owners, stride=slots + 1), :])
        pair_ref[span, :128] = high
        pair_ref[span, 128:] = low
        values = pltpu.roll(info, (128 - 4 * r) % 128, 1)
        high = values.astype(BF16).astype(F32)
        low = pltpu.roll(values - high, 4, 1)
        rims_ref[span, :] = jnp.where(lane < 4, high, low).astype(BF16)
    own, left, right = (places(flat, 4 * slots + k * slots, slots) for k in range(3))
    shape = (8 * groups, owners * slots)
    line = iota(shape, 0)
    row = line & 7
    row = row + jnp.where(row < 4, 0, rows - 8)
    mask = jnp.broadcast_to(own, shape) == (line >> 3) * rows + row
    heat = joined(jnp.dot(select(mask), pair_ref[...], preferred_element_type=F32))
    shape = (16, owners * slots)
    line = iota(shape, 0)
    row = line & 7
    row = row + jnp.where(row < 4, 0, rows - 8)
    mask = jnp.where(
        line < 8,
        jnp.broadcast_to(left, shape) - (groups - 1) * rows,
        jnp.broadcast_to(right, shape),
    ) == row
    lows, highs = side_columns(jnp.dot(select(mask), rims_ref[...], preferred_element_type=F32))
    for ref, edge, at in ((top_ref, low_ref, 0), (bottom_ref, high_ref, 4)):
        ref[:8] = edge[:8]
        ref[12:] = edge[12:]
        for q in range(groups + 2):
            span = slice(128 * q, 128 * (q + 1))
            if q == 0:
                loss = lows[at : at + 4]
            elif q == groups + 1:
                loss = highs[8 + at : 12 + at]
            else:
                loss = heat[8 * (q - 1) + at : 8 * (q - 1) + at + 4]
            ref[8:12, span] = edge[8:12, span] + edge[12:, span] * loss


def rims(got, low, high, owners, slots, rows):
    strip = jax.ShapeDtypeStruct(low.shape, F32)
    numbers = jax.ShapeDtypeStruct((128, owners), I32)
    return pl.pallas_call(
        functools.partial(rims_kernel, owners, slots, rows),
        out_shape=(
            jax.ShapeDtypeStruct((owners * slots, 256), BF16),
            jax.ShapeDtypeStruct((owners * slots, 128), BF16),
            numbers,
            jax.ShapeDtypeStruct((owners, 128), I32),
            strip,
            strip,
        ),
        compiler_params=pltpu.CompilerParams(vmem_limit_bytes=16 << 20),
        name="rims",
    )(got, low, high)


def around(x):
    rows, cols = x.shape
    return (
        pltpu.roll(x, 1, 0) + pltpu.roll(x, rows - 1, 0)
    ) + (pltpu.roll(x, 1, 1) + pltpu.roll(x, cols - 1, 1))


def strips_kernel(width, t_hbm, hc_hbm, c_hbm, low_ref, high_ref, parts_ref, sems):
    cols = t_hbm.shape[1]
    copies = []
    for k, ref in enumerate((t_hbm, hc_hbm, c_hbm)):
        for side, at in enumerate((0, cols - 128)):
            copies.append(
                pltpu.make_async_copy(
                    ref.at[:, pl.ds(at, 128)], parts_ref.at[2 * k + side], sems.at[2 * k + side]
                )
            )
    for copy in copies:
        copy.start()
    low_ref[...] = jnp.zeros_like(low_ref)
    high_ref[...] = jnp.zeros_like(high_ref)
    for k in range(3):
        span = slice(RIM * k, RIM * k + width)
        copies[2 * k].wait()
        copies[2 * k + 1].wait()
        low_ref[span] = parts_ref[2 * k].T[:width]
        high_ref[span] = parts_ref[2 * k + 1].T[128 - width :]


def strips(t, hc, c, width):
    shape = jax.ShapeDtypeStruct((3 * RIM, t.shape[0]), F32)
    return pl.pallas_call(
        functools.partial(strips_kernel, width),
        out_shape=(shape, shape),
        in_specs=[pl.BlockSpec(memory_space=pltpu.HBM)] * 3,
        scratch_shapes=[pltpu.VMEM((6, t.shape[0], 128), F32), pltpu.SemaphoreType.DMA((6,))],
        compiler_params=pltpu.CompilerParams(vmem_limit_bytes=16 << 20),
        name="strips",
    )(t, hc, c)


def sides(part, width, rows):
    lane = iota((rows, 128), 1)
    x = jnp.concatenate([part, jnp.zeros((128 - RIM, rows), F32)], axis=0).T
    return x, pltpu.roll(x, 128 - width, 1)


def prepare_kernel(width, t_ref, hc_ref, c_ref, left_ref, right_ref, t_out, a_out, r_out, g_out, top_ref, bottom_ref):
    rows, cols = t_ref.shape
    for k, (ref, out) in enumerate(((t_ref, t_out), (hc_ref, r_out), (c_ref, a_out))):
        span = slice(RIM * k, RIM * k + RIM)
        right, _ = sides(right_ref[span], width, rows)
        _, left = sides(left_ref[span], width, rows)
        out[:, :SIDE] = left
        out[:, SIDE : SIDE + cols] = ref[...]
        out[:, SIDE + cols :] = right
    hc = r_out[...]
    c = a_out[...]
    diag = hc + 4.0 * c
    g = jnp.where(diag > 0.0, 1.0 / jnp.where(diag > 0.0, diag, 1.0), 0.0)
    g_out[...] = g
    a_out[...] = c * g
    r_out[...] = hc * t_out[...] * g
    for k, out in enumerate((t_out, a_out, r_out, g_out)):
        top_ref[4 * k : 4 * k + 4] = out[:4]
        bottom_ref[4 * k : 4 * k + 4] = out[rows - 4 :]


def prepare(t, hc, c, left, right, width):
    rows, cols = t.shape
    wide = cols + 2 * SIDE
    ext = jax.ShapeDtypeStruct((rows, wide), F32)
    strip = jax.ShapeDtypeStruct((16, wide), F32)
    return pl.pallas_call(
        functools.partial(prepare_kernel, width),
        out_shape=(ext, ext, ext, ext, strip, strip),
        compiler_params=pltpu.CompilerParams(vmem_limit_bytes=16 << 20),
        name="prepare",
    )(t, hc, c, left, right)


def middle_kernel(sweeps, slots, pair_ref, rims_ref, flat_ref, t_ref, a_ref, r_ref, g_ref, temp_ref, top_ref, bottom_ref, rhs_ref):
    rows, cols = temp_ref.shape
    groups = cols // 128
    flat = flat_ref[...]
    own, left, right = (places(flat, 4 * slots + k * slots, slots) for k in range(3))
    shape = (rows, own.shape[1])
    row = iota(shape, 0)
    match = lambda x, first: select(jnp.broadcast_to(x - first, shape) == row)
    for q in range(groups + 2):
        span = slice(q * 128, (q + 1) * 128)
        if q == 0:
            heat = jnp.dot(match(left, (groups - 1) * rows), rims_ref[...], preferred_element_type=F32)
            heat = side_columns(heat)[0]
        elif q == groups + 1:
            heat = jnp.dot(match(right, 0), rims_ref[...], preferred_element_type=F32)
            heat = side_columns(heat)[1]
        else:
            heat = joined(
                jnp.dot(match(own, (q - 1) * rows), pair_ref[...], preferred_element_type=F32)
            )
        rhs_ref[:, span] = r_ref[:, span] + g_ref[:, span] * heat
    for k, ref in enumerate((t_ref, a_ref, rhs_ref)):
        top_ref[k] = ref[: 2 * RIM]
        bottom_ref[k] = ref[rows - 2 * RIM :]
    temp = t_ref[...]
    for _ in range(sweeps):
        temp = rhs_ref[...] + a_ref[...] * around(temp)
    temp_ref[...] = temp[:, SIDE : SIDE + cols]


def middle(pair, rim, flat, t, a, r, g, cols, sweeps, slots):
    rows, wide = t.shape
    strip = jax.ShapeDtypeStruct((3, 2 * RIM, wide), F32)
    return pl.pallas_call(
        functools.partial(middle_kernel, sweeps, slots),
        out_shape=(jax.ShapeDtypeStruct((rows, cols), F32), strip, strip),
        scratch_shapes=[pltpu.VMEM((rows, wide), F32)],
        compiler_params=pltpu.CompilerParams(vmem_limit_bytes=16 << 20),
        name="middle",
    )(pair, rim, flat, t, a, r, g)


def solve_kernel(sweeps, owners, slots, above_ref, below_ref, inner_ref, top_ref, bottom_ref, ids_ref, out_ref, reply_ref, temp_ref, pair_ref, sems):
    rows, cols = inner_ref.shape
    inside = pl.ds(RIM, rows - 2 * RIM)
    writes = [pltpu.make_async_copy(inner_ref.at[inside], out_ref.at[inside], sems.at[0])]
    writes[0].start()
    none = jnp.zeros((4, top_ref.shape[2]), F32)
    groups = cols // 128
    for q in range(groups):
        high, low = halves(inner_ref[:, q * 128 : (q + 1) * 128])
        pair_ref[q * rows : (q + 1) * rows, :128] = high
        pair_ref[q * rows : (q + 1) * rows, 128:] = low
    for k, (strip, ref) in enumerate(((above_ref, top_ref), (below_ref, bottom_ref))):
        t, a, r = (
            jnp.concatenate(
                [none, strip[4 * j : 4 * j + 4], ref[j]] if k == 0 else [ref[j], strip[4 * j : 4 * j + 4], none],
                axis=0,
            )
            for j in range(3)
        )
        for _ in range(sweeps):
            t = r + a * around(t)
        t = t[RIM : 2 * RIM, SIDE : SIDE + cols]
        temp_ref[k] = t
        at = k * (rows - RIM)
        write = pltpu.make_async_copy(temp_ref.at[k], out_ref.at[pl.ds(at, RIM)], sems.at[k + 1])
        write.start()
        writes.append(write)
        for q in range(groups):
            span = slice(q * 128, (q + 1) * 128)
            both = [t[:, span], inner_ref[RIM : 2 * RIM, span]]
            if k == 1:
                both = [inner_ref[rows - 2 * RIM : rows - RIM, span], t[:, span]]
            high, low = halves(jnp.concatenate(both, axis=0))
            at = q * rows + k * (rows - 2 * RIM)
            pair_ref[at : at + 2 * RIM, :128] = high
            pair_ref[at : at + 2 * RIM, 128:] = low
    ids = ids_ref[...]
    for r in range(0, slots, 4):
        column = jnp.concatenate(
            [
                jnp.broadcast_to(ids[:, 4 * slots + k : 4 * slots + k + 1], (owners, 128))
                for k in range(r, r + 4)
            ],
            axis=0,
        )
        mask = jnp.concatenate(
            [column == iota((4 * owners, 128), 1) + 128 * k for k in range(rows * groups // 128)], axis=1
        )
        got = joined(jnp.dot(select(mask), pair_ref[...], preferred_element_type=F32))
        for k in range(4):
            reply_ref[pl.ds(r + k, owners, stride=slots), :] = got[k * owners : (k + 1) * owners]
    for write in writes:
        write.wait()


def solve(above, below, inner, top, bottom, ids, sweeps, owners, slots):
    rows, cols = inner.shape
    return pl.pallas_call(
        functools.partial(solve_kernel, sweeps, owners, slots),
        out_shape=(
            jax.ShapeDtypeStruct((rows, cols), F32),
            jax.ShapeDtypeStruct((owners * slots, 128), F32),
        ),
        out_specs=(pl.BlockSpec(memory_space=pltpu.HBM), pl.BlockSpec(memory_space=pltpu.VMEM)),
        scratch_shapes=[
            pltpu.VMEM((2, RIM, cols), F32),
            pltpu.VMEM((rows * cols // 128, 256), BF16),
            pltpu.SemaphoreType.DMA((3,)),
        ],
        compiler_params=pltpu.CompilerParams(vmem_limit_bytes=16 << 20),
        name="solve",
    )(above, below, inner, top, bottom, ids)


def final_kernel(slot_ref, back_ref, sg_ref, tc_ref, out_ref, pair_ref, new_ref, sems):
    total = back_ref.shape[0]
    blocks = slot_ref.shape[0]
    high, low = halves(back_ref[...])
    pair_ref[:, :128] = high
    pair_ref[:, 128:] = low
    slot = slot_ref[...].T
    writes = []
    for b in range(0, blocks, 4):
        column = jnp.concatenate(
            [jnp.broadcast_to(slot[:, k : k + 1], (128, 128)) for k in range(b, b + 4)], axis=0
        )
        mask = jnp.concatenate(
            [column == iota((512, 128), 1) + 128 * k for k in range(total // 128)], axis=1
        )
        hot = joined(jnp.dot(select(mask), pair_ref[...], preferred_element_type=F32))
        span = pl.ds(b * 128, 512)
        new_ref[span, :] = sg_ref[span, :] / (1.0 + tc_ref[span, :] * hot)
        write = pltpu.make_async_copy(new_ref.at[span], out_ref.at[span], sems.at[b // 4])
        write.start()
        writes.append(write)
    for write in writes:
        write.wait()


def final(slot, back, sg, tc):
    return pl.pallas_call(
        final_kernel,
        out_shape=jax.ShapeDtypeStruct(sg.shape, F32),
        out_specs=pl.BlockSpec(memory_space=pltpu.HBM),
        scratch_shapes=[
            pltpu.VMEM((back.shape[0], 256), BF16),
            pltpu.VMEM(sg.shape, F32),
            pltpu.SemaphoreType.DMA((slot.shape[0] // 4,)),
        ],
        compiler_params=pltpu.CompilerParams(vmem_limit_bytes=16 << 20),
        name="final",
    )(slot, back, sg, tc)


def swap(low_part, high_part, axis):
    count = lax.axis_size(axis)
    up = [(i, i + 1) for i in range(count - 1)]
    down = [(i + 1, i) for i in range(count - 1)]
    return lax.ppermute(high_part, axis, up), lax.ppermute(low_part, axis, down)


def exchanged(x, owners):
    rows = x.shape[0]
    x = x.reshape(owners, 1, rows // owners * 128)
    x = lax.all_to_all(x, ("em", "th"), split_axis=0, concat_axis=0, tiled=True)
    return x.reshape(rows, 128)


SWEEPS = 3


def pinned(*arrays):
    return [pltpu.with_memory_space_constraint(x, pltpu.HBM) for x in arrays]


def local(e_real, e_imag, sigma_em, temp_coef, dest_dev, dest_tile, t_old, heat_cap, conduct):
    owners = lax.axis_size("em") * lax.axis_size("th")
    slots = 2 * e_real.shape[0] // owners
    rows, cols = t_old.shape
    near = lax.axis_size("th")
    send, slot = route(dest_dev, dest_tile, e_real, e_imag, sigma_em, owners, slots, rows, near)
    got = exchanged(send, owners)
    grid = pinned(*lax.optimization_barrier((t_old, heat_cap, conduct, slot))[:3])
    low, high = strips(*grid, SWEEPS)
    left, right = swap(low, high, "em")
    t, a, r, g, low, high = prepare(*grid, left, right, SWEEPS)
    pair, rim, flat, ids, low, high = rims(got, low, high, owners, slots, rows)
    above, below = swap(low, high, "th")
    inner, top, bottom = middle(pair, rim, flat, t, a, r, g, cols, SWEEPS, slots)
    temp, reply = solve(above, below, inner, top, bottom, ids, SWEEPS, owners, slots)
    back = exchanged(reply, owners)
    return temp, final(slot, back, sigma_em, temp_coef)


def solution(mesh):
    tiles = P(("em", "th"), None)
    grid = P("th", "em")
    return jax.shard_map(
        local,
        mesh=mesh,
        in_specs=(tiles,) * 6 + (grid,) * 3,
        out_specs=(grid, tiles),
        check_vma=False,
    )
```

time: 94.1 us -> 78 us (0.83)
  starting transfers between devices: 31 us -> 20.8 us
  waiting for transfers between devices: 16.9 us -> 9.86 us
  Pallas kernels: 10.8 us -> 15.4 us
  local copies, waits for them, and re-layouts: 6.57 us -> 2.41 us
  blocking collectives: 26.9 us -> 28.5 us
    ppermute x4 -> x2, waiting for transfers between devices: 12.4 us -> 4.31 us  [swap(): lax.ppermute(low_part, axis, down)]
    ppermute x4 -> x2, starting transfers between devices: 13.5 us -> 6.04 us  [swap(): lax.ppermute(high_part, axis, up)]
    pallas_call x3 -> x5, Pallas kernels: 6.05 us -> 11.2 us  [the longest x1 4.04 us: route(): pl.pallas_call(functools.partial(route_kernel, owners, slots, rows, near)...]
    ppermute x4 -> x2, starting transfers between devices: 7.82 us -> 3.21 us  [swap(): lax.ppermute(low_part, axis, down)]
    slice x5 -> x0, local copies, waits for them, and re-layouts: 3 us -> none  [the longest x3 2.39 us: widened(): x[:, cols - width:]]
    all_to_all x1, starting transfers between devices: 9.65 us -> 11.5 us  [exchanged(): x = lax.all_to_all(x, ('em', 'th'), split_axis=0, concat_axis=0, tiled=True)]
    all_to_all x1, blocking collectives: 26.9 us -> 28.5 us  [exchanged(): x = lax.all_to_all(x, ('em', 'th'), split_axis=0, concat_axis=0, tiled=True)]
    unnamed x44 -> x12, local copies, waits for them, and re-layouts: 1.91 us -> 2.41 us
  transfers between devices with their start and end apart: 9 -> 5, of which waited for: 4 -> 4; matrix products, arithmetic and copies ran while one was open for 3% -> 0% of each run, Pallas kernels for 5% -> 8%
where the time goes in v2:
time: 78 us; the launch traced here: 77.7 us
  blocking collectives  28.5 us (37%)
  starting transfers between devices  20.8 us (27%)
  Pallas kernels  15.4 us (20%)
  waiting for transfers between devices  9.86 us (13%)
  local copies, waits for them, and re-layouts  2.41 us (3%)
    all_to_all x1, blocking collectives, exchanged(): x = lax.all_to_all(x, ('em', 'th'), split_axis=0, concat_axis=0, tiled=True)  28.5 us
    all_to_all x1, starting transfers between devices, exchanged(): x = lax.all_to_all(x, ('em', 'th'), split_axis=0, concat_axis=0, tiled=True)  11.5 us
    ppermute x2, starting transfers between devices, swap(): lax.ppermute(high_part, axis, up)  6.04 us
    all_to_all x1, waiting for transfers between devices, exchanged(): x = lax.all_to_all(x, ('em', 'th'), split_axis=0, concat_axis=0, tiled=True)  4.61 us
    ppermute x2, waiting for transfers between devices, swap(): lax.ppermute(low_part, axis, down)  4.31 us
    pallas_call x1, Pallas kernels, route(): pl.pallas_call(functools.partial(route_kernel, owners, slots, rows, near)...  4.04 us
    ppermute x2, starting transfers between devices, swap(): lax.ppermute(low_part, axis, down)  3.21 us
    pallas_call x1, Pallas kernels, middle(): pl.pallas_call(functools.partial(middle_kernel, sweeps, slots), out_shape...  2.55 us
  transfers between devices with their start and end apart: 5, of which 4 were waited for; matrix products, arithmetic and copies ran while one was open for 0% of the time, Pallas kernels for 8%

profile of v2, /device:TPU:1, one launch (start us, length us, event | category | flops | bytes accessed | tf_op | source)
XLA Modules:
  0.0 77.7 jit_solution(253263477103930264)
XLA Ops:
  0.6 4.0 %route.1 = (f32[2176,128]{1,0:T(8,128)}, s32[8,128]{1,0:T(8,128)S(1)}) custom-call(s32[8,128]{1,0:T(8,128)} %bitcast.9, s32[8,128]{1,0:T(8,128)} %bitcast.10, f32[1024,128]{1,0:T(8,128)} %er_hbm.1, f32[1024,128]{1,0:T(8,128)} %ei_hbm.1, f32[1024,128]{1,0:T(8,128)} %sg_ref.1), custom_call_target="tpu_custom_call" | custom-call | tf_op jit(solution)/shard_map/route/pallas_call | solution.py:128
  4.7 11.5 %all-to-all-start = ((f32[128,1,2176]{2,1,0:T(1,128)}), f32[128,1,2176]{2,1,0:T(1,128)S(1)}, u32[]{:S(2)}, u32[]{:S(2)}) async-start(f32[128,1,2176]{2,1,0:T(1,128)} %bitcast.2), calls=%async_computation | async-start | bytes 2228224 | tf_op jit(solution)/shard_map/all_to_all | solution.py:476
  16.2 1.4 %strips.1 = (f32[24,256]{1,0:T(8,128)S(1)}, f32[24,256]{1,0:T(8,128)S(1)}) custom-call(f32[256,512]{1,0:T(8,128)} %t_ref, f32[256,512]{1,0:T(8,128)} %hc_ref, f32[256,512]{1,0:T(8,128)} %c_ref), custom_call_target="tpu_custom_call" | custom-call | tf_op jit(solution)/shard_map/strips/pallas_call | solution.py:260
  17.6 3.7 %collective-permute-start = (f32[24,256]{1,0:T(8,128)S(1)}, f32[24,256]{1,0:T(8,128)S(1)}, u32[]{:S(2)}, u32[]{:S(2)}) collective-permute-start(f32[24,256]{1,0:T(8,128)S(1)} %get-tuple-element.31), channel_id=1, source_target_pairs={{0,16},{16,32},{32,48},{48,64},{64,80},{80,96},{96,112},{1,17},{17... | collective-permute-start | bytes 73736 | tf_op jit(solution)/shard_map/ppermute | solution.py:470
  21.3 1.9 %collective-permute-start.1 = (f32[24,256]{1,0:T(8,128)S(1)}, f32[24,256]{1,0:T(8,128)S(1)}, u32[]{:S(2)}, u32[]{:S(2)}) collective-permute-start(f32[24,256]{1,0:T(8,128)S(1)} %get-tuple-element.32), channel_id=1, source_target_pairs={{16,0},{32,16},{48,32},{64,48},{80,64},{96,80},{112,96},{17,1},{33... | collective-permute-start | bytes 73736 | tf_op jit(solution)/shard_map/ppermute | solution.py:470
  23.2 0.9 %collective-permute-done.left_ref = f32[24,256]{1,0:T(8,128)S(1)} collective-permute-done((f32[24,256]{1,0:T(8,128)S(1)}, f32[24,256]{1,0:T(8,128)S(1)}, u32[]{:S(2)}, u32[]{:S(2)}) %collective-permute-start) | collective-permute-done | bytes 24608 | tf_op jit(solution)/shard_map/ppermute | solution.py:470
  24.2 3.3 %collective-permute-done.1.right_ref = f32[24,256]{1,0:T(8,128)S(1)} collective-permute-done((f32[24,256]{1,0:T(8,128)S(1)}, f32[24,256]{1,0:T(8,128)S(1)}, u32[]{:S(2)}, u32[]{:S(2)}) %collective-permute-start.1) | collective-permute-done | bytes 24608 | tf_op jit(solution)/shard_map/ppermute | solution.py:470
  27.5 2.0 %prepare.1 = (f32[256,768]{1,0:T(8,128)S(1)}, f32[256,768]{1,0:T(8,128)S(1)}, f32[256,768]{1,0:T(8,128)S(1)}, f32[256,768]{1,0:T(8,128)S(1)}, f32[16,768]{1,0:T(8,128)S(1)}, /*index=5*/f32[16,768]{1,0:T(8,128)S(1)}) custom-call(f32[256,512]{1,0:T(8,128)} %t_ref, f32[256,512]{1,0:T(8,128)} %hc_ref, f32[256,512]{1,0:T(8,128)} %c_ref, ...), custom_call_target="tpu_custom_call" | custom-call | tf_op jit(solution)/shard_map/prepare/pallas_call | solution.py:302
  29.5 0.0 copy-start.1
  29.5 0.9 %copy-done.1 = f32[256,768]{1,0:T(8,128)} copy-done((f32[256,768]{1,0:T(8,128)}, f32[256,768]{1,0:T(8,128)S(1)}, u32[]{:S(2)}) %copy-start.1) | copy-done | bytes 786456
  30.4 0.0 copy-start.4
  30.4 0.6 copy-done.4
  31.0 4.6 %all-to-all-done = f32[128,1,2176]{2,1,0:T(1,128)S(1)} async-done(((f32[128,1,2176]{2,1,0:T(1,128)}), f32[128,1,2176]{2,1,0:T(1,128)S(1)}, u32[]{:S(2)}, u32[]{:S(2)}) %all-to-all-start) | async-done | bytes 1114144 | tf_op jit(solution)/shard_map/all_to_all | solution.py:476
  35.6 0.0 copy-start.2
  35.6 0.0 copy-start.5
  35.6 0.9 %copy-done.5 = f32[16,768]{1,0:T(8,128)S(1)} copy-done((f32[16,768]{1,0:T(8,128)S(1)}, f32[16,768]{1,0:T(8,128)}, u32[]{:S(2)}) %copy-start.5) | copy-done | bytes 49176
  36.5 1.2 %rims.1 = (bf16[2048,256]{1,0:T(8,128)(2,1)S(1)}, bf16[2048,128]{1,0:T(8,128)(2,1)S(1)}, s32[128,128]{1,0:T(8,128)S(1)}, s32[128,128]{1,0:T(8,128)S(1)}, f32[16,768]{1,0:T(8,128)S(1)}, /*index=5*/f32[16,768]{1,0:T(8,128)S(1)}) custom-call(f32[2176,128]{1,0:T(8,128)S(1)} %bitcast.6, f32[16,768]{1,0:T(8,128)S(1)} %get-tuple-element.33.low_ref, ...), custom_call_target="tpu_custom_call" | custom-call | tf_op jit(solution)/shard_map/rims/pallas_call | solution.py:214
  37.7 2.4 %collective-permute-start.2 = (f32[16,768]{1,0:T(8,128)S(1)}, f32[16,768]{1,0:T(8,128)S(1)}, u32[]{:S(2)}, u32[]{:S(2)}) collective-permute-start(f32[16,768]{1,0:T(8,128)S(1)} %get-tuple-element.35), channel_id=1, source_target_pairs={{0,1},{1,2},{2,3},{3,4},{4,5},{5,6},{6,7},{7,8},{8,9},{9,10},{10,1... | collective-permute-start | bytes 147464 | tf_op jit(solution)/shard_map/ppermute | solution.py:470
  40.1 1.3 %collective-permute-start.3 = (f32[16,768]{1,0:T(8,128)S(1)}, f32[16,768]{1,0:T(8,128)S(1)}, u32[]{:S(2)}, u32[]{:S(2)}) collective-permute-start(f32[16,768]{1,0:T(8,128)S(1)} %get-tuple-element.36), channel_id=1, source_target_pairs={{1,0},{2,1},{3,2},{4,3},{5,4},{6,5},{7,6},{8,7},{9,8},{10,9},{11,1... | collective-permute-start | bytes 147464 | tf_op jit(solution)/shard_map/ppermute | solution.py:470
  41.4 0.0 copy-done.2
  41.4 2.5 %middle.1 = (f32[256,512]{1,0:T(8,128)S(1)}, f32[3,16,768]{2,1,0:T(8,128)S(1)}, f32[3,16,768]{2,1,0:T(8,128)S(1)}) custom-call(bf16[2048,256]{1,0:T(8,128)(2,1)S(1)} %get-tuple-element.37.pair_ref, bf16[2048,128]{1,0:T(8,128)(2,1)S(1)} %get-tuple-element.38.rims_ref, s32[128,128]{1,0:T(8,128)S(1)} %get-tuple-element.39.flat_ref, ...), custom_call_target="tpu_custom_call" | custom-call | tf_op jit(solution)/shard_map/middle/pallas_call | solution.py:343
  44.0 0.0 collective-permute-done.2.above_ref
  44.0 1.0 %collective-permute-done.3.below_ref = f32[16,768]{1,0:T(8,128)S(1)} collective-permute-done((f32[16,768]{1,0:T(8,128)S(1)}, f32[16,768]{1,0:T(8,128)S(1)}, u32[]{:S(2)}, u32[]{:S(2)}) %collective-permute-start.3) | collective-permute-done | bytes 49184 | tf_op jit(solution)/shard_map/ppermute | solution.py:470
  44.9 1.8 %solve.1 = (f32[256,512]{1,0:T(8,128)}, f32[2048,128]{1,0:T(8,128)S(1)}) custom-call(f32[16,768]{1,0:T(8,128)S(1)} %collective-permute-done.2.above_ref, f32[16,768]{1,0:T(8,128)S(1)} %collective-permute-done.3.below_ref, f32[256,512]{1,0:T(8,128)S(1)} %get-tuple-element.44.inner_ref, f32[3,16,768]{2,1,0:T(8,128)S(1)} %get-tuple-element.45.top_ref, ...), custom_call_target="tpu_custom_call" | custom-call | tf_op jit(solution)/shard_map/solve/pallas_call | solution.py:409
  46.8 0.0 copy-start
  46.8 0.0 copy-start.3
  46.8 28.5 %all_to_all.10 = f32[128,1,2048]{2,1,0:T(1,128)S(1)} all-to-all(f32[128,1,2048]{2,1,0:T(1,128)S(1)} %bitcast.8), channel_id=1, replica_groups=mesh['em'=8,'th'=16] {'em','th'}, dimensions={0} | all-to-all | bytes 2097152 | tf_op jit(solution)/shard_map/all_to_all | solution.py:476
  75.3 0.0 copy-done
  75.3 0.0 copy-done.3
  75.3 2.4 %final.1 = f32[1024,128]{1,0:T(8,128)} custom-call(s32[8,128]{1,0:T(8,128)S(1)} %get-tuple-element.27.slot_ref, f32[2048,128]{1,0:T(8,128)S(1)} %bitcast.7, f32[1024,128]{1,0:T(8,128)S(1)} %copy-done, f32[1024,128]{1,0:T(8,128)S(1)} %copy-done.3), custom_call_target="tpu_custom_call" | custom-call | tf_op jit(solution)/shard_map/final/pallas_call | solution.py:452
Async XLA Ops:
  4.7 30.9 %all-to-all-start = ((f32[128,1,2176]{2,1,0:T(1,128)}), f32[128,1,2176]{2,1,0:T(1,128)S(1)}, u32[]{:S(2)}, u32[]{:S(2)}) async-start(f32[128,1,2176]{2,1,0:T(1,128)} %bitcast.2), calls=%async_computation | async-start | bytes 2228224 | tf_op jit(solution)/shard_map/all_to_all | solution.py:476
  17.6 6.5 %collective-permute-start = (f32[24,256]{1,0:T(8,128)S(1)}, f32[24,256]{1,0:T(8,128)S(1)}, u32[]{:S(2)}, u32[]{:S(2)}) collective-permute-start(f32[24,256]{1,0:T(8,128)S(1)} %get-tuple-element.31), channel_id=1, source_target_pairs={{0,16},{16,32},{32,48},{48,64},{64,80},{80,96},{96,112},{1,17},{17... | collective-permute-start | bytes 73736 | tf_op jit(solution)/shard_map/ppermute | solution.py:470
  21.3 6.2 %collective-permute-start.1 = (f32[24,256]{1,0:T(8,128)S(1)}, f32[24,256]{1,0:T(8,128)S(1)}, u32[]{:S(2)}, u32[]{:S(2)}) collective-permute-start(f32[24,256]{1,0:T(8,128)S(1)} %get-tuple-element.32), channel_id=1, source_target_pairs={{16,0},{32,16},{48,32},{64,48},{80,64},{96,80},{112,96},{17,1},{33... | collective-permute-start | bytes 73736 | tf_op jit(solution)/shard_map/ppermute | solution.py:470
  29.5 0.9 %copy-start.1 = (f32[256,768]{1,0:T(8,128)}, f32[256,768]{1,0:T(8,128)S(1)}, u32[]{:S(2)}) copy-start(f32[256,768]{1,0:T(8,128)S(1)} %get-tuple-element.43.g_ref) | copy-start | bytes 2359300
  30.4 0.6 copy-start.4
  35.6 5.8 %copy-start.2 = (f32[256,768]{1,0:T(8,128)S(1)}, f32[256,768]{1,0:T(8,128)}, u32[]{:S(2)}) copy-start(f32[256,768]{1,0:T(8,128)} %copy-done.1) | copy-start | bytes 2359300
  35.6 0.9 %copy-start.5 = (f32[16,768]{1,0:T(8,128)S(1)}, f32[16,768]{1,0:T(8,128)}, u32[]{:S(2)}) copy-start(f32[16,768]{1,0:T(8,128)} %copy-done.4) | copy-start | bytes 147460
  37.7 6.2 %collective-permute-start.2 = (f32[16,768]{1,0:T(8,128)S(1)}, f32[16,768]{1,0:T(8,128)S(1)}, u32[]{:S(2)}, u32[]{:S(2)}) collective-permute-start(f32[16,768]{1,0:T(8,128)S(1)} %get-tuple-element.35), channel_id=1, source_target_pairs={{0,1},{1,2},{2,3},{3,4},{4,5},{5,6},{6,7},{7,8},{8,9},{9,10},{10,1... | collective-permute-start | bytes 147464 | tf_op jit(solution)/shard_map/ppermute | solution.py:470
  40.1 4.8 %collective-permute-start.3 = (f32[16,768]{1,0:T(8,128)S(1)}, f32[16,768]{1,0:T(8,128)S(1)}, u32[]{:S(2)}, u32[]{:S(2)}) collective-permute-start(f32[16,768]{1,0:T(8,128)S(1)} %get-tuple-element.36), channel_id=1, source_target_pairs={{1,0},{2,1},{3,2},{4,3},{5,4},{6,5},{7,6},{8,7},{9,8},{10,9},{11,1... | collective-permute-start | bytes 147464 | tf_op jit(solution)/shard_map/ppermute | solution.py:470
  46.8 28.5 %copy-start = (f32[1024,128]{1,0:T(8,128)S(1)}, f32[1024,128]{1,0:T(8,128)}, u32[]{:S(2)}) copy-start(f32[1024,128]{1,0:T(8,128)} %sg_ref.1) | copy-start | bytes 1572868
  46.8 28.5 %copy-start.3 = (f32[1024,128]{1,0:T(8,128)S(1)}, f32[1024,128]{1,0:T(8,128)}, u32[]{:S(2)}) copy-start(f32[1024,128]{1,0:T(8,128)} %tc_ref.1) | copy-start | bytes 1572868

commit v3 on v2

--- a/solution.py
+++ b/solution.py
@@ -15,6 +15,19 @@
 
 def iota(shape, dim):
     return lax.broadcasted_iota(I32, shape, dim)
+
+
+def to_send(low, high, axis):
+    even = lax.axis_index(axis) % 2 == 0
+    return jnp.where(even, high, low), jnp.where(even, low, high)
+
+
+def received(first, second, axis, count):
+    me = lax.axis_index(axis)
+    even = me % 2 == 0
+    low = jnp.where(me > 0, jnp.where(even, second, first), 0.0)
+    high = jnp.where(me < count - 1, jnp.where(even, first, second), 0.0)
+    return low, high
 
 
 def halves(x):
@@ -161,8 +174,9 @@
     return jnp.where(lane >= 126, x, 0.0), jnp.where(lane < 2, x, 0.0)
 
 
-def rims_kernel(owners, slots, rows, got_ref, low_ref, high_ref, pair_ref, rims_ref, flat_ref, ids_ref, top_ref, bottom_ref):
-    groups = top_ref.shape[1] // 128 - 2
+def rims_kernel(owners, slots, got_ref, ext_ref, pair_ref, rims_ref, flat_ref, ids_ref, first_ref, second_ref):
+    rows = ext_ref.shape[1]
+    groups = ext_ref.shape[2] // 128 - 2
     info = got_ref[pl.ds(slots, owners, stride=slots + 1), :]
     ids_ref[...] = info.astype(I32)
     flat = info.T.astype(I32)
@@ -194,36 +208,33 @@
         jnp.broadcast_to(right, shape),
     ) == row
     lows, highs = side_columns(jnp.dot(select(mask), rims_ref[...], preferred_element_type=F32))
-    for ref, edge, at in ((top_ref, low_ref, 0), (bottom_ref, high_ref, 4)):
-        ref[:8] = edge[:8]
-        ref[12:] = edge[12:]
-        for q in range(groups + 2):
-            span = slice(128 * q, 128 * (q + 1))
-            if q == 0:
-                loss = lows[at : at + 4]
-            elif q == groups + 1:
-                loss = highs[8 + at : 12 + at]
-            else:
-                loss = heat[8 * (q - 1) + at : 8 * (q - 1) + at + 4]
-            ref[8:12, span] = edge[8:12, span] + edge[12:, span] * loss
-
-
-def rims(got, low, high, owners, slots, rows):
-    strip = jax.ShapeDtypeStruct(low.shape, F32)
-    numbers = jax.ShapeDtypeStruct((128, owners), I32)
-    return pl.pallas_call(
-        functools.partial(rims_kernel, owners, slots, rows),
+    edges = []
+    for at, rim in ((0, slice(0, 4)), (4, slice(rows - 4, rows))):
+        loss = [lows[at : at + 4]]
+        loss += [heat[8 * q + at : 8 * q + at + 4] for q in range(groups)]
+        loss += [highs[8 + at : 12 + at]]
+        rhs = ext_ref[2, rim] + ext_ref[3, rim] * jnp.concatenate(loss, axis=1)
+        edges.append((ext_ref[0, rim], ext_ref[1, rim], rhs))
+    for k in range(3):
+        span = slice(4 * k, 4 * k + 4)
+        first_ref[span], second_ref[span] = to_send(edges[0][k], edges[1][k], "th")
+
+
+def rims(got, ext, owners, slots):
+    strip = jax.ShapeDtypeStruct((12, ext.shape[2]), F32)
+    return pl.pallas_call(
+        functools.partial(rims_kernel, owners, slots),
         out_shape=(
             jax.ShapeDtypeStruct((owners * slots, 256), BF16),
             jax.ShapeDtypeStruct((owners * slots, 128), BF16),
-            numbers,
+            jax.ShapeDtypeStruct((128, owners), I32),
             jax.ShapeDtypeStruct((owners, 128), I32),
             strip,
             strip,
         ),
         compiler_params=pltpu.CompilerParams(vmem_limit_bytes=16 << 20),
         name="rims",
-    )(got, low, high)
+    )(got, ext)
 
 
 def around(x):
@@ -233,7 +244,7 @@
     ) + (pltpu.roll(x, 1, 1) + pltpu.roll(x, cols - 1, 1))
 
 
-def strips_kernel(width, t_hbm, hc_hbm, c_hbm, low_ref, high_ref, parts_ref, sems):
+def strips_kernel(width, t_hbm, hc_hbm, c_hbm, first_ref, second_ref, parts_ref, sems):
     cols = t_hbm.shape[1]
     copies = []
     for k, ref in enumerate((t_hbm, hc_hbm, c_hbm)):
@@ -245,14 +256,13 @@
             )
     for copy in copies:
         copy.start()
-    low_ref[...] = jnp.zeros_like(low_ref)
-    high_ref[...] = jnp.zeros_like(high_ref)
     for k in range(3):
-        span = slice(RIM * k, RIM * k + width)
+        span = slice(RIM * k, RIM * k + RIM)
         copies[2 * k].wait()
         copies[2 * k + 1].wait()
-        low_ref[span] = parts_ref[2 * k].T[:width]
-        high_ref[span] = parts_ref[2 * k + 1].T[128 - width :]
+        low = parts_ref[2 * k].T[:RIM]
+        high = pltpu.roll(parts_ref[2 * k + 1].T[128 - RIM :], width, 0)
+        first_ref[span], second_ref[span] = to_send(low, high, "em")
 
 
 def strips(t, hc, c, width):
@@ -273,41 +283,34 @@
     return x, pltpu.roll(x, 128 - width, 1)
 
 
-def prepare_kernel(width, t_ref, hc_ref, c_ref, left_ref, right_ref, t_out, a_out, r_out, g_out, top_ref, bottom_ref):
+def prepare_kernel(width, count, t_ref, hc_ref, c_ref, first_ref, second_ref, ext_ref):
     rows, cols = t_ref.shape
-    for k, (ref, out) in enumerate(((t_ref, t_out), (hc_ref, r_out), (c_ref, a_out))):
+    left, right = received(first_ref[...], second_ref[...], "em", count)
+    for k, ref in enumerate((t_ref, hc_ref, c_ref)):
         span = slice(RIM * k, RIM * k + RIM)
-        right, _ = sides(right_ref[span], width, rows)
-        _, left = sides(left_ref[span], width, rows)
-        out[:, :SIDE] = left
-        out[:, SIDE : SIDE + cols] = ref[...]
-        out[:, SIDE + cols :] = right
-    hc = r_out[...]
-    c = a_out[...]
+        ext_ref[k, :, :SIDE] = sides(left[span], width, rows)[1]
+        ext_ref[k, :, SIDE : SIDE + cols] = ref[...]
+        ext_ref[k, :, SIDE + cols :] = sides(right[span], width, rows)[0]
+    hc = ext_ref[1]
+    c = ext_ref[2]
     diag = hc + 4.0 * c
     g = jnp.where(diag > 0.0, 1.0 / jnp.where(diag > 0.0, diag, 1.0), 0.0)
-    g_out[...] = g
-    a_out[...] = c * g
-    r_out[...] = hc * t_out[...] * g
-    for k, out in enumerate((t_out, a_out, r_out, g_out)):
-        top_ref[4 * k : 4 * k + 4] = out[:4]
-        bottom_ref[4 * k : 4 * k + 4] = out[rows - 4 :]
-
-
-def prepare(t, hc, c, left, right, width):
+    ext_ref[1] = c * g
+    ext_ref[2] = hc * ext_ref[0] * g
+    ext_ref[3] = g
+
+
+def prepare(t, hc, c, first, second, width):
     rows, cols = t.shape
-    wide = cols + 2 * SIDE
-    ext = jax.ShapeDtypeStruct((rows, wide), F32)
-    strip = jax.ShapeDtypeStruct((16, wide), F32)
-    return pl.pallas_call(
-        functools.partial(prepare_kernel, width),
-        out_shape=(ext, ext, ext, ext, strip, strip),
+    return pl.pallas_call(
+        functools.partial(prepare_kernel, width, lax.axis_size("em")),
+        out_shape=jax.ShapeDtypeStruct((4, rows, cols + 2 * SIDE), F32),
         compiler_params=pltpu.CompilerParams(vmem_limit_bytes=16 << 20),
         name="prepare",
-    )(t, hc, c, left, right)
-
-
-def middle_kernel(sweeps, slots, pair_ref, rims_ref, flat_ref, t_ref, a_ref, r_ref, g_ref, temp_ref, top_ref, bottom_ref, rhs_ref):
+    )(t, hc, c, first, second)
+
+
+def middle_kernel(sweeps, slots, pair_ref, rims_ref, flat_ref, ext_ref, temp_ref, top_ref, bottom_ref, rhs_ref):
     rows, cols = temp_ref.shape
     groups = cols // 128
     flat = flat_ref[...]
@@ -327,18 +330,18 @@
             heat = joined(
                 jnp.dot(match(own, (q - 1) * rows), pair_ref[...], preferred_element_type=F32)
             )
-        rhs_ref[:, span] = r_ref[:, span] + g_ref[:, span] * heat
-    for k, ref in enumerate((t_ref, a_ref, rhs_ref)):
+        rhs_ref[:, span] = ext_ref[2, :, span] + ext_ref[3, :, span] * heat
+    for k, ref in enumerate((ext_ref.at[0], ext_ref.at[1], rhs_ref)):
         top_ref[k] = ref[: 2 * RIM]
         bottom_ref[k] = ref[rows - 2 * RIM :]
-    temp = t_ref[...]
+    temp = ext_ref[0]
     for _ in range(sweeps):
-        temp = rhs_ref[...] + a_ref[...] * around(temp)
+        temp = rhs_ref[...] + ext_ref[1] * around(temp)
     temp_ref[...] = temp[:, SIDE : SIDE + cols]
 
 
-def middle(pair, rim, flat, t, a, r, g, cols, sweeps, slots):
-    rows, wide = t.shape
+def middle(pair, rim, flat, ext, cols, sweeps, slots):
+    _, rows, wide = ext.shape
     strip = jax.ShapeDtypeStruct((3, 2 * RIM, wide), F32)
     return pl.pallas_call(
         functools.partial(middle_kernel, sweeps, slots),
@@ -346,10 +349,10 @@
         scratch_shapes=[pltpu.VMEM((rows, wide), F32)],
         compiler_params=pltpu.CompilerParams(vmem_limit_bytes=16 << 20),
         name="middle",
-    )(pair, rim, flat, t, a, r, g)
-
-
-def solve_kernel(sweeps, owners, slots, above_ref, below_ref, inner_ref, top_ref, bottom_ref, ids_ref, out_ref, reply_ref, temp_ref, pair_ref, sems):
+    )(pair, rim, flat, ext)
+
+
+def solve_kernel(sweeps, owners, slots, count, first_ref, second_ref, inner_ref, top_ref, bottom_ref, ids_ref, out_ref, reply_ref, temp_ref, pair_ref, sems):
     rows, cols = inner_ref.shape
     inside = pl.ds(RIM, rows - 2 * RIM)
     writes = [pltpu.make_async_copy(inner_ref.at[inside], out_ref.at[inside], sems.at[0])]
@@ -360,7 +363,8 @@
         high, low = halves(inner_ref[:, q * 128 : (q + 1) * 128])
         pair_ref[q * rows : (q + 1) * rows, :128] = high
         pair_ref[q * rows : (q + 1) * rows, 128:] = low
-    for k, (strip, ref) in enumerate(((above_ref, top_ref), (below_ref, bottom_ref))):
+    above, below = received(first_ref[...], second_ref[...], "th", count)
+    for k, (strip, ref) in enumerate(((above, top_ref), (below, bottom_ref))):
         t, a, r = (
             jnp.concatenate(
                 [none, strip[4 * j : 4 * j + 4], ref[j]] if k == 0 else [ref[j], strip[4 * j : 4 * j + 4], none],
@@ -404,10 +408,10 @@
         write.wait()
 
 
-def solve(above, below, inner, top, bottom, ids, sweeps, owners, slots):
+def solve(first, second, inner, top, bottom, ids, sweeps, owners, slots):
     rows, cols = inner.shape
     return pl.pallas_call(
-        functools.partial(solve_kernel, sweeps, owners, slots),
+        functools.partial(solve_kernel, sweeps, owners, slots, lax.axis_size("th")),
         out_shape=(
             jax.ShapeDtypeStruct((rows, cols), F32),
             jax.ShapeDtypeStruct((owners * slots, 128), F32),
@@ -420,7 +424,7 @@
         ],
         compiler_params=pltpu.CompilerParams(vmem_limit_bytes=16 << 20),
         name="solve",
-    )(above, below, inner, top, bottom, ids)
+    )(first, second, inner, top, bottom, ids)
 
 
 def final_kernel(slot_ref, back_ref, sg_ref, tc_ref, out_ref, pair_ref, new_ref, sems):
@@ -463,11 +467,21 @@
     )(slot, back, sg, tc)
 
 
-def swap(low_part, high_part, axis):
-    count = lax.axis_size(axis)
-    up = [(i, i + 1) for i in range(count - 1)]
-    down = [(i + 1, i) for i in range(count - 1)]
-    return lax.ppermute(high_part, axis, up), lax.ppermute(low_part, axis, down)
+def traded(first, second, axis):
+    n_em, n_th = lax.axis_size("em"), lax.axis_size("th")
+    near, far = [], []
+    for e in range(n_em):
+        for t in range(n_th):
+            if axis == "em":
+                mate = (e + 1 if e % 2 else e - 1) % n_em, t
+                close = e ^ 1, t
+            else:
+                mate = e, t + 1 if t % 2 else t - 1
+                mate = mate if 0 <= mate[1] < n_th else (e ^ 1, t)
+                close = e, t ^ 1
+            near.append((e * n_th + t, close[0] * n_th + close[1]))
+            far.append((e * n_th + t, mate[0] * n_th + mate[1]))
+    return lax.ppermute(first, ("em", "th"), near), lax.ppermute(second, ("em", "th"), far)
 
 
 def exchanged(x, owners):
@@ -492,13 +506,11 @@
     send, slot = route(dest_dev, dest_tile, e_real, e_imag, sigma_em, owners, slots, rows, near)
     got = exchanged(send, owners)
     grid = pinned(*lax.optimization_barrier((t_old, heat_cap, conduct, slot))[:3])
-    low, high = strips(*grid, SWEEPS)
-    left, right = swap(low, high, "em")
-    t, a, r, g, low, high = prepare(*grid, left, right, SWEEPS)
-    pair, rim, flat, ids, low, high = rims(got, low, high, owners, slots, rows)
-    above, below = swap(low, high, "th")
-    inner, top, bottom = middle(pair, rim, flat, t, a, r, g, cols, SWEEPS, slots)
-    temp, reply = solve(above, below, inner, top, bottom, ids, SWEEPS, owners, slots)
+    ext = prepare(*grid, *traded(*strips(*grid, SWEEPS), "em"), SWEEPS)
+    pair, rim, flat, ids, first, second = rims(got, ext, owners, slots)
+    first, second = traded(first, second, "th")
+    inner, top, bottom = middle(pair, rim, flat, ext, cols, SWEEPS, slots)
+    temp, reply = solve(first, second, inner, top, bottom, ids, SWEEPS, owners, slots)
     back = exchanged(reply, owners)
     return temp, final(slot, back, sigma_em, temp_coef)
 

time: 78 us -> 73.2 us (0.938)
  starting transfers between devices: 20.8 us -> 15.9 us
  waiting for transfers between devices: 9.86 us -> 13.7 us
  blocking collectives: 28.5 us -> 25.8 us
  local copies, waits for them, and re-layouts: 2.41 us -> 0.01 us
  Pallas kernels: 15.4 us -> 16.7 us
    ppermute x4, starting transfers between devices: 9.25 us -> 4.02 us  [the longest x2 2.33 us: traded(): lax.ppermute(second, ('em', 'th'), far)]
    all_to_all x1, blocking collectives: 28.5 us -> 25.8 us  [exchanged(): x = lax.all_to_all(x, ('em', 'th'), split_axis=0, concat_axis=0, tiled=True)]
    all_to_all x1, waiting for transfers between devices: 4.61 us -> 7.12 us  [exchanged(): x = lax.all_to_all(x, ('em', 'th'), split_axis=0, concat_axis=0, tiled=True)]
    unnamed x12 -> x4, local copies, waits for them, and re-layouts: 2.41 us -> 0.01 us
    ppermute x4, waiting for transfers between devices: 5.25 us -> 6.58 us  [the longest x2 6.5 us: traded(): lax.ppermute(second, ('em', 'th'), far)]
    pallas_call x3, Pallas kernels: 4.99 us -> 6.29 us  [the longest x1 2.45 us: rims(): pl.pallas_call(functools.partial(rims_kernel, owners, slots), out_shape=(...]
  transfers between devices with their start and end apart: 5 -> 5, of which waited for: 4 -> 3; matrix products, arithmetic and copies ran while one was open for 0% -> 0% of each run, Pallas kernels for 8% -> 8%
where the time goes in v3:
time: 73.2 us; the launch traced here: 72.9 us
  blocking collectives  25.8 us (35%)
  Pallas kernels  16.7 us (23%)
  starting transfers between devices  15.9 us (22%)
  waiting for transfers between devices  13.7 us (19%)
    all_to_all x1, blocking collectives, exchanged(): x = lax.all_to_all(x, ('em', 'th'), split_axis=0, concat_axis=0, tiled=True)  25.8 us
    all_to_all x1, starting transfers between devices, exchanged(): x = lax.all_to_all(x, ('em', 'th'), split_axis=0, concat_axis=0, tiled=True)  11.9 us
    all_to_all x1, waiting for transfers between devices, exchanged(): x = lax.all_to_all(x, ('em', 'th'), split_axis=0, concat_axis=0, tiled=True)  7.12 us
    ppermute x2, waiting for transfers between devices, traded(): lax.ppermute(second, ('em', 'th'), far)  6.5 us
    pallas_call x1, Pallas kernels, route(): pl.pallas_call(functools.partial(route_kernel, owners, slots, rows, near)...  4.08 us
    pallas_call x1, Pallas kernels, middle(): pl.pallas_call(functools.partial(middle_kernel, sweeps, slots), out_shape...  2.54 us
    pallas_call x1, Pallas kernels, rims(): pl.pallas_call(functools.partial(rims_kernel, owners, slots), out_shape=(...  2.45 us
    pallas_call x1, Pallas kernels, final(): pl.pallas_call(final_kernel, out_shape=jax.ShapeDtypeStruct(sg.shape, F32...  2.38 us
  transfers between devices with their start and end apart: 5, of which 3 were waited for; matrix products, arithmetic and copies ran while one was open for 0% of the time, Pallas kernels for 8%

profile of v3, /device:TPU:1, one launch (start us, length us, event | category | flops | bytes accessed | tf_op | source)
XLA Modules:
  0.0 72.9 jit_solution(11878394192698668150)
XLA Ops:
  0.6 4.1 %route.1 = (f32[2176,128]{1,0:T(8,128)}, s32[8,128]{1,0:T(8,128)S(1)}) custom-call(s32[8,128]{1,0:T(8,128)} %bitcast.8, s32[8,128]{1,0:T(8,128)} %bitcast.9, f32[1024,128]{1,0:T(8,128)} %er_hbm.1, f32[1024,128]{1,0:T(8,128)} %ei_hbm.1, f32[1024,128]{1,0:T(8,128)} %sg_ref.1), custom_call_target="tpu_custom_call" | custom-call | tf_op jit(solution)/shard_map/route/pallas_call | solution.py:141
  4.7 11.9 %all-to-all-start = ((f32[128,1,2176]{2,1,0:T(1,128)}), f32[128,1,2176]{2,1,0:T(1,128)}, u32[]{:S(2)}, u32[]{:S(2)}) async-start(f32[128,1,2176]{2,1,0:T(1,128)} %bitcast.2), calls=%async_computation | async-start | bytes 2228224 | tf_op jit(solution)/shard_map/all_to_all | solution.py:490
  16.6 1.4 %strips.1 = (f32[24,256]{1,0:T(8,128)S(1)}, f32[24,256]{1,0:T(8,128)S(1)}) custom-call(f32[256,512]{1,0:T(8,128)} %t_ref, f32[256,512]{1,0:T(8,128)} %hc_ref, f32[256,512]{1,0:T(8,128)} %c_ref), custom_call_target="tpu_custom_call" | custom-call | tf_op jit(solution)/shard_map/strips/pallas_call | solution.py:270
  18.1 1.2 %collective-permute-start = (f32[24,256]{1,0:T(8,128)S(1)}, f32[24,256]{1,0:T(8,128)S(1)}, u32[]{:S(2)}, u32[]{:S(2)}) collective-permute-start(f32[24,256]{1,0:T(8,128)S(1)} %get-tuple-element.25), channel_id=1, source_target_pairs={{0,16},{1,17},{2,18},{3,19},{4,20},{5,21},{6,22},{7,23},{8,24},{9,... | collective-permute-start | bytes 73736 | tf_op jit(solution)/shard_map/ppermute | solution.py:484
  19.3 0.8 %collective-permute-start.1 = (f32[24,256]{1,0:T(8,128)S(1)}, f32[24,256]{1,0:T(8,128)S(1)}, u32[]{:S(2)}, u32[]{:S(2)}) collective-permute-start(f32[24,256]{1,0:T(8,128)S(1)} %get-tuple-element.26), channel_id=1, source_target_pairs={{0,112},{1,113},{2,114},{3,115},{4,116},{5,117},{6,118},{7,119},{8... | collective-permute-start | bytes 73736 | tf_op jit(solution)/shard_map/ppermute | solution.py:484
  20.1 0.1 collective-permute-done.first_ref
  20.1 6.5 %collective-permute-done.1.second_ref = f32[24,256]{1,0:T(8,128)S(1)} collective-permute-done((f32[24,256]{1,0:T(8,128)S(1)}, f32[24,256]{1,0:T(8,128)S(1)}, u32[]{:S(2)}, u32[]{:S(2)}) %collective-permute-start.1) | collective-permute-done | bytes 24608 | tf_op jit(solution)/shard_map/ppermute | solution.py:484
  26.6 2.0 %prepare.1.ext_ref = f32[4,256,768]{2,1,0:T(8,128)S(1)} custom-call(f32[256,512]{1,0:T(8,128)} %t_ref, f32[256,512]{1,0:T(8,128)} %hc_ref, f32[256,512]{1,0:T(8,128)} %c_ref, f32[24,256]{1,0:T(8,128)S(1)} %collective-permute-done.first_ref, f32[24,256]{1,0:T(8,128)S(1)} %collective-permute-done.1.second_ref), custom_call_target="tpu_custom_call" | custom-call | tf_op jit(solution)/shard_map/prepare/pallas_call | solution.py:305
  28.7 7.1 %all-to-all-done = f32[128,1,2176]{2,1,0:T(1,128)} async-done(((f32[128,1,2176]{2,1,0:T(1,128)}), f32[128,1,2176]{2,1,0:T(1,128)}, u32[]{:S(2)}, u32[]{:S(2)}) %all-to-all-start) | async-done | bytes 1114144 | tf_op jit(solution)/shard_map/all_to_all | solution.py:490
  35.8 2.5 %rims.1 = (bf16[2048,256]{1,0:T(8,128)(2,1)S(1)}, bf16[2048,128]{1,0:T(8,128)(2,1)S(1)}, s32[128,128]{1,0:T(8,128)S(1)}, s32[128,128]{1,0:T(8,128)S(1)}, f32[12,768]{1,0:T(8,128)S(1)}, /*index=5*/f32[12,768]{1,0:T(8,128)S(1)}) custom-call(f32[2176,128]{1,0:T(8,128)} %bitcast.3.got_ref, f32[4,256,768]{2,1,0:T(8,128)S(1)} %prepare.1.ext_ref), custom_call_target="tpu_custom_call" | custom-call | tf_op jit(solution)/shard_map/rims/pallas_call | solution.py:225
  38.2 0.5 collective-permute-start.2
  38.7 1.6 %collective-permute-start.3 = (f32[12,768]{1,0:T(8,128)S(1)}, f32[12,768]{1,0:T(8,128)S(1)}, u32[]{:S(2)}, u32[]{:S(2)}) collective-permute-start(f32[12,768]{1,0:T(8,128)S(1)} %get-tuple-element.28), channel_id=1, source_target_pairs={{0,16},{1,2},{2,1},{3,4},{4,3},{5,6},{6,5},{7,8},{8,7},{9,10},{10,... | collective-permute-start | bytes 110600 | tf_op jit(solution)/shard_map/ppermute | solution.py:484
  40.3 2.5 %middle.1 = (f32[256,512]{1,0:T(8,128)S(1)}, f32[3,16,768]{2,1,0:T(8,128)S(1)}, f32[3,16,768]{2,1,0:T(8,128)S(1)}) custom-call(bf16[2048,256]{1,0:T(8,128)(2,1)S(1)} %get-tuple-element.29.pair_ref, bf16[2048,128]{1,0:T(8,128)(2,1)S(1)} %get-tuple-element.30.rims_ref, s32[128,128]{1,0:T(8,128)S(1)} %get-tuple-element.31.flat_ref, ...), custom_call_target="tpu_custom_call" | custom-call | tf_op jit(solution)/shard_map/middle/pallas_call | solution.py:346
  42.8 0.0 collective-permute-done.2.first_ref
  42.8 0.0 collective-permute-done.3.second_ref
  42.8 1.8 %solve.1 = (f32[256,512]{1,0:T(8,128)}, f32[2048,128]{1,0:T(8,128)S(1)}) custom-call(f32[12,768]{1,0:T(8,128)S(1)} %collective-permute-done.2.first_ref, f32[12,768]{1,0:T(8,128)S(1)} %collective-permute-done.3.second_ref, f32[256,512]{1,0:T(8,128)S(1)} %get-tuple-element.32.inner_ref, f32[3,16,768]{2,1,0:T(8,128)S(1)} %get-tuple-element.33.top_ref, ...), custom_call_target="tpu_custom_call" | custom-call | tf_op jit(solution)/shard_map/solve/pallas_call | solution.py:413
  44.7 0.0 copy-start
  44.7 0.0 copy-start.1
  44.7 25.8 %all_to_all.10 = f32[128,1,2048]{2,1,0:T(1,128)S(1)} all-to-all(f32[128,1,2048]{2,1,0:T(1,128)S(1)} %bitcast.7), channel_id=1, replica_groups=mesh['em'=8,'th'=16] {'em','th'}, dimensions={0} | all-to-all | bytes 2097152 | tf_op jit(solution)/shard_map/all_to_all | solution.py:490
  70.5 0.0 copy-done
  70.5 0.0 copy-done.1
  70.5 2.4 %final.1 = f32[1024,128]{1,0:T(8,128)} custom-call(s32[8,128]{1,0:T(8,128)S(1)} %get-tuple-element.21.slot_ref, f32[2048,128]{1,0:T(8,128)S(1)} %bitcast.6, f32[1024,128]{1,0:T(8,128)S(1)} %copy-done, f32[1024,128]{1,0:T(8,128)S(1)} %copy-done.1), custom_call_target="tpu_custom_call" | custom-call | tf_op jit(solution)/shard_map/final/pallas_call | solution.py:456
Async XLA Ops:
  4.7 31.1 %all-to-all-start = ((f32[128,1,2176]{2,1,0:T(1,128)}), f32[128,1,2176]{2,1,0:T(1,128)}, u32[]{:S(2)}, u32[]{:S(2)}) async-start(f32[128,1,2176]{2,1,0:T(1,128)} %bitcast.2), calls=%async_computation | async-start | bytes 2228224 | tf_op jit(solution)/shard_map/all_to_all | solution.py:490
  18.1 2.1 %collective-permute-start = (f32[24,256]{1,0:T(8,128)S(1)}, f32[24,256]{1,0:T(8,128)S(1)}, u32[]{:S(2)}, u32[]{:S(2)}) collective-permute-start(f32[24,256]{1,0:T(8,128)S(1)} %get-tuple-element.25), channel_id=1, source_target_pairs={{0,16},{1,17},{2,18},{3,19},{4,20},{5,21},{6,22},{7,23},{8,24},{9,... | collective-permute-start | bytes 73736 | tf_op jit(solution)/shard_map/ppermute | solution.py:484
  19.3 7.3 %collective-permute-start.1 = (f32[24,256]{1,0:T(8,128)S(1)}, f32[24,256]{1,0:T(8,128)S(1)}, u32[]{:S(2)}, u32[]{:S(2)}) collective-permute-start(f32[24,256]{1,0:T(8,128)S(1)} %get-tuple-element.26), channel_id=1, source_target_pairs={{0,112},{1,113},{2,114},{3,115},{4,116},{5,117},{6,118},{7,119},{8... | collective-permute-start | bytes 73736 | tf_op jit(solution)/shard_map/ppermute | solution.py:484
  38.2 4.6 %collective-permute-start.2 = (f32[12,768]{1,0:T(8,128)S(1)}, f32[12,768]{1,0:T(8,128)S(1)}, u32[]{:S(2)}, u32[]{:S(2)}) collective-permute-start(f32[12,768]{1,0:T(8,128)S(1)} %get-tuple-element.27), channel_id=1, source_target_pairs={{0,1},{1,0},{2,3},{3,2},{4,5},{5,4},{6,7},{7,6},{8,9},{9,8},{10,11... | collective-permute-start | bytes 110600 | tf_op jit(solution)/shard_map/ppermute | solution.py:484
  38.7 4.1 %collective-permute-start.3 = (f32[12,768]{1,0:T(8,128)S(1)}, f32[12,768]{1,0:T(8,128)S(1)}, u32[]{:S(2)}, u32[]{:S(2)}) collective-permute-start(f32[12,768]{1,0:T(8,128)S(1)} %get-tuple-element.28), channel_id=1, source_target_pairs={{0,16},{1,2},{2,1},{3,4},{4,3},{5,6},{6,5},{7,8},{8,7},{9,10},{10,... | collective-permute-start | bytes 110600 | tf_op jit(solution)/shard_map/ppermute | solution.py:484
  44.7 25.8 %copy-start = (f32[1024,128]{1,0:T(8,128)S(1)}, f32[1024,128]{1,0:T(8,128)}, u32[]{:S(2)}) copy-start(f32[1024,128]{1,0:T(8,128)} %sg_ref.1) | copy-start | bytes 1572868
  44.7 25.8 %copy-start.1 = (f32[1024,128]{1,0:T(8,128)S(1)}, f32[1024,128]{1,0:T(8,128)}, u32[]{:S(2)}) copy-start(f32[1024,128]{1,0:T(8,128)} %tc_ref.1) | copy-start | bytes 1572868

commit v4 on v3

--- a/solution.py
+++ b/solution.py
@@ -164,19 +164,23 @@
     )(*pinned(dev.reshape(count // 128, 128), tile.reshape(count // 128, 128), er, ei, sg))
 
 
+def source(t, a, g, heat):
+    return t * (1.0 - 4.0 * a) + g * heat
+
+
 def places(flat, first, slots):
     return jnp.concatenate([flat[first + r : first + r + 1] for r in range(slots)], axis=1)
 
 
-def side_columns(x):
-    lane = iota(x.shape, 1)
-    x = pltpu.roll(x + pltpu.roll(x, 124, 1), 126, 1)
-    return jnp.where(lane >= 126, x, 0.0), jnp.where(lane < 2, x, 0.0)
+def side_columns(low, high):
+    lane = iota(low.shape, 1)
+    low, high = (pltpu.roll(x + pltpu.roll(x, 124, 1), 126, 1) for x in (low, high))
+    return jnp.where(lane >= 126, low, jnp.where(lane < 2, high, 0.0))
 
 
 def rims_kernel(owners, slots, got_ref, ext_ref, pair_ref, rims_ref, flat_ref, ids_ref, first_ref, second_ref):
     rows = ext_ref.shape[1]
-    groups = ext_ref.shape[2] // 128 - 2
+    groups = ext_ref.shape[2] // 128 - 1
     info = got_ref[pl.ds(slots, owners, stride=slots + 1), :]
     ids_ref[...] = info.astype(I32)
     flat = info.T.astype(I32)
@@ -207,14 +211,13 @@
         jnp.broadcast_to(left, shape) - (groups - 1) * rows,
         jnp.broadcast_to(right, shape),
     ) == row
-    lows, highs = side_columns(jnp.dot(select(mask), rims_ref[...], preferred_element_type=F32))
+    side = jnp.dot(select(mask), rims_ref[...], preferred_element_type=F32)
+    side = side_columns(side[:8], side[8:])
     edges = []
     for at, rim in ((0, slice(0, 4)), (4, slice(rows - 4, rows))):
-        loss = [lows[at : at + 4]]
-        loss += [heat[8 * q + at : 8 * q + at + 4] for q in range(groups)]
-        loss += [highs[8 + at : 12 + at]]
-        rhs = ext_ref[2, rim] + ext_ref[3, rim] * jnp.concatenate(loss, axis=1)
-        edges.append((ext_ref[0, rim], ext_ref[1, rim], rhs))
+        loss = [heat[8 * q + at : 8 * q + at + 4] for q in range(groups)] + [side[at : at + 4]]
+        t, a = ext_ref[0, rim], ext_ref[1, rim]
+        edges.append((t, a, source(t, a, ext_ref[2, rim], jnp.concatenate(loss, axis=1))))
     for k in range(3):
         span = slice(4 * k, 4 * k + 4)
         first_ref[span], second_ref[span] = to_send(edges[0][k], edges[1][k], "th")
@@ -277,10 +280,12 @@
     )(t, hc, c)
 
 
-def sides(part, width, rows):
+def sides(left, right, width, rows):
     lane = iota((rows, 128), 1)
-    x = jnp.concatenate([part, jnp.zeros((128 - RIM, rows), F32)], axis=0).T
-    return x, pltpu.roll(x, 128 - width, 1)
+    none = jnp.zeros((128 - RIM, rows), F32)
+    left, right = (jnp.concatenate([x, none], axis=0).T for x in (left, right))
+    left = pltpu.roll(left, 128 - width, 1)
+    return jnp.where(lane >= 128 - width, left, jnp.where(lane < width, right, 0.0))
 
 
 def prepare_kernel(width, count, t_ref, hc_ref, c_ref, first_ref, second_ref, ext_ref):
@@ -288,23 +293,21 @@
     left, right = received(first_ref[...], second_ref[...], "em", count)
     for k, ref in enumerate((t_ref, hc_ref, c_ref)):
         span = slice(RIM * k, RIM * k + RIM)
-        ext_ref[k, :, :SIDE] = sides(left[span], width, rows)[1]
-        ext_ref[k, :, SIDE : SIDE + cols] = ref[...]
-        ext_ref[k, :, SIDE + cols :] = sides(right[span], width, rows)[0]
+        ext_ref[k, :, :cols] = ref[...]
+        ext_ref[k, :, cols:] = sides(left[span], right[span], width, rows)
     hc = ext_ref[1]
     c = ext_ref[2]
     diag = hc + 4.0 * c
     g = jnp.where(diag > 0.0, 1.0 / jnp.where(diag > 0.0, diag, 1.0), 0.0)
     ext_ref[1] = c * g
-    ext_ref[2] = hc * ext_ref[0] * g
-    ext_ref[3] = g
+    ext_ref[2] = g
 
 
 def prepare(t, hc, c, first, second, width):
     rows, cols = t.shape
     return pl.pallas_call(
         functools.partial(prepare_kernel, width, lax.axis_size("em")),
-        out_shape=jax.ShapeDtypeStruct((4, rows, cols + 2 * SIDE), F32),
+        out_shape=jax.ShapeDtypeStruct((3, rows, cols + SIDE), F32),
         compiler_params=pltpu.CompilerParams(vmem_limit_bytes=16 << 20),
         name="prepare",
     )(t, hc, c, first, second)
@@ -318,26 +321,25 @@
     shape = (rows, own.shape[1])
     row = iota(shape, 0)
     match = lambda x, first: select(jnp.broadcast_to(x - first, shape) == row)
-    for q in range(groups + 2):
+    for q in range(groups + 1):
         span = slice(q * 128, (q + 1) * 128)
-        if q == 0:
-            heat = jnp.dot(match(left, (groups - 1) * rows), rims_ref[...], preferred_element_type=F32)
-            heat = side_columns(heat)[0]
-        elif q == groups + 1:
-            heat = jnp.dot(match(right, 0), rims_ref[...], preferred_element_type=F32)
-            heat = side_columns(heat)[1]
+        if q == groups:
+            heat = side_columns(
+                *(
+                    jnp.dot(match(*x), rims_ref[...], preferred_element_type=F32)
+                    for x in ((left, (groups - 1) * rows), (right, 0))
+                )
+            )
         else:
-            heat = joined(
-                jnp.dot(match(own, (q - 1) * rows), pair_ref[...], preferred_element_type=F32)
-            )
-        rhs_ref[:, span] = ext_ref[2, :, span] + ext_ref[3, :, span] * heat
+            heat = joined(jnp.dot(match(own, q * rows), pair_ref[...], preferred_element_type=F32))
+        rhs_ref[:, span] = source(ext_ref[0, :, span], ext_ref[1, :, span], ext_ref[2, :, span], heat)
     for k, ref in enumerate((ext_ref.at[0], ext_ref.at[1], rhs_ref)):
         top_ref[k] = ref[: 2 * RIM]
         bottom_ref[k] = ref[rows - 2 * RIM :]
     temp = ext_ref[0]
     for _ in range(sweeps):
         temp = rhs_ref[...] + ext_ref[1] * around(temp)
-    temp_ref[...] = temp[:, SIDE : SIDE + cols]
+    temp_ref[...] = temp[:, :cols]
 
 
 def middle(pair, rim, flat, ext, cols, sweeps, slots):
@@ -374,7 +376,7 @@
         )
         for _ in range(sweeps):
             t = r + a * around(t)
-        t = t[RIM : 2 * RIM, SIDE : SIDE + cols]
+        t = t[RIM : 2 * RIM, :cols]
         temp_ref[k] = t
         at = k * (rows - RIM)
         write = pltpu.make_async_copy(temp_ref.at[k], out_ref.at[pl.ds(at, RIM)], sems.at[k + 1])

time: 73.2 us -> 71.4 us (0.975)
  Pallas kernels: 16.7 us -> 15.4 us
    pallas_call x1, Pallas kernels: 2.45 us -> 1.22 us  [rims(): pl.pallas_call(functools.partial(rims_kernel, owners, slots), out_shape=(...]
  transfers between devices with their start and end apart: 5 -> 5, of which waited for: 3 -> 2; matrix products, arithmetic and copies ran while one was open for 0% -> 0% of each run, Pallas kernels for 8% -> 8%
where the time goes in v4:
time: 71.4 us; the launch traced here: 71.1 us
  blocking collectives  25.3 us (35%)
  starting transfers between devices  15.5 us (22%)
  Pallas kernels  15.4 us (22%)
  waiting for transfers between devices  14.1 us (20%)
    all_to_all x1, blocking collectives, exchanged(): x = lax.all_to_all(x, ('em', 'th'), split_axis=0, concat_axis=0, tiled=True)  25.3 us
    all_to_all x1, starting transfers between devices, exchanged(): x = lax.all_to_all(x, ('em', 'th'), split_axis=0, concat_axis=0, tiled=True)  11.5 us
    all_to_all x1, waiting for transfers between devices, exchanged(): x = lax.all_to_all(x, ('em', 'th'), split_axis=0, concat_axis=0, tiled=True)  7.45 us
    ppermute x2, waiting for transfers between devices, traded(): lax.ppermute(second, ('em', 'th'), far)  6.65 us
    pallas_call x1, Pallas kernels, route(): pl.pallas_call(functools.partial(route_kernel, owners, slots, rows, near)...  4.06 us
    pallas_call x1, Pallas kernels, middle(): pl.pallas_call(functools.partial(middle_kernel, sweeps, slots), out_shape...  2.66 us
    ppermute x2, starting transfers between devices, traded(): lax.ppermute(second, ('em', 'th'), far)  2.4 us
    pallas_call x1, Pallas kernels, final(): pl.pallas_call(final_kernel, out_shape=jax.ShapeDtypeStruct(sg.shape, F32...  2.38 us
  transfers between devices with their start and end apart: 5, of which 2 were waited for; matrix products, arithmetic and copies ran while one was open for 0% of the time, Pallas kernels for 8%

profile of v4, /device:TPU:1, one launch (start us, length us, event | category | flops | bytes accessed | tf_op | source)
XLA Modules:
  0.0 71.1 jit_solution(17235801809050342872)
XLA Ops:
  0.6 4.1 %route.1 = (f32[2176,128]{1,0:T(8,128)}, s32[8,128]{1,0:T(8,128)S(1)}) custom-call(s32[8,128]{1,0:T(8,128)} %bitcast.9, s32[8,128]{1,0:T(8,128)} %bitcast.10, f32[1024,128]{1,0:T(8,128)} %er_hbm.1, f32[1024,128]{1,0:T(8,128)} %ei_hbm.1, f32[1024,128]{1,0:T(8,128)} %sg_ref.1), custom_call_target="tpu_custom_call" | custom-call | tf_op jit(solution)/shard_map/route/pallas_call | solution.py:141
  4.7 11.5 %all-to-all-start = ((f32[128,1,2176]{2,1,0:T(1,128)}), f32[128,1,2176]{2,1,0:T(1,128)S(1)}, u32[]{:S(2)}, u32[]{:S(2)}) async-start(f32[128,1,2176]{2,1,0:T(1,128)} %bitcast.2), calls=%async_computation | async-start | bytes 2228224 | tf_op jit(solution)/shard_map/all_to_all | solution.py:492
  16.2 1.4 %strips.1 = (f32[24,256]{1,0:T(8,128)S(1)}, f32[24,256]{1,0:T(8,128)S(1)}) custom-call(f32[256,512]{1,0:T(8,128)} %t_ref, f32[256,512]{1,0:T(8,128)} %hc_ref, f32[256,512]{1,0:T(8,128)} %c_ref), custom_call_target="tpu_custom_call" | custom-call | tf_op jit(solution)/shard_map/strips/pallas_call | solution.py:273
  17.7 1.1 %collective-permute-start = (f32[24,256]{1,0:T(8,128)S(1)}, f32[24,256]{1,0:T(8,128)S(1)}, u32[]{:S(2)}, u32[]{:S(2)}) collective-permute-start(f32[24,256]{1,0:T(8,128)S(1)} %get-tuple-element.25), channel_id=1, source_target_pairs={{0,16},{1,17},{2,18},{3,19},{4,20},{5,21},{6,22},{7,23},{8,24},{9,... | collective-permute-start | bytes 73736 | tf_op jit(solution)/shard_map/ppermute | solution.py:486
  18.8 0.8 %collective-permute-start.1 = (f32[24,256]{1,0:T(8,128)S(1)}, f32[24,256]{1,0:T(8,128)S(1)}, u32[]{:S(2)}, u32[]{:S(2)}) collective-permute-start(f32[24,256]{1,0:T(8,128)S(1)} %get-tuple-element.26), channel_id=1, source_target_pairs={{0,112},{1,113},{2,114},{3,115},{4,116},{5,117},{6,118},{7,119},{8... | collective-permute-start | bytes 73736 | tf_op jit(solution)/shard_map/ppermute | solution.py:486
  19.6 0.0 collective-permute-done.first_ref
  19.6 6.7 %collective-permute-done.1.second_ref = f32[24,256]{1,0:T(8,128)S(1)} collective-permute-done((f32[24,256]{1,0:T(8,128)S(1)}, f32[24,256]{1,0:T(8,128)S(1)}, u32[]{:S(2)}, u32[]{:S(2)}) %collective-permute-start.1) | collective-permute-done | bytes 24608 | tf_op jit(solution)/shard_map/ppermute | solution.py:486
  26.3 1.9 %prepare.1.ext_ref = f32[3,256,640]{2,1,0:T(8,128)S(1)} custom-call(f32[256,512]{1,0:T(8,128)} %t_ref, f32[256,512]{1,0:T(8,128)} %hc_ref, f32[256,512]{1,0:T(8,128)} %c_ref, f32[24,256]{1,0:T(8,128)S(1)} %collective-permute-done.first_ref, f32[24,256]{1,0:T(8,128)S(1)} %collective-permute-done.1.second_ref), custom_call_target="tpu_custom_call" | custom-call | tf_op jit(solution)/shard_map/prepare/pallas_call | solution.py:308
  28.2 7.4 %all-to-all-done = f32[128,1,2176]{2,1,0:T(1,128)S(1)} async-done(((f32[128,1,2176]{2,1,0:T(1,128)}), f32[128,1,2176]{2,1,0:T(1,128)S(1)}, u32[]{:S(2)}, u32[]{:S(2)}) %all-to-all-start) | async-done | bytes 1114144 | tf_op jit(solution)/shard_map/all_to_all | solution.py:492
  35.6 1.2 %rims.1 = (bf16[2048,256]{1,0:T(8,128)(2,1)S(1)}, bf16[2048,128]{1,0:T(8,128)(2,1)S(1)}, s32[128,128]{1,0:T(8,128)S(1)}, s32[128,128]{1,0:T(8,128)S(1)}, f32[12,640]{1,0:T(8,128)S(1)}, /*index=5*/f32[12,640]{1,0:T(8,128)S(1)}) custom-call(f32[2176,128]{1,0:T(8,128)S(1)} %bitcast.6, f32[3,256,640]{2,1,0:T(8,128)S(1)} %prepare.1.ext_ref), custom_call_target="tpu_custom_call" | custom-call | tf_op jit(solution)/shard_map/rims/pallas_call | solution.py:228
  36.9 0.5 collective-permute-start.2
  37.3 1.6 %collective-permute-start.3 = (f32[12,640]{1,0:T(8,128)S(1)}, f32[12,640]{1,0:T(8,128)S(1)}, u32[]{:S(2)}, u32[]{:S(2)}) collective-permute-start(f32[12,640]{1,0:T(8,128)S(1)} %get-tuple-element.28), channel_id=1, source_target_pairs={{0,16},{1,2},{2,1},{3,4},{4,3},{5,6},{6,5},{7,8},{8,7},{9,10},{10,... | collective-permute-start | bytes 92168 | tf_op jit(solution)/shard_map/ppermute | solution.py:486
  38.9 2.7 %middle.1 = (f32[256,512]{1,0:T(8,128)S(1)}, f32[3,16,640]{2,1,0:T(8,128)S(1)}, f32[3,16,640]{2,1,0:T(8,128)S(1)}) custom-call(bf16[2048,256]{1,0:T(8,128)(2,1)S(1)} %get-tuple-element.29.pair_ref, bf16[2048,128]{1,0:T(8,128)(2,1)S(1)} %get-tuple-element.30.rims_ref, s32[128,128]{1,0:T(8,128)S(1)} %get-tuple-element.31.flat_ref, ...), custom_call_target="tpu_custom_call" | custom-call | tf_op jit(solution)/shard_map/middle/pallas_call | solution.py:348
  41.6 0.0 collective-permute-done.2.first_ref
  41.6 0.0 collective-permute-done.3.second_ref
  41.6 1.8 %solve.1 = (f32[256,512]{1,0:T(8,128)}, f32[2048,128]{1,0:T(8,128)S(1)}) custom-call(f32[12,640]{1,0:T(8,128)S(1)} %collective-permute-done.2.first_ref, f32[12,640]{1,0:T(8,128)S(1)} %collective-permute-done.3.second_ref, f32[256,512]{1,0:T(8,128)S(1)} %get-tuple-element.32.inner_ref, f32[3,16,640]{2,1,0:T(8,128)S(1)} %get-tuple-element.33.top_ref, ...), custom_call_target="tpu_custom_call" | custom-call | tf_op jit(solution)/shard_map/solve/pallas_call | solution.py:415
  43.4 0.0 copy-start
  43.4 0.0 copy-start.1
  43.4 25.3 %all_to_all.10 = f32[128,1,2048]{2,1,0:T(1,128)S(1)} all-to-all(f32[128,1,2048]{2,1,0:T(1,128)S(1)} %bitcast.8), channel_id=1, replica_groups=mesh['em'=8,'th'=16] {'em','th'}, dimensions={0} | all-to-all | bytes 2097152 | tf_op jit(solution)/shard_map/all_to_all | solution.py:492
  68.8 0.0 copy-done
  68.8 0.0 copy-done.1
  68.8 2.4 %final.1 = f32[1024,128]{1,0:T(8,128)} custom-call(s32[8,128]{1,0:T(8,128)S(1)} %get-tuple-element.21.slot_ref, f32[2048,128]{1,0:T(8,128)S(1)} %bitcast.7, f32[1024,128]{1,0:T(8,128)S(1)} %copy-done, f32[1024,128]{1,0:T(8,128)S(1)} %copy-done.1), custom_call_target="tpu_custom_call" | custom-call | tf_op jit(solution)/shard_map/final/pallas_call | solution.py:458
Async XLA Ops:
  4.7 30.9 %all-to-all-start = ((f32[128,1,2176]{2,1,0:T(1,128)}), f32[128,1,2176]{2,1,0:T(1,128)S(1)}, u32[]{:S(2)}, u32[]{:S(2)}) async-start(f32[128,1,2176]{2,1,0:T(1,128)} %bitcast.2), calls=%async_computation | async-start | bytes 2228224 | tf_op jit(solution)/shard_map/all_to_all | solution.py:492
  17.7 2.0 %collective-permute-start = (f32[24,256]{1,0:T(8,128)S(1)}, f32[24,256]{1,0:T(8,128)S(1)}, u32[]{:S(2)}, u32[]{:S(2)}) collective-permute-start(f32[24,256]{1,0:T(8,128)S(1)} %get-tuple-element.25), channel_id=1, source_target_pairs={{0,16},{1,17},{2,18},{3,19},{4,20},{5,21},{6,22},{7,23},{8,24},{9,... | collective-permute-start | bytes 73736 | tf_op jit(solution)/shard_map/ppermute | solution.py:486
  18.8 7.5 %collective-permute-start.1 = (f32[24,256]{1,0:T(8,128)S(1)}, f32[24,256]{1,0:T(8,128)S(1)}, u32[]{:S(2)}, u32[]{:S(2)}) collective-permute-start(f32[24,256]{1,0:T(8,128)S(1)} %get-tuple-element.26), channel_id=1, source_target_pairs={{0,112},{1,113},{2,114},{3,115},{4,116},{5,117},{6,118},{7,119},{8... | collective-permute-start | bytes 73736 | tf_op jit(solution)/shard_map/ppermute | solution.py:486
  36.9 4.7 %collective-permute-start.2 = (f32[12,640]{1,0:T(8,128)S(1)}, f32[12,640]{1,0:T(8,128)S(1)}, u32[]{:S(2)}, u32[]{:S(2)}) collective-permute-start(f32[12,640]{1,0:T(8,128)S(1)} %get-tuple-element.27), channel_id=1, source_target_pairs={{0,1},{1,0},{2,3},{3,2},{4,5},{5,4},{6,7},{7,6},{8,9},{9,8},{10,11... | collective-permute-start | bytes 92168 | tf_op jit(solution)/shard_map/ppermute | solution.py:486
  37.3 4.2 %collective-permute-start.3 = (f32[12,640]{1,0:T(8,128)S(1)}, f32[12,640]{1,0:T(8,128)S(1)}, u32[]{:S(2)}, u32[]{:S(2)}) collective-permute-start(f32[12,640]{1,0:T(8,128)S(1)} %get-tuple-element.28), channel_id=1, source_target_pairs={{0,16},{1,2},{2,1},{3,4},{4,3},{5,6},{6,5},{7,8},{8,7},{9,10},{10,... | collective-permute-start | bytes 92168 | tf_op jit(solution)/shard_map/ppermute | solution.py:486
  43.4 25.4 %copy-start = (f32[1024,128]{1,0:T(8,128)S(1)}, f32[1024,128]{1,0:T(8,128)}, u32[]{:S(2)}) copy-start(f32[1024,128]{1,0:T(8,128)} %sg_ref.1) | copy-start | bytes 1572868
  43.4 25.3 %copy-start.1 = (f32[1024,128]{1,0:T(8,128)S(1)}, f32[1024,128]{1,0:T(8,128)}, u32[]{:S(2)}) copy-start(f32[1024,128]{1,0:T(8,128)} %tc_ref.1) | copy-start | bytes 1572868

commit v5 on v4

--- a/solution.py
+++ b/solution.py
@@ -313,8 +313,9 @@
     )(t, hc, c, first, second)
 
 
-def middle_kernel(sweeps, slots, pair_ref, rims_ref, flat_ref, ext_ref, temp_ref, top_ref, bottom_ref, rhs_ref):
-    rows, cols = temp_ref.shape
+def middle_kernel(sweeps, slots, pair_ref, rims_ref, flat_ref, ids_ref, ext_ref, out_ref, top_ref, bottom_ref, reply_ref, rhs_ref, temp_ref, tiles_ref, sems):
+    rows, cols = out_ref.shape
+    owners = ids_ref.shape[0]
     groups = cols // 128
     flat = flat_ref[...]
     own, left, right = (places(flat, 4 * slots + k * slots, slots) for k in range(3))
@@ -340,32 +341,63 @@
     for _ in range(sweeps):
         temp = rhs_ref[...] + ext_ref[1] * around(temp)
     temp_ref[...] = temp[:, :cols]
-
-
-def middle(pair, rim, flat, ext, cols, sweeps, slots):
+    inside = pl.ds(RIM, rows - 2 * RIM)
+    write = pltpu.make_async_copy(temp_ref.at[inside], out_ref.at[inside], sems.at[0])
+    write.start()
+    row = iota((rows, 128), 0)
+    inner = (row >= RIM) & (row < rows - RIM)
+    for q in range(groups):
+        high, low = halves(jnp.where(inner, temp[:, q * 128 : (q + 1) * 128], 0.0))
+        tiles_ref[q * rows : (q + 1) * rows, :128] = high
+        tiles_ref[q * rows : (q + 1) * rows, 128:] = low
+    for r in range(0, slots, 4):
+        column = slot_columns(ids_ref[...], 4 * slots + r, owners)
+        mask = jnp.concatenate(
+            [column == iota((4 * owners, 128), 1) + 128 * k for k in range(rows * groups // 128)], axis=1
+        )
+        reply_ref[r * owners : (r + 4) * owners] = joined(
+            jnp.dot(select(mask), tiles_ref[...], preferred_element_type=F32)
+        )
+    write.wait()
+
+
+def slot_columns(ids, first, owners):
+    return jnp.concatenate(
+        [jnp.broadcast_to(ids[:, k : k + 1], (owners, 128)) for k in range(first, first + 4)], axis=0
+    )
+
+
+def middle(pair, rim, flat, ids, ext, cols, sweeps, slots):
     _, rows, wide = ext.shape
     strip = jax.ShapeDtypeStruct((3, 2 * RIM, wide), F32)
+    onchip = pl.BlockSpec(memory_space=pltpu.VMEM)
     return pl.pallas_call(
         functools.partial(middle_kernel, sweeps, slots),
-        out_shape=(jax.ShapeDtypeStruct((rows, cols), F32), strip, strip),
-        scratch_shapes=[pltpu.VMEM((rows, wide), F32)],
+        out_shape=(
+            jax.ShapeDtypeStruct((rows, cols), F32),
+            strip,
+            strip,
+            jax.ShapeDtypeStruct((slots * ids.shape[0], 128), F32),
+        ),
+        out_specs=(pl.BlockSpec(memory_space=pltpu.HBM), onchip, onchip, onchip),
+        scratch_shapes=[
+            pltpu.VMEM((rows, wide), F32),
+            pltpu.VMEM((rows, cols), F32),
+            pltpu.VMEM((rows * cols // 128, 256), BF16),
+            pltpu.SemaphoreType.DMA((1,)),
+        ],
         compiler_params=pltpu.CompilerParams(vmem_limit_bytes=16 << 20),
         name="middle",
-    )(pair, rim, flat, ext)
-
-
-def solve_kernel(sweeps, owners, slots, count, first_ref, second_ref, inner_ref, top_ref, bottom_ref, ids_ref, out_ref, reply_ref, temp_ref, pair_ref, sems):
-    rows, cols = inner_ref.shape
-    inside = pl.ds(RIM, rows - 2 * RIM)
-    writes = [pltpu.make_async_copy(inner_ref.at[inside], out_ref.at[inside], sems.at[0])]
-    writes[0].start()
+    )(pair, rim, flat, ids, ext)
+
+
+def solve_kernel(sweeps, slots, count, first_ref, second_ref, top_ref, bottom_ref, ids_ref, part_ref, inner_ref, out_ref, reply_ref, temp_ref, tiles_ref, sems):
+    rows, cols = out_ref.shape
+    owners = ids_ref.shape[0]
+    groups = cols // 128
     none = jnp.zeros((4, top_ref.shape[2]), F32)
-    groups = cols // 128
-    for q in range(groups):
-        high, low = halves(inner_ref[:, q * 128 : (q + 1) * 128])
-        pair_ref[q * rows : (q + 1) * rows, :128] = high
-        pair_ref[q * rows : (q + 1) * rows, 128:] = low
     above, below = received(first_ref[...], second_ref[...], "th", count)
+    writes, edges = [], []
     for k, (strip, ref) in enumerate(((above, top_ref), (below, bottom_ref))):
         t, a, r = (
             jnp.concatenate(
@@ -377,56 +409,57 @@
         for _ in range(sweeps):
             t = r + a * around(t)
         t = t[RIM : 2 * RIM, :cols]
+        edges.append(t)
         temp_ref[k] = t
-        at = k * (rows - RIM)
-        write = pltpu.make_async_copy(temp_ref.at[k], out_ref.at[pl.ds(at, RIM)], sems.at[k + 1])
+        write = pltpu.make_async_copy(
+            temp_ref.at[k], out_ref.at[pl.ds(k * (rows - RIM), RIM)], sems.at[k]
+        )
         write.start()
         writes.append(write)
-        for q in range(groups):
-            span = slice(q * 128, (q + 1) * 128)
-            both = [t[:, span], inner_ref[RIM : 2 * RIM, span]]
-            if k == 1:
-                both = [inner_ref[rows - 2 * RIM : rows - RIM, span], t[:, span]]
-            high, low = halves(jnp.concatenate(both, axis=0))
-            at = q * rows + k * (rows - 2 * RIM)
-            pair_ref[at : at + 2 * RIM, :128] = high
-            pair_ref[at : at + 2 * RIM, 128:] = low
+    for q in range(128 // (2 * RIM)):
+        both = jnp.zeros((2 * RIM, 128), F32)
+        if q < groups:
+            both = jnp.concatenate([t[:, q * 128 : (q + 1) * 128] for t in edges], axis=0)
+        high, low = halves(both)
+        tiles_ref[2 * RIM * q : 2 * RIM * (q + 1), :128] = high
+        tiles_ref[2 * RIM * q : 2 * RIM * (q + 1), 128:] = low
     ids = ids_ref[...]
+    bits = rows.bit_length() - 1
+    row = ids & (rows - 1)
+    line = jnp.where(row < RIM, row, jnp.where(row >= rows - RIM, row - (rows - 2 * RIM), -128))
+    code = (ids >> bits) * (2 * RIM) + line
+    lane = iota((4 * owners, 128), 1)
     for r in range(0, slots, 4):
-        column = jnp.concatenate(
-            [
-                jnp.broadcast_to(ids[:, 4 * slots + k : 4 * slots + k + 1], (owners, 128))
-                for k in range(r, r + 4)
-            ],
-            axis=0,
-        )
-        mask = jnp.concatenate(
-            [column == iota((4 * owners, 128), 1) + 128 * k for k in range(rows * groups // 128)], axis=1
-        )
-        got = joined(jnp.dot(select(mask), pair_ref[...], preferred_element_type=F32))
+        mask = slot_columns(code, 4 * slots + r, owners) == lane
+        got = part_ref[r * owners : (r + 4) * owners] + joined(
+            jnp.dot(select(mask), tiles_ref[...], preferred_element_type=F32)
+        )
         for k in range(4):
             reply_ref[pl.ds(r + k, owners, stride=slots), :] = got[k * owners : (k + 1) * owners]
     for write in writes:
         write.wait()
 
 
-def solve(first, second, inner, top, bottom, ids, sweeps, owners, slots):
+def solve(first, second, top, bottom, ids, part, inner, sweeps, owners, slots):
     rows, cols = inner.shape
-    return pl.pallas_call(
-        functools.partial(solve_kernel, sweeps, owners, slots, lax.axis_size("th")),
+    onchip = pl.BlockSpec(memory_space=pltpu.VMEM)
+    return pl.pallas_call(
+        functools.partial(solve_kernel, sweeps, slots, lax.axis_size("th")),
         out_shape=(
             jax.ShapeDtypeStruct((rows, cols), F32),
             jax.ShapeDtypeStruct((owners * slots, 128), F32),
         ),
-        out_specs=(pl.BlockSpec(memory_space=pltpu.HBM), pl.BlockSpec(memory_space=pltpu.VMEM)),
+        in_specs=[onchip] * 6 + [pl.BlockSpec(memory_space=pltpu.HBM)],
+        out_specs=(pl.BlockSpec(memory_space=pltpu.HBM), onchip),
         scratch_shapes=[
             pltpu.VMEM((2, RIM, cols), F32),
-            pltpu.VMEM((rows * cols // 128, 256), BF16),
-            pltpu.SemaphoreType.DMA((3,)),
+            pltpu.VMEM((128, 256), BF16),
+            pltpu.SemaphoreType.DMA((2,)),
         ],
+        input_output_aliases={6: 0},
         compiler_params=pltpu.CompilerParams(vmem_limit_bytes=16 << 20),
         name="solve",
-    )(first, second, inner, top, bottom, ids)
+    )(first, second, top, bottom, ids, part, inner)
 
 
 def final_kernel(slot_ref, back_ref, sg_ref, tc_ref, out_ref, pair_ref, new_ref, sems):
@@ -511,8 +544,9 @@
     ext = prepare(*grid, *traded(*strips(*grid, SWEEPS), "em"), SWEEPS)
     pair, rim, flat, ids, first, second = rims(got, ext, owners, slots)
     first, second = traded(first, second, "th")
-    inner, top, bottom = middle(pair, rim, flat, ext, cols, SWEEPS, slots)
-    temp, reply = solve(first, second, inner, top, bottom, ids, SWEEPS, owners, slots)
+    inner, top, bottom, part = middle(pair, rim, flat, ids, ext, cols, SWEEPS, slots)
+    (inner,) = pinned(inner)
+    temp, reply = solve(first, second, top, bottom, ids, part, inner, SWEEPS, owners, slots)
     back = exchanged(reply, owners)
     return temp, final(slot, back, sigma_em, temp_coef)
 

time: 71.4 us -> 70.6 us (0.989)
  blocking collectives: 25.3 us -> 24.1 us
    pallas_call x1, Pallas kernels: 2.66 us -> 3.93 us  [middle(): pl.pallas_call(functools.partial(middle_kernel, sweeps, slots), out_shape...]
    all_to_all x1, blocking collectives: 25.3 us -> 24.1 us  [exchanged(): x = lax.all_to_all(x, ('em', 'th'), split_axis=0, concat_axis=0, tiled=True)]
    pallas_call x1, Pallas kernels: 1.8 us -> 1.02 us  [solve(): pl.pallas_call(functools.partial(solve_kernel, sweeps, slots, lax.axis_si...]
  transfers between devices with their start and end apart: 5 -> 5, of which waited for: 2 -> 2; matrix products, arithmetic and copies ran while one was open for 0% -> 0% of each run, Pallas kernels for 8% -> 10%
where the time goes in v5:
time: 70.6 us; the launch traced here: 70.4 us
  blocking collectives  24.1 us (34%)
  Pallas kernels  15.9 us (23%)
  starting transfers between devices  15.5 us (22%)
  waiting for transfers between devices  14.1 us (20%)
  between operations  0.72 us (1%)
    all_to_all x1, blocking collectives, exchanged(): x = lax.all_to_all(x, ('em', 'th'), split_axis=0, concat_axis=0, tiled=True)  24.1 us
    all_to_all x1, starting transfers between devices, exchanged(): x = lax.all_to_all(x, ('em', 'th'), split_axis=0, concat_axis=0, tiled=True)  11.5 us
    all_to_all x1, waiting for transfers between devices, exchanged(): x = lax.all_to_all(x, ('em', 'th'), split_axis=0, concat_axis=0, tiled=True)  7.45 us
    ppermute x2, waiting for transfers between devices, traded(): lax.ppermute(second, ('em', 'th'), far)  6.65 us
    pallas_call x1, Pallas kernels, route(): pl.pallas_call(functools.partial(route_kernel, owners, slots, rows, near)...  4.06 us
    pallas_call x1, Pallas kernels, middle(): pl.pallas_call(functools.partial(middle_kernel, sweeps, slots), out_shape...  3.93 us
    ppermute x2, starting transfers between devices, traded(): lax.ppermute(second, ('em', 'th'), far)  2.4 us
    pallas_call x1, Pallas kernels, final(): pl.pallas_call(final_kernel, out_shape=jax.ShapeDtypeStruct(sg.shape, F32...  2.38 us
  transfers between devices with their start and end apart: 5, of which 2 were waited for; matrix products, arithmetic and copies ran while one was open for 0% of the time, Pallas kernels for 10%

profile of v5, /device:TPU:1, one launch (start us, length us, event | category | flops | bytes accessed | tf_op | source)
XLA Modules:
  0.0 70.4 jit_solution(17426334231896107580)
XLA Ops:
  0.6 4.1 %route.1 = (f32[2176,128]{1,0:T(8,128)}, s32[8,128]{1,0:T(8,128)S(1)}) custom-call(s32[8,128]{1,0:T(8,128)} %bitcast.9, s32[8,128]{1,0:T(8,128)} %bitcast.10, f32[1024,128]{1,0:T(8,128)} %er_hbm.1, f32[1024,128]{1,0:T(8,128)} %ei_hbm.1, f32[1024,128]{1,0:T(8,128)} %sg_ref.1), custom_call_target="tpu_custom_call" | custom-call | tf_op jit(solution)/shard_map/route/pallas_call | solution.py:141
  4.7 11.5 %all-to-all-start = ((f32[128,1,2176]{2,1,0:T(1,128)}), f32[128,1,2176]{2,1,0:T(1,128)S(1)}, u32[]{:S(2)}, u32[]{:S(2)}) async-start(f32[128,1,2176]{2,1,0:T(1,128)} %bitcast.2), calls=%async_computation | async-start | bytes 2228224 | tf_op jit(solution)/shard_map/all_to_all | solution.py:525
  16.2 1.4 %strips.1 = (f32[24,256]{1,0:T(8,128)S(1)}, f32[24,256]{1,0:T(8,128)S(1)}) custom-call(f32[256,512]{1,0:T(8,128)} %t_ref, f32[256,512]{1,0:T(8,128)} %hc_ref, f32[256,512]{1,0:T(8,128)} %c_ref), custom_call_target="tpu_custom_call" | custom-call | tf_op jit(solution)/shard_map/strips/pallas_call | solution.py:273
  17.7 1.1 %collective-permute-start = (f32[24,256]{1,0:T(8,128)S(1)}, f32[24,256]{1,0:T(8,128)S(1)}, u32[]{:S(2)}, u32[]{:S(2)}) collective-permute-start(f32[24,256]{1,0:T(8,128)S(1)} %get-tuple-element.26), channel_id=1, source_target_pairs={{0,16},{1,17},{2,18},{3,19},{4,20},{5,21},{6,22},{7,23},{8,24},{9,... | collective-permute-start | bytes 73736 | tf_op jit(solution)/shard_map/ppermute | solution.py:519
  18.8 0.8 %collective-permute-start.1 = (f32[24,256]{1,0:T(8,128)S(1)}, f32[24,256]{1,0:T(8,128)S(1)}, u32[]{:S(2)}, u32[]{:S(2)}) collective-permute-start(f32[24,256]{1,0:T(8,128)S(1)} %get-tuple-element.27), channel_id=1, source_target_pairs={{0,112},{1,113},{2,114},{3,115},{4,116},{5,117},{6,118},{7,119},{8... | collective-permute-start | bytes 73736 | tf_op jit(solution)/shard_map/ppermute | solution.py:519
  19.6 0.0 collective-permute-done.first_ref
  19.6 6.7 %collective-permute-done.1.second_ref = f32[24,256]{1,0:T(8,128)S(1)} collective-permute-done((f32[24,256]{1,0:T(8,128)S(1)}, f32[24,256]{1,0:T(8,128)S(1)}, u32[]{:S(2)}, u32[]{:S(2)}) %collective-permute-start.1) | collective-permute-done | bytes 24608 | tf_op jit(solution)/shard_map/ppermute | solution.py:519
  26.3 1.9 %prepare.1.ext_ref = f32[3,256,640]{2,1,0:T(8,128)S(1)} custom-call(f32[256,512]{1,0:T(8,128)} %t_ref, f32[256,512]{1,0:T(8,128)} %hc_ref, f32[256,512]{1,0:T(8,128)} %c_ref, f32[24,256]{1,0:T(8,128)S(1)} %collective-permute-done.first_ref, f32[24,256]{1,0:T(8,128)S(1)} %collective-permute-done.1.second_ref), custom_call_target="tpu_custom_call" | custom-call | tf_op jit(solution)/shard_map/prepare/pallas_call | solution.py:308
  28.2 7.4 %all-to-all-done = f32[128,1,2176]{2,1,0:T(1,128)S(1)} async-done(((f32[128,1,2176]{2,1,0:T(1,128)}), f32[128,1,2176]{2,1,0:T(1,128)S(1)}, u32[]{:S(2)}, u32[]{:S(2)}) %all-to-all-start) | async-done | bytes 1114144 | tf_op jit(solution)/shard_map/all_to_all | solution.py:525
  35.6 1.2 %rims.1 = (bf16[2048,256]{1,0:T(8,128)(2,1)S(1)}, bf16[2048,128]{1,0:T(8,128)(2,1)S(1)}, s32[128,128]{1,0:T(8,128)S(1)}, s32[128,128]{1,0:T(8,128)S(1)}, f32[12,640]{1,0:T(8,128)S(1)}, /*index=5*/f32[12,640]{1,0:T(8,128)S(1)}) custom-call(f32[2176,128]{1,0:T(8,128)S(1)} %bitcast.6, f32[3,256,640]{2,1,0:T(8,128)S(1)} %prepare.1.ext_ref), custom_call_target="tpu_custom_call" | custom-call | tf_op jit(solution)/shard_map/rims/pallas_call | solution.py:228
  36.9 0.5 collective-permute-start.2
  37.3 1.6 %collective-permute-start.3 = (f32[12,640]{1,0:T(8,128)S(1)}, f32[12,640]{1,0:T(8,128)S(1)}, u32[]{:S(2)}, u32[]{:S(2)}) collective-permute-start(f32[12,640]{1,0:T(8,128)S(1)} %get-tuple-element.29), channel_id=1, source_target_pairs={{0,16},{1,2},{2,1},{3,4},{4,3},{5,6},{6,5},{7,8},{8,7},{9,10},{10,... | collective-permute-start | bytes 92168 | tf_op jit(solution)/shard_map/ppermute | solution.py:519
  38.9 3.9 %middle.1 = (f32[256,512]{1,0:T(8,128)}, f32[3,16,640]{2,1,0:T(8,128)S(1)}, f32[3,16,640]{2,1,0:T(8,128)S(1)}, f32[2048,128]{1,0:T(8,128)S(1)}) custom-call(bf16[2048,256]{1,0:T(8,128)(2,1)S(1)} %get-tuple-element.30.pair_ref, bf16[2048,128]{1,0:T(8,128)(2,1)S(1)} %get-tuple-element.31.rims_ref, s32[128,128]{1,0:T(8,128)S(1)} %get-tuple-element.32.flat_ref, ...), custom_call_target="tpu_custom_call" | custom-call | tf_op jit(solution)/shard_map/middle/pallas_call | solution.py:374
  42.8 0.0 collective-permute-done.2.first_ref
  42.9 0.0 collective-permute-done.3.second_ref
  42.9 1.0 %solve.1 = (f32[256,512]{1,0:T(8,128)}, f32[2048,128]{1,0:T(8,128)S(1)}) custom-call(f32[12,640]{1,0:T(8,128)S(1)} %collective-permute-done.2.first_ref, f32[12,640]{1,0:T(8,128)S(1)} %collective-permute-done.3.second_ref, f32[3,16,640]{2,1,0:T(8,128)S(1)} %get-tuple-element.34.top_ref, ...), custom_call_target="tpu_custom_call", output_to_operand_aliasing={{0}: (6, {})} | custom-call | tf_op jit(solution)/shard_map/solve/pallas_call | solution.py:446
  43.9 0.0 copy-start
  43.9 0.0 copy-start.1
  43.9 24.1 %all_to_all.10 = f32[128,1,2048]{2,1,0:T(1,128)S(1)} all-to-all(f32[128,1,2048]{2,1,0:T(1,128)S(1)} %bitcast.8), channel_id=1, replica_groups=mesh['em'=8,'th'=16] {'em','th'}, dimensions={0} | all-to-all | bytes 2097152 | tf_op jit(solution)/shard_map/all_to_all | solution.py:525
  68.0 0.0 copy-done
  68.0 0.0 copy-done.1
  68.0 2.4 %final.1 = f32[1024,128]{1,0:T(8,128)} custom-call(s32[8,128]{1,0:T(8,128)S(1)} %get-tuple-element.22.slot_ref, f32[2048,128]{1,0:T(8,128)S(1)} %bitcast.7, f32[1024,128]{1,0:T(8,128)S(1)} %copy-done, f32[1024,128]{1,0:T(8,128)S(1)} %copy-done.1), custom_call_target="tpu_custom_call" | custom-call | tf_op jit(solution)/shard_map/final/pallas_call | solution.py:491
Async XLA Ops:
  4.7 30.9 %all-to-all-start = ((f32[128,1,2176]{2,1,0:T(1,128)}), f32[128,1,2176]{2,1,0:T(1,128)S(1)}, u32[]{:S(2)}, u32[]{:S(2)}) async-start(f32[128,1,2176]{2,1,0:T(1,128)} %bitcast.2), calls=%async_computation | async-start | bytes 2228224 | tf_op jit(solution)/shard_map/all_to_all | solution.py:525
  17.7 2.0 %collective-permute-start = (f32[24,256]{1,0:T(8,128)S(1)}, f32[24,256]{1,0:T(8,128)S(1)}, u32[]{:S(2)}, u32[]{:S(2)}) collective-permute-start(f32[24,256]{1,0:T(8,128)S(1)} %get-tuple-element.26), channel_id=1, source_target_pairs={{0,16},{1,17},{2,18},{3,19},{4,20},{5,21},{6,22},{7,23},{8,24},{9,... | collective-permute-start | bytes 73736 | tf_op jit(solution)/shard_map/ppermute | solution.py:519
  18.8 7.5 %collective-permute-start.1 = (f32[24,256]{1,0:T(8,128)S(1)}, f32[24,256]{1,0:T(8,128)S(1)}, u32[]{:S(2)}, u32[]{:S(2)}) collective-permute-start(f32[24,256]{1,0:T(8,128)S(1)} %get-tuple-element.27), channel_id=1, source_target_pairs={{0,112},{1,113},{2,114},{3,115},{4,116},{5,117},{6,118},{7,119},{8... | collective-permute-start | bytes 73736 | tf_op jit(solution)/shard_map/ppermute | solution.py:519
  36.9 6.0 %collective-permute-start.2 = (f32[12,640]{1,0:T(8,128)S(1)}, f32[12,640]{1,0:T(8,128)S(1)}, u32[]{:S(2)}, u32[]{:S(2)}) collective-permute-start(f32[12,640]{1,0:T(8,128)S(1)} %get-tuple-element.28), channel_id=1, source_target_pairs={{0,1},{1,0},{2,3},{3,2},{4,5},{5,4},{6,7},{7,6},{8,9},{9,8},{10,11... | collective-permute-start | bytes 92168 | tf_op jit(solution)/shard_map/ppermute | solution.py:519
  37.3 5.5 %collective-permute-start.3 = (f32[12,640]{1,0:T(8,128)S(1)}, f32[12,640]{1,0:T(8,128)S(1)}, u32[]{:S(2)}, u32[]{:S(2)}) collective-permute-start(f32[12,640]{1,0:T(8,128)S(1)} %get-tuple-element.29), channel_id=1, source_target_pairs={{0,16},{1,2},{2,1},{3,4},{4,3},{5,6},{6,5},{7,8},{8,7},{9,10},{10,... | collective-permute-start | bytes 92168 | tf_op jit(solution)/shard_map/ppermute | solution.py:519
  43.9 24.1 %copy-start = (f32[1024,128]{1,0:T(8,128)S(1)}, f32[1024,128]{1,0:T(8,128)}, u32[]{:S(2)}) copy-start(f32[1024,128]{1,0:T(8,128)} %sg_ref.1) | copy-start | bytes 1572868
  43.9 24.1 %copy-start.1 = (f32[1024,128]{1,0:T(8,128)S(1)}, f32[1024,128]{1,0:T(8,128)}, u32[]{:S(2)}) copy-start(f32[1024,128]{1,0:T(8,128)} %tc_ref.1) | copy-start | bytes 1572868

commit v6 on v5

--- a/solution.py
+++ b/solution.py
@@ -172,47 +172,41 @@
     return jnp.concatenate([flat[first + r : first + r + 1] for r in range(slots)], axis=1)
 
 
-def side_columns(low, high):
-    lane = iota(low.shape, 1)
-    low, high = (pltpu.roll(x + pltpu.roll(x, 124, 1), 126, 1) for x in (low, high))
-    return jnp.where(lane >= 126, low, jnp.where(lane < 2, high, 0.0))
-
-
-def rims_kernel(owners, slots, got_ref, ext_ref, pair_ref, rims_ref, flat_ref, ids_ref, first_ref, second_ref):
+def side_columns(flat, slots, row, last):
+    rows = row.shape[0]
+    left, right = (places(flat, k * slots, slots) for k in (5, 6))
+    sums = []
+    for k, ids in enumerate((left - last, left - last, right, right)):
+        value = jnp.concatenate([flat[4 * r + k : 4 * r + k + 1] for r in range(slots)], axis=1)
+        hit = jnp.broadcast_to(ids, row.shape) == row
+        sums.append(jnp.sum(jnp.where(hit, jnp.broadcast_to(value, row.shape), 0.0), axis=1, keepdims=True))
+    lane = iota((rows, 128), 1)
+    out = jnp.zeros((rows, 128), F32)
+    for at, x in zip((126, 127, 0, 1), sums):
+        out = jnp.where(lane == at, jnp.broadcast_to(x, (rows, 128)), out)
+    return out
+
+
+def rims_kernel(owners, slots, got_ref, ext_ref, pair_ref, flat_ref, ids_ref, first_ref, second_ref):
     rows = ext_ref.shape[1]
     groups = ext_ref.shape[2] // 128 - 1
     info = got_ref[pl.ds(slots, owners, stride=slots + 1), :]
     ids_ref[...] = info.astype(I32)
-    flat = info.T.astype(I32)
+    flat = info.T
     flat_ref[...] = flat
-    lane = iota((owners, 128), 1)
     for r in range(slots):
         span = slice(r * owners, (r + 1) * owners)
         high, low = halves(got_ref[pl.ds(r, owners, stride=slots + 1), :])
         pair_ref[span, :128] = high
         pair_ref[span, 128:] = low
-        values = pltpu.roll(info, (128 - 4 * r) % 128, 1)
-        high = values.astype(BF16).astype(F32)
-        low = pltpu.roll(values - high, 4, 1)
-        rims_ref[span, :] = jnp.where(lane < 4, high, low).astype(BF16)
-    own, left, right = (places(flat, 4 * slots + k * slots, slots) for k in range(3))
+    own = places(flat, 4 * slots, slots)
     shape = (8 * groups, owners * slots)
     line = iota(shape, 0)
     row = line & 7
     row = row + jnp.where(row < 4, 0, rows - 8)
-    mask = jnp.broadcast_to(own, shape) == (line >> 3) * rows + row
+    mask = jnp.broadcast_to(own, shape) == ((line >> 3) * rows + row).astype(F32)
     heat = joined(jnp.dot(select(mask), pair_ref[...], preferred_element_type=F32))
-    shape = (16, owners * slots)
-    line = iota(shape, 0)
-    row = line & 7
-    row = row + jnp.where(row < 4, 0, rows - 8)
-    mask = jnp.where(
-        line < 8,
-        jnp.broadcast_to(left, shape) - (groups - 1) * rows,
-        jnp.broadcast_to(right, shape),
-    ) == row
-    side = jnp.dot(select(mask), rims_ref[...], preferred_element_type=F32)
-    side = side_columns(side[:8], side[8:])
+    side = side_columns(flat, slots, row[:8].astype(F32), (groups - 1) * rows)
     edges = []
     for at, rim in ((0, slice(0, 4)), (4, slice(rows - 4, rows))):
         loss = [heat[8 * q + at : 8 * q + at + 4] for q in range(groups)] + [side[at : at + 4]]
@@ -229,8 +223,7 @@
         functools.partial(rims_kernel, owners, slots),
         out_shape=(
             jax.ShapeDtypeStruct((owners * slots, 256), BF16),
-            jax.ShapeDtypeStruct((owners * slots, 128), BF16),
-            jax.ShapeDtypeStruct((128, owners), I32),
+            jax.ShapeDtypeStruct((128, owners), F32),
             jax.ShapeDtypeStruct((owners, 128), I32),
             strip,
             strip,
@@ -313,24 +306,19 @@
     )(t, hc, c, first, second)
 
 
-def middle_kernel(sweeps, slots, pair_ref, rims_ref, flat_ref, ids_ref, ext_ref, out_ref, top_ref, bottom_ref, reply_ref, rhs_ref, temp_ref, tiles_ref, sems):
+def middle_kernel(sweeps, slots, pair_ref, flat_ref, ids_ref, ext_ref, out_ref, top_ref, bottom_ref, reply_ref, rhs_ref, temp_ref, tiles_ref, sems):
     rows, cols = out_ref.shape
     owners = ids_ref.shape[0]
     groups = cols // 128
     flat = flat_ref[...]
-    own, left, right = (places(flat, 4 * slots + k * slots, slots) for k in range(3))
+    own = places(flat, 4 * slots, slots)
     shape = (rows, own.shape[1])
-    row = iota(shape, 0)
+    row = iota(shape, 0).astype(F32)
     match = lambda x, first: select(jnp.broadcast_to(x - first, shape) == row)
     for q in range(groups + 1):
         span = slice(q * 128, (q + 1) * 128)
         if q == groups:
-            heat = side_columns(
-                *(
-                    jnp.dot(match(*x), rims_ref[...], preferred_element_type=F32)
-                    for x in ((left, (groups - 1) * rows), (right, 0))
-                )
-            )
+            heat = side_columns(flat, slots, row, (groups - 1) * rows)
         else:
             heat = joined(jnp.dot(match(own, q * rows), pair_ref[...], preferred_element_type=F32))
         rhs_ref[:, span] = source(ext_ref[0, :, span], ext_ref[1, :, span], ext_ref[2, :, span], heat)
@@ -367,7 +355,7 @@
     )
 
 
-def middle(pair, rim, flat, ids, ext, cols, sweeps, slots):
+def middle(pair, flat, ids, ext, cols, sweeps, slots):
     _, rows, wide = ext.shape
     strip = jax.ShapeDtypeStruct((3, 2 * RIM, wide), F32)
     onchip = pl.BlockSpec(memory_space=pltpu.VMEM)
@@ -388,7 +376,7 @@
         ],
         compiler_params=pltpu.CompilerParams(vmem_limit_bytes=16 << 20),
         name="middle",
-    )(pair, rim, flat, ids, ext)
+    )(pair, flat, ids, ext)
 
 
 def solve_kernel(sweeps, slots, count, first_ref, second_ref, top_ref, bottom_ref, ids_ref, part_ref, inner_ref, out_ref, reply_ref, temp_ref, tiles_ref, sems):
@@ -470,17 +458,17 @@
     pair_ref[:, 128:] = low
     slot = slot_ref[...].T
     writes = []
-    for b in range(0, blocks, 4):
+    for b in range(0, blocks, 2):
         column = jnp.concatenate(
-            [jnp.broadcast_to(slot[:, k : k + 1], (128, 128)) for k in range(b, b + 4)], axis=0
+            [jnp.broadcast_to(slot[:, k : k + 1], (128, 128)) for k in range(b, b + 2)], axis=0
         )
         mask = jnp.concatenate(
-            [column == iota((512, 128), 1) + 128 * k for k in range(total // 128)], axis=1
+            [column == iota((256, 128), 1) + 128 * k for k in range(total // 128)], axis=1
         )
         hot = joined(jnp.dot(select(mask), pair_ref[...], preferred_element_type=F32))
-        span = pl.ds(b * 128, 512)
+        span = pl.ds(b * 128, 256)
         new_ref[span, :] = sg_ref[span, :] / (1.0 + tc_ref[span, :] * hot)
-        write = pltpu.make_async_copy(new_ref.at[span], out_ref.at[span], sems.at[b // 4])
+        write = pltpu.make_async_copy(new_ref.at[span], out_ref.at[span], sems.at[b // 2])
         write.start()
         writes.append(write)
     for write in writes:
@@ -495,7 +483,7 @@
         scratch_shapes=[
             pltpu.VMEM((back.shape[0], 256), BF16),
             pltpu.VMEM(sg.shape, F32),
-            pltpu.SemaphoreType.DMA((slot.shape[0] // 4,)),
+            pltpu.SemaphoreType.DMA((slot.shape[0] // 2,)),
         ],
         compiler_params=pltpu.CompilerParams(vmem_limit_bytes=16 << 20),
         name="final",
@@ -542,9 +530,9 @@
     got = exchanged(send, owners)
     grid = pinned(*lax.optimization_barrier((t_old, heat_cap, conduct, slot))[:3])
     ext = prepare(*grid, *traded(*strips(*grid, SWEEPS), "em"), SWEEPS)
-    pair, rim, flat, ids, first, second = rims(got, ext, owners, slots)
+    pair, flat, ids, first, second = rims(got, ext, owners, slots)
     first, second = traded(first, second, "th")
-    inner, top, bottom, part = middle(pair, rim, flat, ids, ext, cols, SWEEPS, slots)
+    inner, top, bottom, part = middle(pair, flat, ids, ext, cols, SWEEPS, slots)
     (inner,) = pinned(inner)
     temp, reply = solve(first, second, top, bottom, ids, part, inner, SWEEPS, owners, slots)
     back = exchanged(reply, owners)

time: 70.6 us -> 69.7 us (0.987)
  Pallas kernels: 15.9 us -> 14.9 us
    pallas_call x1, Pallas kernels: 1.22 us -> 0.43 us  [rims(): pl.pallas_call(functools.partial(rims_kernel, owners, slots), out_shape=(...]
where the time goes in v6:
time: 69.7 us; the launch traced here: 69.5 us
  blocking collectives  24.1 us (35%)
  starting transfers between devices  15.6 us (22%)
  Pallas kernels  14.9 us (21%)
  waiting for transfers between devices  14.1 us (20%)
  between operations  0.72 us (1%)
    all_to_all x1, blocking collectives, exchanged(): x = lax.all_to_all(x, ('em', 'th'), split_axis=0, concat_axis=0, tiled=True)  24.1 us
    all_to_all x1, starting transfers between devices, exchanged(): x = lax.all_to_all(x, ('em', 'th'), split_axis=0, concat_axis=0, tiled=True)  11.5 us
    all_to_all x1, waiting for transfers between devices, exchanged(): x = lax.all_to_all(x, ('em', 'th'), split_axis=0, concat_axis=0, tiled=True)  7.45 us
    ppermute x2, waiting for transfers between devices, traded(): lax.ppermute(second, ('em', 'th'), far)  6.65 us
    pallas_call x1, Pallas kernels, route(): pl.pallas_call(functools.partial(route_kernel, owners, slots, rows, near)...  4.06 us
    pallas_call x1, Pallas kernels, middle(): pl.pallas_call(functools.partial(middle_kernel, sweeps, slots), out_shape...  3.85 us
    ppermute x2, starting transfers between devices, traded(): lax.ppermute(second, ('em', 'th'), far)  2.4 us
    pallas_call x1, Pallas kernels, final(): pl.pallas_call(final_kernel, out_shape=jax.ShapeDtypeStruct(sg.shape, F32...  2.23 us
  transfers between devices with their start and end apart: 5, of which 2 were waited for; matrix products, arithmetic and copies ran while one was open for 0% of the time, Pallas kernels for 10%

profile of v6, /device:TPU:1, one launch (start us, length us, event | category | flops | bytes accessed | tf_op | source)
XLA Modules:
  0.0 69.5 jit_solution(8795444372494892043)
XLA Ops:
  0.6 4.1 %route.1 = (f32[2176,128]{1,0:T(8,128)}, s32[8,128]{1,0:T(8,128)S(1)}) custom-call(s32[8,128]{1,0:T(8,128)} %bitcast.9, s32[8,128]{1,0:T(8,128)} %bitcast.10, f32[1024,128]{1,0:T(8,128)} %er_hbm.1, f32[1024,128]{1,0:T(8,128)} %ei_hbm.1, f32[1024,128]{1,0:T(8,128)} %sg_ref.1), custom_call_target="tpu_custom_call" | custom-call | tf_op jit(solution)/shard_map/route/pallas_call | solution.py:141
  4.7 11.5 %all-to-all-start = ((f32[128,1,2176]{2,1,0:T(1,128)}), f32[128,1,2176]{2,1,0:T(1,128)S(1)}, u32[]{:S(2)}, u32[]{:S(2)}) async-start(f32[128,1,2176]{2,1,0:T(1,128)} %bitcast.2), calls=%async_computation | async-start | bytes 2228224 | tf_op jit(solution)/shard_map/all_to_all | solution.py:513
  16.2 1.4 %strips.1 = (f32[24,256]{1,0:T(8,128)S(1)}, f32[24,256]{1,0:T(8,128)S(1)}) custom-call(f32[256,512]{1,0:T(8,128)} %t_ref, f32[256,512]{1,0:T(8,128)} %hc_ref, f32[256,512]{1,0:T(8,128)} %c_ref), custom_call_target="tpu_custom_call" | custom-call | tf_op jit(solution)/shard_map/strips/pallas_call | solution.py:266
  17.7 1.1 %collective-permute-start = (f32[24,256]{1,0:T(8,128)S(1)}, f32[24,256]{1,0:T(8,128)S(1)}, u32[]{:S(2)}, u32[]{:S(2)}) collective-permute-start(f32[24,256]{1,0:T(8,128)S(1)} %get-tuple-element.25), channel_id=1, source_target_pairs={{0,16},{1,17},{2,18},{3,19},{4,20},{5,21},{6,22},{7,23},{8,24},{9,... | collective-permute-start | bytes 73736 | tf_op jit(solution)/shard_map/ppermute | solution.py:507
  18.8 0.8 %collective-permute-start.1 = (f32[24,256]{1,0:T(8,128)S(1)}, f32[24,256]{1,0:T(8,128)S(1)}, u32[]{:S(2)}, u32[]{:S(2)}) collective-permute-start(f32[24,256]{1,0:T(8,128)S(1)} %get-tuple-element.26), channel_id=1, source_target_pairs={{0,112},{1,113},{2,114},{3,115},{4,116},{5,117},{6,118},{7,119},{8... | collective-permute-start | bytes 73736 | tf_op jit(solution)/shard_map/ppermute | solution.py:507
  19.6 0.0 collective-permute-done.first_ref
  19.6 6.7 %collective-permute-done.1.second_ref = f32[24,256]{1,0:T(8,128)S(1)} collective-permute-done((f32[24,256]{1,0:T(8,128)S(1)}, f32[24,256]{1,0:T(8,128)S(1)}, u32[]{:S(2)}, u32[]{:S(2)}) %collective-permute-start.1) | collective-permute-done | bytes 24608 | tf_op jit(solution)/shard_map/ppermute | solution.py:507
  26.3 1.9 %prepare.1.ext_ref = f32[3,256,640]{2,1,0:T(8,128)S(1)} custom-call(f32[256,512]{1,0:T(8,128)} %t_ref, f32[256,512]{1,0:T(8,128)} %hc_ref, f32[256,512]{1,0:T(8,128)} %c_ref, f32[24,256]{1,0:T(8,128)S(1)} %collective-permute-done.first_ref, f32[24,256]{1,0:T(8,128)S(1)} %collective-permute-done.1.second_ref), custom_call_target="tpu_custom_call" | custom-call | tf_op jit(solution)/shard_map/prepare/pallas_call | solution.py:301
  28.2 7.4 %all-to-all-done = f32[128,1,2176]{2,1,0:T(1,128)S(1)} async-done(((f32[128,1,2176]{2,1,0:T(1,128)}), f32[128,1,2176]{2,1,0:T(1,128)S(1)}, u32[]{:S(2)}, u32[]{:S(2)}) %all-to-all-start) | async-done | bytes 1114144 | tf_op jit(solution)/shard_map/all_to_all | solution.py:513
  35.6 0.4 rims.1
  36.1 0.5 collective-permute-start.2
  36.6 1.6 %collective-permute-start.3 = (f32[12,640]{1,0:T(8,128)S(1)}, f32[12,640]{1,0:T(8,128)S(1)}, u32[]{:S(2)}, u32[]{:S(2)}) collective-permute-start(f32[12,640]{1,0:T(8,128)S(1)} %get-tuple-element.28), channel_id=1, source_target_pairs={{0,16},{1,2},{2,1},{3,4},{4,3},{5,6},{6,5},{7,8},{8,7},{9,10},{10,... | collective-permute-start | bytes 92168 | tf_op jit(solution)/shard_map/ppermute | solution.py:507
  38.2 3.8 %middle.1 = (f32[256,512]{1,0:T(8,128)}, f32[3,16,640]{2,1,0:T(8,128)S(1)}, f32[3,16,640]{2,1,0:T(8,128)S(1)}, f32[2048,128]{1,0:T(8,128)S(1)}) custom-call(bf16[2048,256]{1,0:T(8,128)(2,1)S(1)} %get-tuple-element.29.pair_ref, f32[128,128]{1,0:T(8,128)S(1)} %get-tuple-element.30.flat_ref, s32[128,128]{1,0:T(8,128)S(1)} %get-tuple-element.31.ids_ref, ...), custom_call_target="tpu_custom_call" | custom-call | tf_op jit(solution)/shard_map/middle/pallas_call | solution.py:362
  42.1 0.0 collective-permute-done.2.first_ref
  42.1 0.0 collective-permute-done.3.second_ref
  42.1 1.0 %solve.1 = (f32[256,512]{1,0:T(8,128)}, f32[2048,128]{1,0:T(8,128)S(1)}) custom-call(f32[12,640]{1,0:T(8,128)S(1)} %collective-permute-done.2.first_ref, f32[12,640]{1,0:T(8,128)S(1)} %collective-permute-done.3.second_ref, f32[3,16,640]{2,1,0:T(8,128)S(1)} %get-tuple-element.32.top_ref, ...), custom_call_target="tpu_custom_call", output_to_operand_aliasing={{0}: (6, {})} | custom-call | tf_op jit(solution)/shard_map/solve/pallas_call | solution.py:434
  43.1 0.0 copy-start
  43.1 0.0 copy-start.1
  43.1 24.1 %all_to_all.10 = f32[128,1,2048]{2,1,0:T(1,128)S(1)} all-to-all(f32[128,1,2048]{2,1,0:T(1,128)S(1)} %bitcast.8), channel_id=1, replica_groups=mesh['em'=8,'th'=16] {'em','th'}, dimensions={0} | all-to-all | bytes 2097152 | tf_op jit(solution)/shard_map/all_to_all | solution.py:513
  67.2 0.0 copy-done
  67.2 0.0 copy-done.1
  67.3 2.2 %final.1 = f32[1024,128]{1,0:T(8,128)} custom-call(s32[8,128]{1,0:T(8,128)S(1)} %get-tuple-element.21.slot_ref, f32[2048,128]{1,0:T(8,128)S(1)} %bitcast.7, f32[1024,128]{1,0:T(8,128)S(1)} %copy-done, f32[1024,128]{1,0:T(8,128)S(1)} %copy-done.1), custom_call_target="tpu_custom_call" | custom-call | tf_op jit(solution)/shard_map/final/pallas_call | solution.py:479
Async XLA Ops:
  4.7 30.9 %all-to-all-start = ((f32[128,1,2176]{2,1,0:T(1,128)}), f32[128,1,2176]{2,1,0:T(1,128)S(1)}, u32[]{:S(2)}, u32[]{:S(2)}) async-start(f32[128,1,2176]{2,1,0:T(1,128)} %bitcast.2), calls=%async_computation | async-start | bytes 2228224 | tf_op jit(solution)/shard_map/all_to_all | solution.py:513
  17.7 2.0 %collective-permute-start = (f32[24,256]{1,0:T(8,128)S(1)}, f32[24,256]{1,0:T(8,128)S(1)}, u32[]{:S(2)}, u32[]{:S(2)}) collective-permute-start(f32[24,256]{1,0:T(8,128)S(1)} %get-tuple-element.25), channel_id=1, source_target_pairs={{0,16},{1,17},{2,18},{3,19},{4,20},{5,21},{6,22},{7,23},{8,24},{9,... | collective-permute-start | bytes 73736 | tf_op jit(solution)/shard_map/ppermute | solution.py:507
  18.8 7.5 %collective-permute-start.1 = (f32[24,256]{1,0:T(8,128)S(1)}, f32[24,256]{1,0:T(8,128)S(1)}, u32[]{:S(2)}, u32[]{:S(2)}) collective-permute-start(f32[24,256]{1,0:T(8,128)S(1)} %get-tuple-element.26), channel_id=1, source_target_pairs={{0,112},{1,113},{2,114},{3,115},{4,116},{5,117},{6,118},{7,119},{8... | collective-permute-start | bytes 73736 | tf_op jit(solution)/shard_map/ppermute | solution.py:507
  36.1 6.0 %collective-permute-start.2 = (f32[12,640]{1,0:T(8,128)S(1)}, f32[12,640]{1,0:T(8,128)S(1)}, u32[]{:S(2)}, u32[]{:S(2)}) collective-permute-start(f32[12,640]{1,0:T(8,128)S(1)} %get-tuple-element.27), channel_id=1, source_target_pairs={{0,1},{1,0},{2,3},{3,2},{4,5},{5,4},{6,7},{7,6},{8,9},{9,8},{10,11... | collective-permute-start | bytes 92168 | tf_op jit(solution)/shard_map/ppermute | solution.py:507
  36.6 5.4 %collective-permute-start.3 = (f32[12,640]{1,0:T(8,128)S(1)}, f32[12,640]{1,0:T(8,128)S(1)}, u32[]{:S(2)}, u32[]{:S(2)}) collective-permute-start(f32[12,640]{1,0:T(8,128)S(1)} %get-tuple-element.28), channel_id=1, source_target_pairs={{0,16},{1,2},{2,1},{3,4},{4,3},{5,6},{6,5},{7,8},{8,7},{9,10},{10,... | collective-permute-start | bytes 92168 | tf_op jit(solution)/shard_map/ppermute | solution.py:507
  43.1 24.2 %copy-start = (f32[1024,128]{1,0:T(8,128)S(1)}, f32[1024,128]{1,0:T(8,128)}, u32[]{:S(2)}) copy-start(f32[1024,128]{1,0:T(8,128)} %sg_ref.1) | copy-start | bytes 1572868
  43.1 24.1 %copy-start.1 = (f32[1024,128]{1,0:T(8,128)S(1)}, f32[1024,128]{1,0:T(8,128)}, u32[]{:S(2)}) copy-start(f32[1024,128]{1,0:T(8,128)} %tc_ref.1) | copy-start | bytes 1572868

commit v7 on v6

--- a/solution.py
+++ b/solution.py
@@ -187,6 +187,30 @@
     return out
 
 
+def all_side_columns(flat, slots, rows, last):
+    wide = slots * flat.shape[1]
+    left, right = (places(flat, k * slots, slots).astype(I32) for k in (5, 6))
+    left = left - last
+    value = jnp.concatenate([flat[4 * r : 4 * r + 4] for r in range(slots)], axis=1)
+    high = value.astype(BF16).astype(F32)
+    value = jnp.concatenate([high, value - high], axis=0)
+    pick = lambda x: jnp.broadcast_to(x, (8, wide))
+    group = jnp.where(iota((8, wide), 0) & 3 < 2, pick(left >> 4), pick(right >> 4))
+    spread = [jnp.where(group == k, value, 0.0) for k in range(rows // 16)]
+    spread = jnp.concatenate(spread, axis=0).astype(BF16)
+    pick = lambda x: jnp.broadcast_to(x & 15, (16, wide)) == iota((16, wide), 0)
+    within = jnp.concatenate([select(pick(left)), select(pick(right))], axis=0)
+    sums = lax.dot_general(
+        within, spread, (((1,), (1,)), ((), ())), preferred_element_type=F32
+    )
+    sums = sums + pltpu.roll(sums, 124, 1)
+    lane = iota((16, 128), 1)
+    sums = jnp.where(lane & 3 < 2, sums[:16], sums[16:])
+    ends = (lane >= 126) | (lane < 2)
+    parts = [jnp.where(ends, pltpu.roll(sums, 126 - 8 * k, 1), 0.0) for k in range(rows // 16)]
+    return jnp.concatenate(parts, axis=0)
+
+
 def rims_kernel(owners, slots, got_ref, ext_ref, pair_ref, flat_ref, ids_ref, first_ref, second_ref):
     rows = ext_ref.shape[1]
     groups = ext_ref.shape[2] // 128 - 1
@@ -318,7 +342,7 @@
     for q in range(groups + 1):
         span = slice(q * 128, (q + 1) * 128)
         if q == groups:
-            heat = side_columns(flat, slots, row, (groups - 1) * rows)
+            heat = all_side_columns(flat, slots, rows, (groups - 1) * rows)
         else:
             heat = joined(jnp.dot(match(own, q * rows), pair_ref[...], preferred_element_type=F32))
         rhs_ref[:, span] = source(ext_ref[0, :, span], ext_ref[1, :, span], ext_ref[2, :, span], heat)

time: 69.7 us -> 69.7 us (level)
  no operation moved by 1% of the time
where the time goes in v7:
time: 69.7 us; the launch traced here: 69.5 us
  blocking collectives  24.4 us (35%)
  starting transfers between devices  15.6 us (22%)
  Pallas kernels  14.7 us (21%)
  waiting for transfers between devices  14.1 us (20%)
  between operations  0.72 us (1%)
    all_to_all x1, blocking collectives, exchanged(): x = lax.all_to_all(x, ('em', 'th'), split_axis=0, concat_axis=0, tiled=True)  24.4 us
    all_to_all x1, starting transfers between devices, exchanged(): x = lax.all_to_all(x, ('em', 'th'), split_axis=0, concat_axis=0, tiled=True)  11.5 us
    all_to_all x1, waiting for transfers between devices, exchanged(): x = lax.all_to_all(x, ('em', 'th'), split_axis=0, concat_axis=0, tiled=True)  7.45 us
    ppermute x2, waiting for transfers between devices, traded(): lax.ppermute(second, ('em', 'th'), far)  6.65 us
    pallas_call x1, Pallas kernels, route(): pl.pallas_call(functools.partial(route_kernel, owners, slots, rows, near)...  4.06 us
    pallas_call x1, Pallas kernels, middle(): pl.pallas_call(functools.partial(middle_kernel, sweeps, slots), out_shape...  3.61 us
    ppermute x2, starting transfers between devices, traded(): lax.ppermute(second, ('em', 'th'), far)  2.4 us
    pallas_call x1, Pallas kernels, final(): pl.pallas_call(final_kernel, out_shape=jax.ShapeDtypeStruct(sg.shape, F32...  2.23 us
  transfers between devices with their start and end apart: 5, of which 2 were waited for; matrix products, arithmetic and copies ran while one was open for 0% of the time, Pallas kernels for 10%

profile of v7, /device:TPU:1, one launch (start us, length us, event | category | flops | bytes accessed | tf_op | source)
XLA Modules:
  0.0 69.5 jit_solution(4119527182171618333)
XLA Ops:
  0.6 4.1 %route.1 = (f32[2176,128]{1,0:T(8,128)}, s32[8,128]{1,0:T(8,128)S(1)}) custom-call(s32[8,128]{1,0:T(8,128)} %bitcast.9, s32[8,128]{1,0:T(8,128)} %bitcast.10, f32[1024,128]{1,0:T(8,128)} %er_hbm.1, f32[1024,128]{1,0:T(8,128)} %ei_hbm.1, f32[1024,128]{1,0:T(8,128)} %sg_ref.1), custom_call_target="tpu_custom_call" | custom-call | tf_op jit(solution)/shard_map/route/pallas_call | solution.py:141
  4.7 11.5 %all-to-all-start = ((f32[128,1,2176]{2,1,0:T(1,128)}), f32[128,1,2176]{2,1,0:T(1,128)S(1)}, u32[]{:S(2)}, u32[]{:S(2)}) async-start(f32[128,1,2176]{2,1,0:T(1,128)} %bitcast.2), calls=%async_computation | async-start | bytes 2228224 | tf_op jit(solution)/shard_map/all_to_all | solution.py:537
  16.2 1.4 %strips.1 = (f32[24,256]{1,0:T(8,128)S(1)}, f32[24,256]{1,0:T(8,128)S(1)}) custom-call(f32[256,512]{1,0:T(8,128)} %t_ref, f32[256,512]{1,0:T(8,128)} %hc_ref, f32[256,512]{1,0:T(8,128)} %c_ref), custom_call_target="tpu_custom_call" | custom-call | tf_op jit(solution)/shard_map/strips/pallas_call | solution.py:290
  17.7 1.1 %collective-permute-start = (f32[24,256]{1,0:T(8,128)S(1)}, f32[24,256]{1,0:T(8,128)S(1)}, u32[]{:S(2)}, u32[]{:S(2)}) collective-permute-start(f32[24,256]{1,0:T(8,128)S(1)} %get-tuple-element.25), channel_id=1, source_target_pairs={{0,16},{1,17},{2,18},{3,19},{4,20},{5,21},{6,22},{7,23},{8,24},{9,... | collective-permute-start | bytes 73736 | tf_op jit(solution)/shard_map/ppermute | solution.py:531
  18.8 0.8 %collective-permute-start.1 = (f32[24,256]{1,0:T(8,128)S(1)}, f32[24,256]{1,0:T(8,128)S(1)}, u32[]{:S(2)}, u32[]{:S(2)}) collective-permute-start(f32[24,256]{1,0:T(8,128)S(1)} %get-tuple-element.26), channel_id=1, source_target_pairs={{0,112},{1,113},{2,114},{3,115},{4,116},{5,117},{6,118},{7,119},{8... | collective-permute-start | bytes 73736 | tf_op jit(solution)/shard_map/ppermute | solution.py:531
  19.6 0.0 collective-permute-done.first_ref
  19.6 6.7 %collective-permute-done.1.second_ref = f32[24,256]{1,0:T(8,128)S(1)} collective-permute-done((f32[24,256]{1,0:T(8,128)S(1)}, f32[24,256]{1,0:T(8,128)S(1)}, u32[]{:S(2)}, u32[]{:S(2)}) %collective-permute-start.1) | collective-permute-done | bytes 24608 | tf_op jit(solution)/shard_map/ppermute | solution.py:531
  26.3 1.9 %prepare.1.ext_ref = f32[3,256,640]{2,1,0:T(8,128)S(1)} custom-call(f32[256,512]{1,0:T(8,128)} %t_ref, f32[256,512]{1,0:T(8,128)} %hc_ref, f32[256,512]{1,0:T(8,128)} %c_ref, f32[24,256]{1,0:T(8,128)S(1)} %collective-permute-done.first_ref, f32[24,256]{1,0:T(8,128)S(1)} %collective-permute-done.1.second_ref), custom_call_target="tpu_custom_call" | custom-call | tf_op jit(solution)/shard_map/prepare/pallas_call | solution.py:325
  28.2 7.4 %all-to-all-done = f32[128,1,2176]{2,1,0:T(1,128)S(1)} async-done(((f32[128,1,2176]{2,1,0:T(1,128)}), f32[128,1,2176]{2,1,0:T(1,128)S(1)}, u32[]{:S(2)}, u32[]{:S(2)}) %all-to-all-start) | async-done | bytes 1114144 | tf_op jit(solution)/shard_map/all_to_all | solution.py:537
  35.6 0.4 rims.1
  36.1 0.5 collective-permute-start.2
  36.6 1.6 %collective-permute-start.3 = (f32[12,640]{1,0:T(8,128)S(1)}, f32[12,640]{1,0:T(8,128)S(1)}, u32[]{:S(2)}, u32[]{:S(2)}) collective-permute-start(f32[12,640]{1,0:T(8,128)S(1)} %get-tuple-element.28), channel_id=1, source_target_pairs={{0,16},{1,2},{2,1},{3,4},{4,3},{5,6},{6,5},{7,8},{8,7},{9,10},{10,... | collective-permute-start | bytes 92168 | tf_op jit(solution)/shard_map/ppermute | solution.py:531
  38.2 3.6 %middle.1 = (f32[256,512]{1,0:T(8,128)}, f32[3,16,640]{2,1,0:T(8,128)S(1)}, f32[3,16,640]{2,1,0:T(8,128)S(1)}, f32[2048,128]{1,0:T(8,128)S(1)}) custom-call(bf16[2048,256]{1,0:T(8,128)(2,1)S(1)} %get-tuple-element.29.pair_ref, f32[128,128]{1,0:T(8,128)S(1)} %get-tuple-element.30.flat_ref, s32[128,128]{1,0:T(8,128)S(1)} %get-tuple-element.31.ids_ref, ...), custom_call_target="tpu_custom_call" | custom-call | tf_op jit(solution)/shard_map/middle/pallas_call | solution.py:386
  41.8 0.0 collective-permute-done.2.first_ref
  41.8 0.0 collective-permute-done.3.second_ref
  41.8 1.0 %solve.1 = (f32[256,512]{1,0:T(8,128)}, f32[2048,128]{1,0:T(8,128)S(1)}) custom-call(f32[12,640]{1,0:T(8,128)S(1)} %collective-permute-done.2.first_ref, f32[12,640]{1,0:T(8,128)S(1)} %collective-permute-done.3.second_ref, f32[3,16,640]{2,1,0:T(8,128)S(1)} %get-tuple-element.32.top_ref, ...), custom_call_target="tpu_custom_call", output_to_operand_aliasing={{0}: (6, {})} | custom-call | tf_op jit(solution)/shard_map/solve/pallas_call | solution.py:458
  42.9 0.0 copy-start
  42.9 0.0 copy-start.1
  42.9 24.4 %all_to_all.10 = f32[128,1,2048]{2,1,0:T(1,128)S(1)} all-to-all(f32[128,1,2048]{2,1,0:T(1,128)S(1)} %bitcast.8), channel_id=1, replica_groups=mesh['em'=8,'th'=16] {'em','th'}, dimensions={0} | all-to-all | bytes 2097152 | tf_op jit(solution)/shard_map/all_to_all | solution.py:537
  67.2 0.0 copy-done
  67.2 0.0 copy-done.1
  67.3 2.2 %final.1 = f32[1024,128]{1,0:T(8,128)} custom-call(s32[8,128]{1,0:T(8,128)S(1)} %get-tuple-element.21.slot_ref, f32[2048,128]{1,0:T(8,128)S(1)} %bitcast.7, f32[1024,128]{1,0:T(8,128)S(1)} %copy-done, f32[1024,128]{1,0:T(8,128)S(1)} %copy-done.1), custom_call_target="tpu_custom_call" | custom-call | tf_op jit(solution)/shard_map/final/pallas_call | solution.py:503
Async XLA Ops:
  4.7 30.9 %all-to-all-start = ((f32[128,1,2176]{2,1,0:T(1,128)}), f32[128,1,2176]{2,1,0:T(1,128)S(1)}, u32[]{:S(2)}, u32[]{:S(2)}) async-start(f32[128,1,2176]{2,1,0:T(1,128)} %bitcast.2), calls=%async_computation | async-start | bytes 2228224 | tf_op jit(solution)/shard_map/all_to_all | solution.py:537
  17.7 2.0 %collective-permute-start = (f32[24,256]{1,0:T(8,128)S(1)}, f32[24,256]{1,0:T(8,128)S(1)}, u32[]{:S(2)}, u32[]{:S(2)}) collective-permute-start(f32[24,256]{1,0:T(8,128)S(1)} %get-tuple-element.25), channel_id=1, source_target_pairs={{0,16},{1,17},{2,18},{3,19},{4,20},{5,21},{6,22},{7,23},{8,24},{9,... | collective-permute-start | bytes 73736 | tf_op jit(solution)/shard_map/ppermute | solution.py:531
  18.8 7.5 %collective-permute-start.1 = (f32[24,256]{1,0:T(8,128)S(1)}, f32[24,256]{1,0:T(8,128)S(1)}, u32[]{:S(2)}, u32[]{:S(2)}) collective-permute-start(f32[24,256]{1,0:T(8,128)S(1)} %get-tuple-element.26), channel_id=1, source_target_pairs={{0,112},{1,113},{2,114},{3,115},{4,116},{5,117},{6,118},{7,119},{8... | collective-permute-start | bytes 73736 | tf_op jit(solution)/shard_map/ppermute | solution.py:531
  36.1 5.7 %collective-permute-start.2 = (f32[12,640]{1,0:T(8,128)S(1)}, f32[12,640]{1,0:T(8,128)S(1)}, u32[]{:S(2)}, u32[]{:S(2)}) collective-permute-start(f32[12,640]{1,0:T(8,128)S(1)} %get-tuple-element.27), channel_id=1, source_target_pairs={{0,1},{1,0},{2,3},{3,2},{4,5},{5,4},{6,7},{7,6},{8,9},{9,8},{10,11... | collective-permute-start | bytes 92168 | tf_op jit(solution)/shard_map/ppermute | solution.py:531
  36.6 5.2 %collective-permute-start.3 = (f32[12,640]{1,0:T(8,128)S(1)}, f32[12,640]{1,0:T(8,128)S(1)}, u32[]{:S(2)}, u32[]{:S(2)}) collective-permute-start(f32[12,640]{1,0:T(8,128)S(1)} %get-tuple-element.28), channel_id=1, source_target_pairs={{0,16},{1,2},{2,1},{3,4},{4,3},{5,6},{6,5},{7,8},{8,7},{9,10},{10,... | collective-permute-start | bytes 92168 | tf_op jit(solution)/shard_map/ppermute | solution.py:531
  42.9 24.4 %copy-start = (f32[1024,128]{1,0:T(8,128)S(1)}, f32[1024,128]{1,0:T(8,128)}, u32[]{:S(2)}) copy-start(f32[1024,128]{1,0:T(8,128)} %sg_ref.1) | copy-start | bytes 1572868
  42.9 24.4 %copy-start.1 = (f32[1024,128]{1,0:T(8,128)S(1)}, f32[1024,128]{1,0:T(8,128)}, u32[]{:S(2)}) copy-start(f32[1024,128]{1,0:T(8,128)} %tc_ref.1) | copy-start | bytes 1572868

commit v8 on v7

--- a/solution.py
+++ b/solution.py
@@ -339,7 +339,7 @@
     shape = (rows, own.shape[1])
     row = iota(shape, 0).astype(F32)
     match = lambda x, first: select(jnp.broadcast_to(x - first, shape) == row)
-    for q in range(groups + 1):
+    for q in (groups, *range(groups)):
         span = slice(q * 128, (q + 1) * 128)
         if q == groups:
             heat = all_side_columns(flat, slots, rows, (groups - 1) * rows)

time: 69.7 us -> 69.7 us (level)
  no operation moved by 1% of the time
where the time goes in v8:
time: 69.7 us; the launch traced here: 69.5 us
  blocking collectives  24.6 us (35%)
  starting transfers between devices  15.6 us (22%)
  Pallas kernels  14.4 us (21%)
  waiting for transfers between devices  14.1 us (20%)
  between operations  0.72 us (1%)
    all_to_all x1, blocking collectives, exchanged(): x = lax.all_to_all(x, ('em', 'th'), split_axis=0, concat_axis=0, tiled=True)  24.6 us
    all_to_all x1, starting transfers between devices, exchanged(): x = lax.all_to_all(x, ('em', 'th'), split_axis=0, concat_axis=0, tiled=True)  11.5 us
    all_to_all x1, waiting for transfers between devices, exchanged(): x = lax.all_to_all(x, ('em', 'th'), split_axis=0, concat_axis=0, tiled=True)  7.45 us
    ppermute x2, waiting for transfers between devices, traded(): lax.ppermute(second, ('em', 'th'), far)  6.65 us
    pallas_call x1, Pallas kernels, route(): pl.pallas_call(functools.partial(route_kernel, owners, slots, rows, near)...  4.06 us
    pallas_call x1, Pallas kernels, middle(): pl.pallas_call(functools.partial(middle_kernel, sweeps, slots), out_shape...  3.34 us
    ppermute x2, starting transfers between devices, traded(): lax.ppermute(second, ('em', 'th'), far)  2.4 us
    pallas_call x1, Pallas kernels, final(): pl.pallas_call(final_kernel, out_shape=jax.ShapeDtypeStruct(sg.shape, F32...  2.23 us
  transfers between devices with their start and end apart: 5, of which 2 were waited for; matrix products, arithmetic and copies ran while one was open for 0% of the time, Pallas kernels for 10%

profile of v8, /device:TPU:1, one launch (start us, length us, event | category | flops | bytes accessed | tf_op | source)
XLA Modules:
  0.0 69.5 jit_solution(8605038327680145746)
XLA Ops:
  0.6 4.1 %route.1 = (f32[2176,128]{1,0:T(8,128)}, s32[8,128]{1,0:T(8,128)S(1)}) custom-call(s32[8,128]{1,0:T(8,128)} %bitcast.9, s32[8,128]{1,0:T(8,128)} %bitcast.10, f32[1024,128]{1,0:T(8,128)} %er_hbm.1, f32[1024,128]{1,0:T(8,128)} %ei_hbm.1, f32[1024,128]{1,0:T(8,128)} %sg_ref.1), custom_call_target="tpu_custom_call" | custom-call | tf_op jit(solution)/shard_map/route/pallas_call | solution.py:141
  4.7 11.5 %all-to-all-start = ((f32[128,1,2176]{2,1,0:T(1,128)}), f32[128,1,2176]{2,1,0:T(1,128)S(1)}, u32[]{:S(2)}, u32[]{:S(2)}) async-start(f32[128,1,2176]{2,1,0:T(1,128)} %bitcast.2), calls=%async_computation | async-start | bytes 2228224 | tf_op jit(solution)/shard_map/all_to_all | solution.py:537
  16.2 1.4 %strips.1 = (f32[24,256]{1,0:T(8,128)S(1)}, f32[24,256]{1,0:T(8,128)S(1)}) custom-call(f32[256,512]{1,0:T(8,128)} %t_ref, f32[256,512]{1,0:T(8,128)} %hc_ref, f32[256,512]{1,0:T(8,128)} %c_ref), custom_call_target="tpu_custom_call" | custom-call | tf_op jit(solution)/shard_map/strips/pallas_call | solution.py:290
  17.7 1.1 %collective-permute-start = (f32[24,256]{1,0:T(8,128)S(1)}, f32[24,256]{1,0:T(8,128)S(1)}, u32[]{:S(2)}, u32[]{:S(2)}) collective-permute-start(f32[24,256]{1,0:T(8,128)S(1)} %get-tuple-element.25), channel_id=1, source_target_pairs={{0,16},{1,17},{2,18},{3,19},{4,20},{5,21},{6,22},{7,23},{8,24},{9,... | collective-permute-start | bytes 73736 | tf_op jit(solution)/shard_map/ppermute | solution.py:531
  18.8 0.8 %collective-permute-start.1 = (f32[24,256]{1,0:T(8,128)S(1)}, f32[24,256]{1,0:T(8,128)S(1)}, u32[]{:S(2)}, u32[]{:S(2)}) collective-permute-start(f32[24,256]{1,0:T(8,128)S(1)} %get-tuple-element.26), channel_id=1, source_target_pairs={{0,112},{1,113},{2,114},{3,115},{4,116},{5,117},{6,118},{7,119},{8... | collective-permute-start | bytes 73736 | tf_op jit(solution)/shard_map/ppermute | solution.py:531
  19.6 0.0 collective-permute-done.first_ref
  19.6 6.7 %collective-permute-done.1.second_ref = f32[24,256]{1,0:T(8,128)S(1)} collective-permute-done((f32[24,256]{1,0:T(8,128)S(1)}, f32[24,256]{1,0:T(8,128)S(1)}, u32[]{:S(2)}, u32[]{:S(2)}) %collective-permute-start.1) | collective-permute-done | bytes 24608 | tf_op jit(solution)/shard_map/ppermute | solution.py:531
  26.3 1.9 %prepare.1.ext_ref = f32[3,256,640]{2,1,0:T(8,128)S(1)} custom-call(f32[256,512]{1,0:T(8,128)} %t_ref, f32[256,512]{1,0:T(8,128)} %hc_ref, f32[256,512]{1,0:T(8,128)} %c_ref, f32[24,256]{1,0:T(8,128)S(1)} %collective-permute-done.first_ref, f32[24,256]{1,0:T(8,128)S(1)} %collective-permute-done.1.second_ref), custom_call_target="tpu_custom_call" | custom-call | tf_op jit(solution)/shard_map/prepare/pallas_call | solution.py:325
  28.2 7.4 %all-to-all-done = f32[128,1,2176]{2,1,0:T(1,128)S(1)} async-done(((f32[128,1,2176]{2,1,0:T(1,128)}), f32[128,1,2176]{2,1,0:T(1,128)S(1)}, u32[]{:S(2)}, u32[]{:S(2)}) %all-to-all-start) | async-done | bytes 1114144 | tf_op jit(solution)/shard_map/all_to_all | solution.py:537
  35.6 0.4 rims.1
  36.1 0.5 collective-permute-start.2
  36.6 1.6 %collective-permute-start.3 = (f32[12,640]{1,0:T(8,128)S(1)}, f32[12,640]{1,0:T(8,128)S(1)}, u32[]{:S(2)}, u32[]{:S(2)}) collective-permute-start(f32[12,640]{1,0:T(8,128)S(1)} %get-tuple-element.28), channel_id=1, source_target_pairs={{0,16},{1,2},{2,1},{3,4},{4,3},{5,6},{6,5},{7,8},{8,7},{9,10},{10,... | collective-permute-start | bytes 92168 | tf_op jit(solution)/shard_map/ppermute | solution.py:531
  38.2 3.3 %middle.1 = (f32[256,512]{1,0:T(8,128)}, f32[3,16,640]{2,1,0:T(8,128)S(1)}, f32[3,16,640]{2,1,0:T(8,128)S(1)}, f32[2048,128]{1,0:T(8,128)S(1)}) custom-call(bf16[2048,256]{1,0:T(8,128)(2,1)S(1)} %get-tuple-element.29.pair_ref, f32[128,128]{1,0:T(8,128)S(1)} %get-tuple-element.30.flat_ref, s32[128,128]{1,0:T(8,128)S(1)} %get-tuple-element.31.ids_ref, ...), custom_call_target="tpu_custom_call" | custom-call | tf_op jit(solution)/shard_map/middle/pallas_call | solution.py:386
  41.5 0.0 collective-permute-done.2.first_ref
  41.6 0.0 collective-permute-done.3.second_ref
  41.6 1.0 %solve.1 = (f32[256,512]{1,0:T(8,128)}, f32[2048,128]{1,0:T(8,128)S(1)}) custom-call(f32[12,640]{1,0:T(8,128)S(1)} %collective-permute-done.2.first_ref, f32[12,640]{1,0:T(8,128)S(1)} %collective-permute-done.3.second_ref, f32[3,16,640]{2,1,0:T(8,128)S(1)} %get-tuple-element.32.top_ref, ...), custom_call_target="tpu_custom_call", output_to_operand_aliasing={{0}: (6, {})} | custom-call | tf_op jit(solution)/shard_map/solve/pallas_call | solution.py:458
  42.6 0.0 copy-start
  42.6 0.0 copy-start.1
  42.6 24.6 %all_to_all.10 = f32[128,1,2048]{2,1,0:T(1,128)S(1)} all-to-all(f32[128,1,2048]{2,1,0:T(1,128)S(1)} %bitcast.8), channel_id=1, replica_groups=mesh['em'=8,'th'=16] {'em','th'}, dimensions={0} | all-to-all | bytes 2097152 | tf_op jit(solution)/shard_map/all_to_all | solution.py:537
  67.2 0.0 copy-done
  67.2 0.0 copy-done.1
  67.3 2.2 %final.1 = f32[1024,128]{1,0:T(8,128)} custom-call(s32[8,128]{1,0:T(8,128)S(1)} %get-tuple-element.21.slot_ref, f32[2048,128]{1,0:T(8,128)S(1)} %bitcast.7, f32[1024,128]{1,0:T(8,128)S(1)} %copy-done, f32[1024,128]{1,0:T(8,128)S(1)} %copy-done.1), custom_call_target="tpu_custom_call" | custom-call | tf_op jit(solution)/shard_map/final/pallas_call | solution.py:503
Async XLA Ops:
  4.7 30.9 %all-to-all-start = ((f32[128,1,2176]{2,1,0:T(1,128)}), f32[128,1,2176]{2,1,0:T(1,128)S(1)}, u32[]{:S(2)}, u32[]{:S(2)}) async-start(f32[128,1,2176]{2,1,0:T(1,128)} %bitcast.2), calls=%async_computation | async-start | bytes 2228224 | tf_op jit(solution)/shard_map/all_to_all | solution.py:537
  17.7 2.0 %collective-permute-start = (f32[24,256]{1,0:T(8,128)S(1)}, f32[24,256]{1,0:T(8,128)S(1)}, u32[]{:S(2)}, u32[]{:S(2)}) collective-permute-start(f32[24,256]{1,0:T(8,128)S(1)} %get-tuple-element.25), channel_id=1, source_target_pairs={{0,16},{1,17},{2,18},{3,19},{4,20},{5,21},{6,22},{7,23},{8,24},{9,... | collective-permute-start | bytes 73736 | tf_op jit(solution)/shard_map/ppermute | solution.py:531
  18.8 7.5 %collective-permute-start.1 = (f32[24,256]{1,0:T(8,128)S(1)}, f32[24,256]{1,0:T(8,128)S(1)}, u32[]{:S(2)}, u32[]{:S(2)}) collective-permute-start(f32[24,256]{1,0:T(8,128)S(1)} %get-tuple-element.26), channel_id=1, source_target_pairs={{0,112},{1,113},{2,114},{3,115},{4,116},{5,117},{6,118},{7,119},{8... | collective-permute-start | bytes 73736 | tf_op jit(solution)/shard_map/ppermute | solution.py:531
  36.1 5.5 %collective-permute-start.2 = (f32[12,640]{1,0:T(8,128)S(1)}, f32[12,640]{1,0:T(8,128)S(1)}, u32[]{:S(2)}, u32[]{:S(2)}) collective-permute-start(f32[12,640]{1,0:T(8,128)S(1)} %get-tuple-element.27), channel_id=1, source_target_pairs={{0,1},{1,0},{2,3},{3,2},{4,5},{5,4},{6,7},{7,6},{8,9},{9,8},{10,11... | collective-permute-start | bytes 92168 | tf_op jit(solution)/shard_map/ppermute | solution.py:531
  36.6 4.9 %collective-permute-start.3 = (f32[12,640]{1,0:T(8,128)S(1)}, f32[12,640]{1,0:T(8,128)S(1)}, u32[]{:S(2)}, u32[]{:S(2)}) collective-permute-start(f32[12,640]{1,0:T(8,128)S(1)} %get-tuple-element.28), channel_id=1, source_target_pairs={{0,16},{1,2},{2,1},{3,4},{4,3},{5,6},{6,5},{7,8},{8,7},{9,10},{10,... | collective-permute-start | bytes 92168 | tf_op jit(solution)/shard_map/ppermute | solution.py:531
  42.6 24.7 %copy-start = (f32[1024,128]{1,0:T(8,128)S(1)}, f32[1024,128]{1,0:T(8,128)}, u32[]{:S(2)}) copy-start(f32[1024,128]{1,0:T(8,128)} %sg_ref.1) | copy-start | bytes 1572868
  42.6 24.7 %copy-start.1 = (f32[1024,128]{1,0:T(8,128)S(1)}, f32[1024,128]{1,0:T(8,128)}, u32[]{:S(2)}) copy-start(f32[1024,128]{1,0:T(8,128)} %tc_ref.1) | copy-start | bytes 1572868

commit v9 on v8

--- a/solution.py
+++ b/solution.py
@@ -482,17 +482,15 @@
     pair_ref[:, 128:] = low
     slot = slot_ref[...].T
     writes = []
-    for b in range(0, blocks, 2):
-        column = jnp.concatenate(
-            [jnp.broadcast_to(slot[:, k : k + 1], (128, 128)) for k in range(b, b + 2)], axis=0
-        )
+    for b in range(blocks):
+        column = jnp.broadcast_to(slot[:, b : b + 1], (128, 128))
         mask = jnp.concatenate(
-            [column == iota((256, 128), 1) + 128 * k for k in range(total // 128)], axis=1
+            [column == iota((128, 128), 1) + 128 * k for k in range(total // 128)], axis=1
         )
         hot = joined(jnp.dot(select(mask), pair_ref[...], preferred_element_type=F32))
-        span = pl.ds(b * 128, 256)
+        span = pl.ds(b * 128, 128)
         new_ref[span, :] = sg_ref[span, :] / (1.0 + tc_ref[span, :] * hot)
-        write = pltpu.make_async_copy(new_ref.at[span], out_ref.at[span], sems.at[b // 2])
+        write = pltpu.make_async_copy(new_ref.at[span], out_ref.at[span], sems.at[b])
         write.start()
         writes.append(write)
     for write in writes:
@@ -507,7 +505,7 @@
         scratch_shapes=[
             pltpu.VMEM((back.shape[0], 256), BF16),
             pltpu.VMEM(sg.shape, F32),
-            pltpu.SemaphoreType.DMA((slot.shape[0] // 2,)),
+            pltpu.SemaphoreType.DMA((slot.shape[0],)),
         ],
         compiler_params=pltpu.CompilerParams(vmem_limit_bytes=16 << 20),
         name="final",

time: 69.7 us -> 69.7 us (level)
  no operation moved by 1% of the time
where the time goes in v9:
time: 69.7 us; the launch traced here: 69.4 us
  blocking collectives  24.6 us (35%)
  starting transfers between devices  15.6 us (22%)
  Pallas kernels  14.4 us (21%)
  waiting for transfers between devices  14.1 us (20%)
  between operations  0.72 us (1%)
    all_to_all x1, blocking collectives, exchanged(): x = lax.all_to_all(x, ('em', 'th'), split_axis=0, concat_axis=0, tiled=True)  24.6 us
    all_to_all x1, starting transfers between devices, exchanged(): x = lax.all_to_all(x, ('em', 'th'), split_axis=0, concat_axis=0, tiled=True)  11.5 us
    all_to_all x1, waiting for transfers between devices, exchanged(): x = lax.all_to_all(x, ('em', 'th'), split_axis=0, concat_axis=0, tiled=True)  7.45 us
    ppermute x2, waiting for transfers between devices, traded(): lax.ppermute(second, ('em', 'th'), far)  6.65 us
    pallas_call x1, Pallas kernels, route(): pl.pallas_call(functools.partial(route_kernel, owners, slots, rows, near)...  4.06 us
    pallas_call x1, Pallas kernels, middle(): pl.pallas_call(functools.partial(middle_kernel, sweeps, slots), out_shape...  3.34 us
    ppermute x2, starting transfers between devices, traded(): lax.ppermute(second, ('em', 'th'), far)  2.4 us
    pallas_call x1, Pallas kernels, final(): pl.pallas_call(final_kernel, out_shape=jax.ShapeDtypeStruct(sg.shape, F32...  2.19 us
  transfers between devices with their start and end apart: 5, of which 2 were waited for; matrix products, arithmetic and copies ran while one was open for 0% of the time, Pallas kernels for 10%

profile of v9, /device:TPU:1, one launch (start us, length us, event | category | flops | bytes accessed | tf_op | source)
XLA Modules:
  0.0 69.4 jit_solution(18438673509286018763)
XLA Ops:
  0.6 4.1 %route.1 = (f32[2176,128]{1,0:T(8,128)}, s32[8,128]{1,0:T(8,128)S(1)}) custom-call(s32[8,128]{1,0:T(8,128)} %bitcast.9, s32[8,128]{1,0:T(8,128)} %bitcast.10, f32[1024,128]{1,0:T(8,128)} %er_hbm.1, f32[1024,128]{1,0:T(8,128)} %ei_hbm.1, f32[1024,128]{1,0:T(8,128)} %sg_ref.1), custom_call_target="tpu_custom_call" | custom-call | tf_op jit(solution)/shard_map/route/pallas_call | solution.py:141
  4.7 11.5 %all-to-all-start = ((f32[128,1,2176]{2,1,0:T(1,128)}), f32[128,1,2176]{2,1,0:T(1,128)S(1)}, u32[]{:S(2)}, u32[]{:S(2)}) async-start(f32[128,1,2176]{2,1,0:T(1,128)} %bitcast.2), calls=%async_computation | async-start | bytes 2228224 | tf_op jit(solution)/shard_map/all_to_all | solution.py:535
  16.2 1.4 %strips.1 = (f32[24,256]{1,0:T(8,128)S(1)}, f32[24,256]{1,0:T(8,128)S(1)}) custom-call(f32[256,512]{1,0:T(8,128)} %t_ref, f32[256,512]{1,0:T(8,128)} %hc_ref, f32[256,512]{1,0:T(8,128)} %c_ref), custom_call_target="tpu_custom_call" | custom-call | tf_op jit(solution)/shard_map/strips/pallas_call | solution.py:290
  17.7 1.1 %collective-permute-start = (f32[24,256]{1,0:T(8,128)S(1)}, f32[24,256]{1,0:T(8,128)S(1)}, u32[]{:S(2)}, u32[]{:S(2)}) collective-permute-start(f32[24,256]{1,0:T(8,128)S(1)} %get-tuple-element.25), channel_id=1, source_target_pairs={{0,16},{1,17},{2,18},{3,19},{4,20},{5,21},{6,22},{7,23},{8,24},{9,... | collective-permute-start | bytes 73736 | tf_op jit(solution)/shard_map/ppermute | solution.py:529
  18.8 0.8 %collective-permute-start.1 = (f32[24,256]{1,0:T(8,128)S(1)}, f32[24,256]{1,0:T(8,128)S(1)}, u32[]{:S(2)}, u32[]{:S(2)}) collective-permute-start(f32[24,256]{1,0:T(8,128)S(1)} %get-tuple-element.26), channel_id=1, source_target_pairs={{0,112},{1,113},{2,114},{3,115},{4,116},{5,117},{6,118},{7,119},{8... | collective-permute-start | bytes 73736 | tf_op jit(solution)/shard_map/ppermute | solution.py:529
  19.6 0.0 collective-permute-done.first_ref
  19.6 6.7 %collective-permute-done.1.second_ref = f32[24,256]{1,0:T(8,128)S(1)} collective-permute-done((f32[24,256]{1,0:T(8,128)S(1)}, f32[24,256]{1,0:T(8,128)S(1)}, u32[]{:S(2)}, u32[]{:S(2)}) %collective-permute-start.1) | collective-permute-done | bytes 24608 | tf_op jit(solution)/shard_map/ppermute | solution.py:529
  26.3 1.9 %prepare.1.ext_ref = f32[3,256,640]{2,1,0:T(8,128)S(1)} custom-call(f32[256,512]{1,0:T(8,128)} %t_ref, f32[256,512]{1,0:T(8,128)} %hc_ref, f32[256,512]{1,0:T(8,128)} %c_ref, f32[24,256]{1,0:T(8,128)S(1)} %collective-permute-done.first_ref, f32[24,256]{1,0:T(8,128)S(1)} %collective-permute-done.1.second_ref), custom_call_target="tpu_custom_call" | custom-call | tf_op jit(solution)/shard_map/prepare/pallas_call | solution.py:325
  28.2 7.4 %all-to-all-done = f32[128,1,2176]{2,1,0:T(1,128)S(1)} async-done(((f32[128,1,2176]{2,1,0:T(1,128)}), f32[128,1,2176]{2,1,0:T(1,128)S(1)}, u32[]{:S(2)}, u32[]{:S(2)}) %all-to-all-start) | async-done | bytes 1114144 | tf_op jit(solution)/shard_map/all_to_all | solution.py:535
  35.6 0.4 rims.1
  36.1 0.5 collective-permute-start.2
  36.6 1.6 %collective-permute-start.3 = (f32[12,640]{1,0:T(8,128)S(1)}, f32[12,640]{1,0:T(8,128)S(1)}, u32[]{:S(2)}, u32[]{:S(2)}) collective-permute-start(f32[12,640]{1,0:T(8,128)S(1)} %get-tuple-element.28), channel_id=1, source_target_pairs={{0,16},{1,2},{2,1},{3,4},{4,3},{5,6},{6,5},{7,8},{8,7},{9,10},{10,... | collective-permute-start | bytes 92168 | tf_op jit(solution)/shard_map/ppermute | solution.py:529
  38.2 3.3 %middle.1 = (f32[256,512]{1,0:T(8,128)}, f32[3,16,640]{2,1,0:T(8,128)S(1)}, f32[3,16,640]{2,1,0:T(8,128)S(1)}, f32[2048,128]{1,0:T(8,128)S(1)}) custom-call(bf16[2048,256]{1,0:T(8,128)(2,1)S(1)} %get-tuple-element.29.pair_ref, f32[128,128]{1,0:T(8,128)S(1)} %get-tuple-element.30.flat_ref, s32[128,128]{1,0:T(8,128)S(1)} %get-tuple-element.31.ids_ref, ...), custom_call_target="tpu_custom_call" | custom-call | tf_op jit(solution)/shard_map/middle/pallas_call | solution.py:386
  41.5 0.0 collective-permute-done.2.first_ref
  41.6 0.0 collective-permute-done.3.second_ref
  41.6 1.0 %solve.1 = (f32[256,512]{1,0:T(8,128)}, f32[2048,128]{1,0:T(8,128)S(1)}) custom-call(f32[12,640]{1,0:T(8,128)S(1)} %collective-permute-done.2.first_ref, f32[12,640]{1,0:T(8,128)S(1)} %collective-permute-done.3.second_ref, f32[3,16,640]{2,1,0:T(8,128)S(1)} %get-tuple-element.32.top_ref, ...), custom_call_target="tpu_custom_call", output_to_operand_aliasing={{0}: (6, {})} | custom-call | tf_op jit(solution)/shard_map/solve/pallas_call | solution.py:458
  42.6 0.0 copy-start
  42.6 0.0 copy-start.1
  42.6 24.6 %all_to_all.10 = f32[128,1,2048]{2,1,0:T(1,128)S(1)} all-to-all(f32[128,1,2048]{2,1,0:T(1,128)S(1)} %bitcast.8), channel_id=1, replica_groups=mesh['em'=8,'th'=16] {'em','th'}, dimensions={0} | all-to-all | bytes 2097152 | tf_op jit(solution)/shard_map/all_to_all | solution.py:535
  67.2 0.0 copy-done
  67.2 0.0 copy-done.1
  67.3 2.2 %final.1 = f32[1024,128]{1,0:T(8,128)} custom-call(s32[8,128]{1,0:T(8,128)S(1)} %get-tuple-element.21.slot_ref, f32[2048,128]{1,0:T(8,128)S(1)} %bitcast.7, f32[1024,128]{1,0:T(8,128)S(1)} %copy-done, f32[1024,128]{1,0:T(8,128)S(1)} %copy-done.1), custom_call_target="tpu_custom_call" | custom-call | tf_op jit(solution)/shard_map/final/pallas_call | solution.py:501
Async XLA Ops:
  4.7 30.9 %all-to-all-start = ((f32[128,1,2176]{2,1,0:T(1,128)}), f32[128,1,2176]{2,1,0:T(1,128)S(1)}, u32[]{:S(2)}, u32[]{:S(2)}) async-start(f32[128,1,2176]{2,1,0:T(1,128)} %bitcast.2), calls=%async_computation | async-start | bytes 2228224 | tf_op jit(solution)/shard_map/all_to_all | solution.py:535
  17.7 2.0 %collective-permute-start = (f32[24,256]{1,0:T(8,128)S(1)}, f32[24,256]{1,0:T(8,128)S(1)}, u32[]{:S(2)}, u32[]{:S(2)}) collective-permute-start(f32[24,256]{1,0:T(8,128)S(1)} %get-tuple-element.25), channel_id=1, source_target_pairs={{0,16},{1,17},{2,18},{3,19},{4,20},{5,21},{6,22},{7,23},{8,24},{9,... | collective-permute-start | bytes 73736 | tf_op jit(solution)/shard_map/ppermute | solution.py:529
  18.8 7.5 %collective-permute-start.1 = (f32[24,256]{1,0:T(8,128)S(1)}, f32[24,256]{1,0:T(8,128)S(1)}, u32[]{:S(2)}, u32[]{:S(2)}) collective-permute-start(f32[24,256]{1,0:T(8,128)S(1)} %get-tuple-element.26), channel_id=1, source_target_pairs={{0,112},{1,113},{2,114},{3,115},{4,116},{5,117},{6,118},{7,119},{8... | collective-permute-start | bytes 73736 | tf_op jit(solution)/shard_map/ppermute | solution.py:529
  36.1 5.5 %collective-permute-start.2 = (f32[12,640]{1,0:T(8,128)S(1)}, f32[12,640]{1,0:T(8,128)S(1)}, u32[]{:S(2)}, u32[]{:S(2)}) collective-permute-start(f32[12,640]{1,0:T(8,128)S(1)} %get-tuple-element.27), channel_id=1, source_target_pairs={{0,1},{1,0},{2,3},{3,2},{4,5},{5,4},{6,7},{7,6},{8,9},{9,8},{10,11... | collective-permute-start | bytes 92168 | tf_op jit(solution)/shard_map/ppermute | solution.py:529
  36.6 4.9 %collective-permute-start.3 = (f32[12,640]{1,0:T(8,128)S(1)}, f32[12,640]{1,0:T(8,128)S(1)}, u32[]{:S(2)}, u32[]{:S(2)}) collective-permute-start(f32[12,640]{1,0:T(8,128)S(1)} %get-tuple-element.28), channel_id=1, source_target_pairs={{0,16},{1,2},{2,1},{3,4},{4,3},{5,6},{6,5},{7,8},{8,7},{9,10},{10,... | collective-permute-start | bytes 92168 | tf_op jit(solution)/shard_map/ppermute | solution.py:529
  42.6 24.7 %copy-start = (f32[1024,128]{1,0:T(8,128)S(1)}, f32[1024,128]{1,0:T(8,128)}, u32[]{:S(2)}) copy-start(f32[1024,128]{1,0:T(8,128)} %sg_ref.1) | copy-start | bytes 1572868
  42.6 24.7 %copy-start.1 = (f32[1024,128]{1,0:T(8,128)S(1)}, f32[1024,128]{1,0:T(8,128)}, u32[]{:S(2)}) copy-start(f32[1024,128]{1,0:T(8,128)} %tc_ref.1) | copy-start | bytes 1572868
